TPU v7x, 32 devices: a whole 2x2x4 slice. The times are simulated.
32 devices in a mesh: groups: 2 (over x), ctx: 16 (over z, y, core).
Axes of the slice: x: 2, y: 2, z: 4, core: 2. Of those that a mesh axis runs over, the one named last changes fastest.
Arguments:
- queries: bfloat16 [32768, 1024], P(('groups', 'ctx')), parts along dimension 0, may hold values from -8 to 8
- key_rows: bfloat16 [32768, 1024], P(('groups', 'ctx')), parts along dimension 0, may hold values from -8 to 8
- value_rows: bfloat16 [32768, 1024], P(('groups', 'ctx')), parts along dimension 0, may hold values from -6 to 6
- grad_out: bfloat16 [32768, 1024], P(('groups', 'ctx')), parts along dimension 0, may hold values from -6 to 6
- tile_keys: int32 [256, 8], P(('groups', 'ctx')), parts along dimension 0, may hold values from 0 to 127, as said below
Outputs:
- grad_queries: bfloat16 [32768, 1024], P(('groups', 'ctx')), parts along dimension 0
- grad_keys: bfloat16 [32768, 1024], P(('groups', 'ctx')), parts along dimension 0
- grad_values: bfloat16 [32768, 1024], P(('groups', 'ctx')), parts along dimension 0
There are 2 independent parts, one for each index of `groups`. A program takes and returns all parts, laid end to end along the dimension named above; each array names one. Nothing has to cross between parts.
Inputs may be any that keep to these rules, and one draw needn't show every extreme that they name: `tile_keys`: block j lies on index j // 8 of ctx. A row names 8 blocks on 8 different indices of ctx, none on the index that holds the row's own query block; all query blocks on one index that name some block of another index name the same block of it.
All inputs are finite; a program needn't handle non-finite values.
Results may differ from a plain program's by a relative error of at most 0.012.
Values may be sent and summed in bfloat16 or wider, within the bound.
No kernel may reach another device: no remote copies, remote signals or barrier semaphores. Data moves between devices by JAX's collectives and lax.ppermute only.
A program may use at most 256 MiB of HBM per device.

v0:
```python
import jax
import jax.numpy as jnp
from jax import lax
from jax.sharding import PartitionSpec as P

HEADS = 16
HD = 64
TILE = 128


def block_backward(query_heads, grad_heads, own_keys, own_values, far_keys, far_values):
    factor = HD ** (-0.5)
    own_scores = (
        jnp.einsum("hqd,hkd->hqk", query_heads, own_keys, preferred_element_type=jnp.float32)
        * factor
    )
    far_scores = (
        jnp.einsum("hqd,shkd->hqsk", query_heads, far_keys, preferred_element_type=jnp.float32)
        * factor
    )
    row_max = jnp.maximum(jnp.max(own_scores, axis=2), jnp.max(far_scores, axis=(2, 3)))
    own_raised = jnp.exp(own_scores - row_max[:, :, None])
    far_raised = jnp.exp(far_scores - row_max[:, :, None, None])
    row_total = jnp.sum(own_raised, axis=2) + jnp.sum(far_raised, axis=(2, 3))
    own_weights = own_raised / row_total[:, :, None]
    far_weights = far_raised / row_total[:, :, None, None]
    own_low = own_weights.astype(jnp.bfloat16)
    far_low = far_weights.astype(jnp.bfloat16)
    attended = jnp.einsum(
        "hqk,hkd->hqd", own_low, own_values, preferred_element_type=jnp.float32
    ) + jnp.einsum("hqsk,shkd->hqd", far_low, far_values, preferred_element_type=jnp.float32)
    delta_row = jnp.sum(grad_heads.astype(jnp.float32) * attended, axis=2)
    own_gw = jnp.einsum("hqd,hkd->hqk", grad_heads, own_values, preferred_element_type=jnp.float32)
    far_gw = jnp.einsum(
        "hqd,shkd->hqsk", grad_heads, far_values, preferred_element_type=jnp.float32
    )
    own_gs = (own_weights * (own_gw - delta_row[:, :, None])).astype(jnp.bfloat16)
    far_gs = (far_weights * (far_gw - delta_row[:, :, None, None])).astype(jnp.bfloat16)
    grad_query = (
        jnp.einsum("hqk,hkd->hqd", own_gs, own_keys, preferred_element_type=jnp.float32)
        + jnp.einsum("hqsk,shkd->hqd", far_gs, far_keys, preferred_element_type=jnp.float32)
    ) * factor
    own_gk = (
        jnp.einsum("hqk,hqd->hkd", own_gs, query_heads, preferred_element_type=jnp.float32) * factor
    )
    far_gk = (
        jnp.einsum("hqsk,hqd->shkd", far_gs, query_heads, preferred_element_type=jnp.float32)
        * factor
    )
    own_gv = jnp.einsum("hqk,hqd->hkd", own_low, grad_heads, preferred_element_type=jnp.float32)
    far_gv = jnp.einsum("hqsk,hqd->shkd", far_low, grad_heads, preferred_element_type=jnp.float32)
    return (grad_query, own_gk, own_gv, far_gk, far_gv)


def on_device(queries, key_rows, value_rows, grad_out, tile_keys):
    row_total, feature_total = queries.shape
    block_count = row_total // TILE
    device_count = lax.axis_size("ctx")
    peer_range = jnp.arange(device_count, dtype=jnp.int32)
    owners = tile_keys // block_count
    local_ids = tile_keys % block_count
    matches = owners[:, :, None] == peer_range[None, None, :]
    wanted = jnp.max(jnp.where(matches, local_ids[:, :, None], -1), axis=(0, 1))
    requested = lax.all_to_all(wanted, "ctx", split_axis=0, concat_axis=0, tiled=True)
    served = requested >= 0
    serve_ids = jnp.maximum(requested, 0)

    def to_heads(rows):
        return rows.reshape(block_count, TILE, HEADS, HD).transpose(0, 2, 1, 3)

    def from_heads(blocks):
        return blocks.transpose(0, 2, 1, 3).reshape(row_total, feature_total)

    key_heads = to_heads(key_rows)
    value_heads = to_heads(value_rows)
    query_heads = to_heads(queries)
    grad_heads = to_heads(grad_out)
    fetched_keys, fetched_values = (
        lax.all_to_all(key_heads[serve_ids], "ctx", split_axis=0, concat_axis=0, tiled=True),
        lax.all_to_all(value_heads[serve_ids], "ctx", split_axis=0, concat_axis=0, tiled=True),
    )

    def one_step(summed, entries):
        summed_keys, summed_values = summed
        query_block, grad_block, own_keys, own_values, peer_ids = entries
        grad_query, own_gk, own_gv, far_gk, far_gv = block_backward(
            query_block,
            grad_block,
            own_keys,
            own_values,
            fetched_keys[peer_ids],
            fetched_values[peer_ids],
        )
        summed_keys = summed_keys.at[peer_ids].add(far_gk)
        summed_values = summed_values.at[peer_ids].add(far_gv)
        return ((summed_keys, summed_values), (grad_query, own_gk, own_gv))

    empty = jnp.zeros((device_count, HEADS, TILE, HD), jnp.float32)
    (summed_keys, summed_values), (grad_query, own_key_terms, own_value_terms) = lax.scan(
        one_step, (empty, empty), (query_heads, grad_heads, key_heads, value_heads, owners)
    )
    returned_keys, returned_values = (
        lax.all_to_all(
            summed_keys.astype(jnp.bfloat16), "ctx", split_axis=0, concat_axis=0, tiled=True
        ),
        lax.all_to_all(
            summed_values.astype(jnp.bfloat16), "ctx", split_axis=0, concat_axis=0, tiled=True
        ),
    )
    keep_mask = served[:, None, None, None]
    grad_keys = own_key_terms.at[serve_ids].add(
        jnp.where(keep_mask, returned_keys.astype(jnp.float32), 0.0)
    )
    grad_values = own_value_terms.at[serve_ids].add(
        jnp.where(keep_mask, returned_values.astype(jnp.float32), 0.0)
    )
    return (
        from_heads(grad_query).astype(jnp.bfloat16),
        from_heads(grad_keys).astype(jnp.bfloat16),
        from_heads(grad_values).astype(jnp.bfloat16),
    )


def solution(mesh):
    in_specs = (
        P(("groups", "ctx"), None),
        P(("groups", "ctx"), None),
        P(("groups", "ctx"), None),
        P(("groups", "ctx"), None),
        P(("groups", "ctx"), None),
    )
    out_specs = (P(("groups", "ctx"), None), P(("groups", "ctx"), None), P(("groups", "ctx"), None))
    return jax.shard_map(
        on_device, mesh=mesh, in_specs=in_specs, out_specs=out_specs, check_vma=False
    )
```

profile of v0, /device:TPU:13, one launch (start us, length us, event | category | flops | bytes accessed | tf_op | source)
XLA Modules:
  0.0 1043.8 jit_solution(13547787037150975544)
XLA Ops:
  2.1 6.6 all-to-all-start
  46.2 75.7 %all-to-all-done.1 = bf16[16,16,128,64]{2,3,1,0:T(8,128)(2,1)} async-done(((bf16[16,16,128,64]{2,3,1,0:T(8,128)(2,1)}), bf16[16,16,128,64]{2,3,1,0:T(8,128)(2,1)}, u32[]{:S(2)}, u32[]{:S(2)}) %all-to-all-start.1) | async-done | bytes 4194336 | tf_op jit(solution)/shard_map/all_to_all | solution.py:79
  142.9 8.4 copy.181
  151.3 68.0 %all-to-all-done.2 = bf16[16,16,128,64]{2,3,1,0:T(8,128)(2,1)} async-done(((bf16[16,16,128,64]{2,3,1,0:T(8,128)(2,1)}), bf16[16,16,128,64]{2,3,1,0:T(8,128)(2,1)}, u32[]{:S(2)}, u32[]{:S(2)}) %all-to-all-start.2) | async-done | bytes 4194336 | tf_op jit(solution)/shard_map/all_to_all | solution.py:80
  219.3 8.5 copy.183
  236.3 530.0 %while.18 = (s32[]{:T(128)}, f32[16,16,128,64]{2,3,1,0:T(8,128)}, f32[16,16,128,64]{2,3,1,0:T(8,128)}, bf16[8,16,128,64]{2,3,1,0:T(8,128)(2,1)}, f32[8,16,128,64...) while((s32[]{:T(128)}, f32[16,16,128,64]{2,3,1,0:T(8,128)}, ...), condition=%wide.region_9.10_spmd, body=%wide.region_1.9_spmd.sunk | while | flops 1859775488 | bytes 154634688 | solution.py:99
  282.8 9.4 scatter_fusion.1
  292.2 9.4 scatter_fusion
  347.8 9.5 scatter_fusion.1
  357.3 9.4 scatter_fusion
  413.0 9.4 scatter_fusion.1
  422.4 9.4 scatter_fusion
  477.9 9.5 scatter_fusion.1
  487.4 9.4 scatter_fusion
  543.0 9.4 scatter_fusion.1
  552.5 9.4 scatter_fusion
  608.1 9.5 scatter_fusion.1
  617.7 9.5 scatter_fusion
  673.3 9.6 scatter_fusion.1
  682.9 9.4 scatter_fusion
  738.5 9.4 scatter_fusion.1
  748.0 9.4 scatter_fusion
  766.4 6.5 convert_element_type.57
  778.0 6.4 convert_element_type.62
  784.4 86.0 %all-to-all-done.3 = bf16[16,16,128,64]{2,3,1,0:T(8,128)(2,1)} async-done(((bf16[16,16,128,64]{2,3,1,0:T(8,128)(2,1)}), bf16[16,16,128,64]{2,3,1,0:T(8,128)(2,1)}, u32[]{:S(2)}, u32[]{:S(2)}) %all-to-all-start.3) | async-done | bytes 4194336 | tf_op jit(solution)/shard_map/all_to_all | solution.py:103
  880.1 6.5 reshape.175
  886.6 81.3 %all-to-all-done.4 = bf16[16,16,128,64]{2,3,1,0:T(8,128)(2,1)} async-done(((bf16[16,16,128,64]{2,3,1,0:T(8,128)(2,1)}), bf16[16,16,128,64]{2,3,1,0:T(8,128)(2,1)}, u32[]{:S(2)}, u32[]{:S(2)}) %all-to-all-start.4) | async-done | bytes 4194336 | tf_op jit(solution)/shard_map/all_to_all | solution.py:106
  967.9 11.8 %convert_select_fusion = (f32[16,16,128,64]{2,3,1,0:T(8,128)}, f32[16,16,128,64]{2,3,1,0:T(8,128)}) fusion(bf16[16,16,128,64]{2,3,1,0:T(8,128)(2,1)} %all-to-all-done.4, pred[16]{0:T(512)(128)(4,1)S(1)} %compare_reduce_fusion, bf16[16,16,128,64]{2,3,1,0:T(8,128)(2,1)} %all-to-all-done.3), kind=kLoop, calls=%fused_computation.86 | loop fusion | flops 8388608 | bytes 25165840 | tf_op jit(solution)/shard_map/jit(_where)/select_n | solution.py:115
  979.6 17.2 %scatter_fusion.2 = f32[8,16,128,64]{2,3,1,0:T(8,128)} fusion(f32[8,16,128,64]{2,3,1,0:T(8,128)} %get-tuple-element.75, s32[16]{0:T(128)S(1)} %copy-done.6, f32[16,16,128,64]{2,3,1,0:T(8,128)} %get-tuple-element.205), kind=kCustom, calls=%fused_computation.6 | custom fusion | flops 2097152 | bytes 25165888 | tf_op jit(solution)/shard_map/scatter-add | solution.py:111
  999.5 17.3 %scatter_fusion.3 = f32[8,16,128,64]{2,3,1,0:T(8,128)} fusion(f32[8,16,128,64]{2,3,1,0:T(8,128)} %get-tuple-element.77, s32[16]{0:T(128)S(1)} %copy-done.6, f32[16,16,128,64]{2,3,1,0:T(8,128)} %get-tuple-element.204), kind=kCustom, calls=%fused_computation.7 | custom fusion | flops 2097152 | bytes 25165888 | tf_op jit(solution)/shard_map/scatter-add | solution.py:114
  1026.4 6.5 reshape.177
  1037.2 6.5 reshape.176
  (251 shorter events, 468.7 us)
Async XLA Ops:
  2.1 17.9 %all-to-all-start = ((s32[16,1,1]{2,1,0:T(1,128)}), s32[16,1,1]{2,1,0:T(1,128)S(1)}, u32[]{:S(2)}, u32[]{:S(2)}) async-start(s32[16,1,1]{2,1,0:T(1,128)} %copy.176), calls=%async_computation | async-start | bytes 16384 | tf_op jit(solution)/shard_map/all_to_all | solution.py:64
  20.0 3.4 copy-start.3
  20.4 3.0 copy-start.5
  23.4 98.5 %all-to-all-start.1 = ((bf16[16,16,128,64]{2,3,1,0:T(8,128)(2,1)}), bf16[16,16,128,64]{2,3,1,0:T(8,128)(2,1)}, u32[]{:S(2)}, u32[]{:S(2)}) async-start(bf16[16,16,128,64]{2,3,1,0:T(8,128)(2,1)} %gather_fusion.2), calls=%async_computation.1 | async-start | bytes 8388608 | tf_op jit(solution)/shard_map/all_to_all | solution.py:79
  121.9 97.4 %all-to-all-start.2 = ((bf16[16,16,128,64]{2,3,1,0:T(8,128)(2,1)}), bf16[16,16,128,64]{2,3,1,0:T(8,128)(2,1)}, u32[]{:S(2)}, u32[]{:S(2)}) async-start(bf16[16,16,128,64]{2,3,1,0:T(8,128)(2,1)} %gather_fusion.3), calls=%async_computation.2 | async-start | bytes 8388608 | tf_op jit(solution)/shard_map/all_to_all | solution.py:80
  254.2 2.2 copy-start.1
  264.0 3.3 copy-start
  319.3 2.2 copy-start.1
  329.0 3.3 copy-start
  384.4 2.2 copy-start.1
  394.1 3.3 copy-start
  449.4 2.2 copy-start.1
  459.1 3.3 copy-start
  514.5 2.2 copy-start.1
  524.2 3.3 copy-start
  579.6 2.2 copy-start.1
  589.3 3.3 copy-start
  644.8 2.2 copy-start.1
  654.5 3.3 copy-start
  709.9 2.2 copy-start.1
  719.7 3.3 copy-start
  772.8 97.7 %all-to-all-start.3 = ((bf16[16,16,128,64]{2,3,1,0:T(8,128)(2,1)}), bf16[16,16,128,64]{2,3,1,0:T(8,128)(2,1)}, u32[]{:S(2)}, u32[]{:S(2)}) async-start(bf16[16,16,128,64]{2,3,1,0:T(8,128)(2,1)} %convert_element_type.57), calls=%async_computation.3 | async-start | bytes 8388608 | tf_op jit(solution)/shard_map/all_to_all | solution.py:103
  784.4 91.0 %copy-start.4 = (s32[16,1,1]{2,1,0:T(1,128)S(1)}, s32[16,1,1]{2,1,0:T(1,128)}, u32[]{:S(2)}) copy-start(s32[16,1,1]{2,1,0:T(1,128)} %copy-done.3) | copy-start | bytes 196
  784.4 91.3 %copy-start.2 = (bf16[8,16,128,64]{2,3,1,0:T(8,128)(2,1)S(1)}, bf16[8,16,128,64]{2,3,1,0:T(8,128)(2,1)}, u32[]{:S(2)}) copy-start(bf16[8,16,128,64]{2,3,1,0:T(8,128)(2,1)} %get-tuple-element.74) | copy-start | bytes 6291460
  870.5 97.4 %all-to-all-start.4 = ((bf16[16,16,128,64]{2,3,1,0:T(8,128)(2,1)}), bf16[16,16,128,64]{2,3,1,0:T(8,128)(2,1)}, u32[]{:S(2)}, u32[]{:S(2)}) async-start(bf16[16,16,128,64]{2,3,1,0:T(8,128)(2,1)} %convert_element_type.62), calls=%async_computation.4 | async-start | bytes 8388608 | tf_op jit(solution)/shard_map/all_to_all | solution.py:106
  886.6 93.0 %copy-start.6 = (s32[16]{0:T(128)S(1)}, s32[16]{0:T(128)}, u32[]{:S(2)}) copy-start(s32[16]{0:T(128)} %copy-done.5) | copy-start | bytes 196
where the time goes:
time: 1060 us; the launch traced here: 1040 us
  waiting for transfers between devices  311 us (29%)
  local copies, waits for them, and re-layouts  252 us (24%)
  other arithmetic  231 us (22%)
  matrix products  211 us (20%)
  starting transfers between devices  27.6 us (3%)
    all_to_all x1, waiting for transfers between devices, on_device(): lax.all_to_all(summed_keys.astype(jnp.bfloat16), 'ctx', split_axis=0, con...  86 us
    all_to_all x1, waiting for transfers between devices, on_device(): lax.all_to_all(summed_values.astype(jnp.bfloat16), 'ctx', split_axis=0, c...  81.3 us
    scatter-add x8, other arithmetic, one_step(): summed_values = summed_values.at[peer_ids].add(far_gv)  75.8 us
    all_to_all x1, waiting for transfers between devices, on_device(): lax.all_to_all(key_heads[serve_ids], 'ctx', split_axis=0, concat_axis=0,...  75.7 us
    scatter-add x8, other arithmetic, one_step(): summed_keys = summed_keys.at[peer_ids].add(far_gk)  75.3 us
    all_to_all x1, waiting for transfers between devices, on_device(): lax.all_to_all(value_heads[serve_ids], 'ctx', split_axis=0, concat_axis=0...  68 us
    gather x8, local copies, waits for them, and re-layouts, one_step(): fetched_values[peer_ids]  51.2 us
    gather x8, local copies, waits for them, and re-layouts, one_step(): fetched_keys[peer_ids]  51 us
  transfers between devices with their start and end apart: 5, of which 4 were waited for; matrix products, arithmetic and copies ran while one was open for 7% of the time, Pallas kernels for 0%

commit v1 on v0

v1 whole, which is shorter than its diff:
```python
import functools

import jax
import jax.numpy as jnp
from jax import lax
from jax.experimental import pallas as pl
from jax.experimental.pallas import tpu as pltpu
from jax.sharding import PartitionSpec as P

HD = 64
TILE = 128
PAIR = 2 * HD
LOG2E = 1.4426950408889634
CHUNKS = 2
VMEM_LIMIT = 48 * 1024 * 1024


def dot_nt(a, b):
    return lax.dot_general(a, b, (((1,), (1,)), ((), ())), preferred_element_type=jnp.float32)


def dot_nn(a, b):
    return lax.dot_general(a, b, (((1,), (0,)), ((), ())), preferred_element_type=jnp.float32)


def gather_kernel(peers, chunk_width, chunk, ids_ref, k_ref, v_ref, out_ref, sems):
    cols = pl.ds(chunk * chunk_width, chunk_width)

    def copies(p):
        rows = pl.ds(pl.multiple_of(ids_ref[p] * TILE, TILE), TILE)
        return (
            pltpu.make_async_copy(k_ref.at[rows, cols], out_ref.at[p, pl.ds(0, TILE)], sems.at[0, p]),
            pltpu.make_async_copy(v_ref.at[rows, cols], out_ref.at[p, pl.ds(TILE, TILE)], sems.at[1, p]),
        )

    for p in range(peers):
        for copy in copies(p):
            copy.start()
    for p in range(peers):
        for copy in copies(p):
            copy.wait()


def gather_blocks(ids, key_rows, value_rows, chunk, chunk_width):
    peers = ids.shape[0]
    return pl.pallas_call(
        functools.partial(gather_kernel, peers, chunk_width, chunk),
        grid_spec=pltpu.PrefetchScalarGridSpec(
            num_scalar_prefetch=1,
            grid=(),
            in_specs=[pl.BlockSpec(memory_space=pl.ANY)] * 2,
            out_specs=pl.BlockSpec(memory_space=pl.ANY),
            scratch_shapes=[pltpu.SemaphoreType.DMA((2, peers))],
        ),
        out_shape=jax.ShapeDtypeStruct((peers, 2 * TILE, chunk_width), jnp.bfloat16),
        name="gather_blocks",
    )(ids, key_rows, value_rows)


def attend_kernel(peers, blocks, picks, aliased, slots_ref, q_ref, g_ref, k_ref, v_ref, recv_ref, *rest):
    if aliased:
        rest = rest[1:]
    dq_ref, own_ref, out_ref, s_scr, w_scr, p_scr, kt_scr, acc_scr = rest
    lane = lax.broadcasted_iota(jnp.int32, (TILE, PAIR), 1)
    first = lane < HD

    def prepare(p, carry):
        kt_scr[p] = recv_ref[p, :TILE, :].T
        acc_scr[p] = jnp.zeros((2 * TILE, PAIR), jnp.float32)
        return carry

    lax.fori_loop(0, peers, prepare, 0)

    def split(x):
        zero = jnp.zeros_like(x)
        return jnp.concatenate([jnp.where(first, x, zero), jnp.where(first, zero, x)], axis=0)

    def one_block(b, carry):
        rows = pl.ds(pl.multiple_of(b * TILE, TILE), TILE)
        q2f = split(q_ref[rows, :].astype(jnp.float32) * (HD**-0.5))
        g2f = split(g_ref[rows, :].astype(jnp.float32))
        q2 = q2f.astype(jnp.bfloat16)
        g2 = g2f.astype(jnp.bfloat16)
        slots = [slots_ref[b * picks + j] for j in range(picks)]

        def fold(x, op):
            x = x.reshape(TILE // 8, 8, 2 * TILE)
            return op(x, axis=0)

        top = None
        for j in range(picks + 1):
            if j < picks:
                kb, vb = recv_ref[slots[j], :TILE, :], recv_ref[slots[j], TILE:, :]
            else:
                kb, vb = k_ref[rows, :], v_ref[rows, :]
            s = dot_nt(kb, q2)
            s_scr[j] = s
            w_scr[j] = dot_nt(vb, g2)
            part = fold(s, jnp.max)
            top = part if top is None else jnp.maximum(top, part)
        top = jnp.max(top, axis=0, keepdims=True)
        total = jnp.zeros((8, 2 * TILE), jnp.float32)
        inner = jnp.zeros((8, 2 * TILE), jnp.float32)
        for j in range(picks + 1):
            p = jnp.exp2((s_scr[j] - top) * LOG2E)
            s_scr[j] = p
            p_scr[j] = p.astype(jnp.bfloat16)
            total += fold(p, jnp.sum)
            inner += fold(p * w_scr[j], jnp.sum)
        recip = 1.0 / jnp.sum(total, axis=0, keepdims=True)
        delta = jnp.sum(inner, axis=0, keepdims=True) * recip
        column = jnp.broadcast_to(recip, (PAIR, 2 * TILE)).T
        rq = (q2f * column).astype(jnp.bfloat16)
        rg = (g2f * column).astype(jnp.bfloat16)
        dqt = jnp.zeros((PAIR, 2 * TILE), jnp.float32)
        for j in range(picks + 1):
            ds = (s_scr[j] * (w_scr[j] - delta)).astype(jnp.bfloat16)
            dk = dot_nn(ds, rq)
            dv = dot_nn(p_scr[j], rg)
            if j < picks:
                acc_scr[slots[j], :TILE, :] += dk
                acc_scr[slots[j], TILE:, :] += dv
                kt = kt_scr[slots[j]]
            else:
                own_ref[0, rows, :] = dk
                own_ref[1, rows, :] = dv
                kt = k_ref[rows, :].T
            dqt += dot_nn(kt, ds)
        dqt = dqt * (recip * (HD**-0.5))
        dqt = jnp.concatenate([dqt[:HD, :TILE], dqt[HD:, TILE:]], axis=0)
        dq_ref[rows, :] = dqt.T.astype(jnp.bfloat16)
        return carry

    lax.fori_loop(0, blocks, one_block, 0)

    def finish(p, carry):
        out_ref[p] = acc_scr[p].astype(jnp.bfloat16)
        return carry

    lax.fori_loop(0, peers, finish, 0)


def attend(slots, queries, grad_out, key_rows, value_rows, received, previous, chunk):
    peers, _, chunk_width = received.shape
    rows, width = queries.shape
    blocks = rows // TILE
    picks = slots.shape[0] // blocks
    pairs = chunk_width // PAIR
    base = chunk * pairs
    rows_spec = pl.BlockSpec((rows, PAIR), lambda i, s: (0, base + i))
    pack_spec = pl.BlockSpec((peers, 2 * TILE, PAIR), lambda i, s: (0, 0, i))
    in_specs = [rows_spec] * 4 + [pack_spec]
    operands = [slots, queries, grad_out, key_rows, value_rows, received]
    aliases = {}
    if previous is not None:
        in_specs.append(pl.BlockSpec(memory_space=pl.ANY))
        operands.append(previous)
        aliases = {6: 0}
    keys = TILE * (picks + 1)
    flops = 5 * 2 * 2 * TILE * PAIR * keys * blocks * pairs
    return pl.pallas_call(
        functools.partial(attend_kernel, peers, blocks, picks, previous is not None),
        grid_spec=pltpu.PrefetchScalarGridSpec(
            num_scalar_prefetch=1,
            grid=(pairs,),
            in_specs=in_specs,
            out_specs=[
                rows_spec,
                pl.BlockSpec((2, rows, PAIR), lambda i, s: (0, 0, i)),
                pack_spec,
            ],
            scratch_shapes=[
                pltpu.VMEM((picks + 1, TILE, 2 * TILE), jnp.float32),
                pltpu.VMEM((picks + 1, TILE, 2 * TILE), jnp.float32),
                pltpu.VMEM((picks + 1, TILE, 2 * TILE), jnp.bfloat16),
                pltpu.VMEM((peers, PAIR, TILE), jnp.bfloat16),
                pltpu.VMEM((peers, 2 * TILE, PAIR), jnp.float32),
            ],
        ),
        out_shape=[
            jax.ShapeDtypeStruct((rows, width), jnp.bfloat16),
            jax.ShapeDtypeStruct((2, rows, chunk_width), jnp.float32),
            jax.ShapeDtypeStruct(received.shape, jnp.bfloat16),
        ],
        input_output_aliases=aliases,
        cost_estimate=pl.CostEstimate(
            flops=flops,
            bytes_accessed=24 * 1024 * 1024,
            transcendentals=blocks * pairs * keys * 2 * TILE,
        ),
        compiler_params=pltpu.CompilerParams(vmem_limit_bytes=VMEM_LIMIT),
        name="attend",
    )(*operands)


def combine_kernel(peers, blocks, aliased, ids_ref, own_ref, back_ref, *rest):
    if aliased:
        rest = rest[2:]
    gk_ref, gv_ref, acc = rest
    for b in range(blocks):
        acc[b, :TILE, :] = own_ref[0, b * TILE : (b + 1) * TILE, :]
        acc[b, TILE:, :] = own_ref[1, b * TILE : (b + 1) * TILE, :]

    def add(p, carry):
        target = ids_ref[p]

        @pl.when(target >= 0)
        def _():
            acc[jnp.maximum(target, 0)] += back_ref[p].astype(jnp.float32)

        return carry

    lax.fori_loop(0, peers, add, 0)
    for b in range(blocks):
        gk_ref[b * TILE : (b + 1) * TILE, :] = acc[b, :TILE, :].astype(jnp.bfloat16)
        gv_ref[b * TILE : (b + 1) * TILE, :] = acc[b, TILE:, :].astype(jnp.bfloat16)


def combine(requested, own, returned, previous, chunk, width):
    peers, _, chunk_width = returned.shape
    rows = own.shape[1]
    blocks = rows // TILE
    step = 2 * PAIR
    base = chunk * (chunk_width // step)
    in_specs = [
        pl.BlockSpec((2, rows, step), lambda i, s: (0, 0, i)),
        pl.BlockSpec((peers, 2 * TILE, step), lambda i, s: (0, 0, i)),
    ]
    operands = [requested, own, returned]
    aliases = {}
    if previous is not None:
        in_specs += [pl.BlockSpec(memory_space=pl.ANY)] * 2
        operands += list(previous)
        aliases = {3: 0, 4: 1}
    out_spec = pl.BlockSpec((rows, step), lambda i, s: (0, base + i))
    return pl.pallas_call(
        functools.partial(combine_kernel, peers, blocks, previous is not None),
        grid_spec=pltpu.PrefetchScalarGridSpec(
            num_scalar_prefetch=1,
            grid=(chunk_width // step,),
            in_specs=in_specs,
            out_specs=[out_spec, out_spec],
            scratch_shapes=[pltpu.VMEM((blocks, 2 * TILE, step), jnp.float32)],
        ),
        out_shape=[jax.ShapeDtypeStruct((rows, width), jnp.bfloat16)] * 2,
        input_output_aliases=aliases,
        cost_estimate=pl.CostEstimate(flops=0, bytes_accessed=12 * 1024 * 1024, transcendentals=0),
        compiler_params=pltpu.CompilerParams(vmem_limit_bytes=VMEM_LIMIT),
        name="combine",
    )(*operands)


def exchange(x):
    return lax.all_to_all(x, "ctx", split_axis=0, concat_axis=0, tiled=True)


def on_device(queries, key_rows, value_rows, grad_out, tile_keys):
    rows, width = queries.shape
    blocks = rows // TILE
    peers = lax.axis_size("ctx")
    peer_range = jnp.arange(peers, dtype=jnp.int32)
    owners = tile_keys // blocks
    local_ids = tile_keys % blocks
    matches = owners[:, :, None] == peer_range[None, None, :]
    wanted = jnp.max(jnp.where(matches, local_ids[:, :, None], -1), axis=(0, 1))
    requested = exchange(wanted)
    serve_ids = jnp.maximum(requested, 0)
    slots = owners.reshape(-1)
    chunk_width = width // CHUNKS

    received = [
        exchange(gather_blocks(serve_ids, key_rows, value_rows, c, chunk_width)) for c in range(CHUNKS)
    ]
    grad_queries = None
    owns, backs = [], []
    for c in range(CHUNKS):
        grad_queries, own, out = attend(
            slots, queries, grad_out, key_rows, value_rows, received[c], grad_queries, c
        )
        owns.append(own)
        backs.append(exchange(out))
    result = None
    for c in range(CHUNKS):
        result = combine(requested, owns[c], backs[c], result, c, width)
    return grad_queries, result[0], result[1]


def solution(mesh):
    spec = P(("groups", "ctx"), None)
    return jax.shard_map(
        on_device, mesh=mesh, in_specs=(spec,) * 5, out_specs=(spec,) * 3, check_vma=False
    )
```

time: 1060 us -> 579 us (0.55); the launches traced: 1040 us -> 578 us
  Pallas kernels: 0 us -> 389 us
  local copies, waits for them, and re-layouts: 252 us -> 7.72 us
  other arithmetic: 231 us -> 1.7 us
  matrix products: 211 us -> 0 us
  waiting for transfers between devices: 311 us -> 146 us
    pallas_call x0 -> x6, Pallas kernels: none -> 389 us  [the longest x2 258 us: gather_blocks(): pl.pallas_call(functools.partial(gather_kernel, peers, chunk_width, chunk...]
    dot_general x96 -> x0, matrix products: 211 us -> none  [the longest x8 29.2 us: block_backward(): jnp.einsum('hqd,shkd->hqsk', grad_heads, far_values, preferred_element_ty...]
    scatter-add x18 -> x0, other arithmetic: 186 us -> none  [the longest x8 75.8 us: one_step(): summed_values = summed_values.at[peer_ids].add(far_gv)]
    all_to_all x5 -> x4, waiting for transfers between devices: 311 us -> 146 us  [exchange(): return lax.all_to_all(x, 'ctx', split_axis=0, concat_axis=0, tiled=True)]
    gather x18 -> x0, local copies, waits for them, and re-layouts: 110 us -> none  [the longest x8 51.2 us: one_step(): fetched_values[peer_ids]]
    unnamed x20 -> x10, local copies, waits for them, and re-layouts: 46 us -> 7.56 us
    while x36 -> x0, local copies, waits for them, and re-layouts: 25.6 us -> none  [the longest x4 20.6 us: on_device(): lax.scan(one_step, (empty, empty), (query_heads, grad_heads, key_heads, v...]
    reshape x4 -> x1, local copies, waits for them, and re-layouts: 23.5 us -> 0.08 us  [on_device(): slots = owners.reshape(-1)]
  transfers between devices with their start and end apart: 5 -> 4, of which waited for: 4 -> 3; matrix products, arithmetic and copies ran while one was open for 7% -> 0% of each run, Pallas kernels for 0% -> 44%
where the time goes in v1:
time: 579 us; the launch traced here: 578 us
  Pallas kernels  389 us (67%)
  waiting for transfers between devices  146 us (25%)
  starting transfers between devices  23.1 us (4%)
  blocking collectives  10.1 us (2%)
  local copies, waits for them, and re-layouts  7.72 us (1%)
    pallas_call x2, Pallas kernels, gather_blocks(): pl.pallas_call(functools.partial(gather_kernel, peers, chunk_width, chunk...  258 us
    all_to_all x4, waiting for transfers between devices, exchange(): return lax.all_to_all(x, 'ctx', split_axis=0, concat_axis=0, tiled=True)  146 us
    pallas_call x2, Pallas kernels, attend(): pl.pallas_call(functools.partial(attend_kernel, peers, blocks, picks, pre...  121 us
    all_to_all x4, starting transfers between devices, exchange(): return lax.all_to_all(x, 'ctx', split_axis=0, concat_axis=0, tiled=True)  23.1 us
  transfers between devices with their start and end apart: 4, of which 3 were waited for; matrix products, arithmetic and copies ran while one was open for 0% of the time, Pallas kernels for 44%

profile of v1, /device:TPU:13, one launch (start us, length us, event | category | flops | bytes accessed | tf_op | source)
XLA Modules:
  0.0 578.3 jit_solution(3377836295046802838)
XLA Ops:
  0.6 0.7 add_select_fusion
  1.3 0.1 select_reduce_fusion
  1.4 0.1 copy.13
  1.5 10.1 %all_to_all.31 = s32[16,1,1]{2,1,0:T(1,128)S(1)} all-to-all(s32[16,1,1]{2,1,0:T(1,128)S(1)} %copy.13), channel_id=1, replica_groups=mesh['groups'=2,'ctx'=16] {'ctx'}, dimensions={0} | all-to-all | bytes 128 | tf_op jit(solution)/shard_map/all_to_all | solution.py:254
  11.7 0.4 reduce.ids_ref
  12.0 0.5 broadcast_maximum_fusion.ids_ref
  12.6 129.1 %gather_blocks.3 = bf16[16,256,512]{2,1,0:T(8,128)(2,1)} custom-call(s32[16]{0:T(128)} %broadcast_maximum_fusion.ids_ref, bf16[1024,1024]{1,0:T(8,128)(2,1)} %k_ref.7, bf16[1024,1024]{1,0:T(8,128)(2,1)} %v_ref.7), custom_call_target="tpu_custom_call" | custom-call | tf_op jit(solution)/shard_map/gather_blocks/pallas_call | solution.py:46
  141.7 7.0 %all-to-all-start.2 = ((bf16[16,256,512]{2,1,0:T(8,128)(2,1)}), bf16[16,256,512]{2,1,0:T(8,128)(2,1)}, u32[]{:S(2)}, u32[]{:S(2)}) async-start(bf16[16,256,512]{2,1,0:T(8,128)(2,1)} %gather_blocks.3), calls=%async_computation.2 | async-start | bytes 8388608 | tf_op jit(solution)/shard_map/all_to_all | solution.py:254
  148.7 129.1 %gather_blocks.2 = bf16[16,256,512]{2,1,0:T(8,128)(2,1)} custom-call(s32[16]{0:T(128)} %broadcast_maximum_fusion.ids_ref, bf16[1024,1024]{1,0:T(8,128)(2,1)} %k_ref.7, bf16[1024,1024]{1,0:T(8,128)(2,1)} %v_ref.7), custom_call_target="tpu_custom_call" | custom-call | tf_op jit(solution)/shard_map/gather_blocks/pallas_call | solution.py:46
  277.8 0.0 copy-start.2
  277.8 0.0 all-to-all-done.2.recv_ref
  277.8 6.2 %all-to-all-start.1 = ((bf16[16,256,512]{2,1,0:T(8,128)(2,1)}), bf16[16,256,512]{2,1,0:T(8,128)(2,1)}, u32[]{:S(2)}, u32[]{:S(2)}) async-start(bf16[16,256,512]{2,1,0:T(8,128)(2,1)} %gather_blocks.2), calls=%async_computation.1 | async-start | bytes 8388608 | tf_op jit(solution)/shard_map/all_to_all | solution.py:254
  284.0 0.1 reshape.13.slots_ref
  284.1 0.0 copy-done.2
  284.1 0.0 copy-start.3
  284.1 1.6 copy-done.3
  285.7 60.4 %attend.2 = (bf16[1024,1024]{1,0:T(8,128)(2,1)}, f32[2,1024,512]{2,1,0:T(8,128)}, bf16[16,256,512]{2,1,0:T(8,128)(2,1)}) custom-call(s32[64]{0:T(128)S(1)} %reshape.13.slots_ref, bf16[1024,1024]{1,0:T(8,128)(2,1)S(1)} %copy-done.2, bf16[1024,1024]{1,0:T(8,128)(2,1)S(1)} %copy-done.3, bf16[1024,1024]{1,0:T(8,128)(2,1)} %k_ref.7, bf16[1024,1024]{1,0:T(8,128)(2,1)} %v_ref.7, ...), custom_call_target="tpu_custom_call" | custom-call | flops 12079595520 | bytes 25165824 | tf_op jit(solution)/shard_map/attend/pallas_call | solution.py:161
  346.2 30.4 %all-to-all-done.1.recv_ref = bf16[16,256,512]{2,1,0:T(8,128)(2,1)} async-done(((bf16[16,256,512]{2,1,0:T(8,128)(2,1)}), bf16[16,256,512]{2,1,0:T(8,128)(2,1)}, u32[]{:S(2)}, u32[]{:S(2)}) %all-to-all-start.1) | async-done | bytes 4194336 | tf_op jit(solution)/shard_map/all_to_all | solution.py:254
  376.5 4.9 all-to-all-start.4
  381.4 0.0 copy-start.4
  381.4 1.6 copy-done.4
  383.0 60.6 %attend.3 = (bf16[1024,1024]{1,0:T(8,128)(2,1)}, f32[2,1024,512]{2,1,0:T(8,128)}, bf16[16,256,512]{2,1,0:T(8,128)(2,1)}) custom-call(s32[64]{0:T(128)S(1)} %reshape.13.slots_ref, bf16[1024,1024]{1,0:T(8,128)(2,1)S(1)} %copy-done.2, bf16[1024,1024]{1,0:T(8,128)(2,1)S(1)} %copy-done.4, bf16[1024,1024]{1,0:T(8,128)(2,1)} %k_ref.7, ...), custom_call_target="tpu_custom_call", output_to_operand_aliasing={{0}: (6, {})} | custom-call | flops 12079595520 | bytes 25165824 | tf_op jit(solution)/shard_map/attend/pallas_call | solution.py:161
  443.6 30.3 %all-to-all-done.4.back_ref = bf16[16,256,512]{2,1,0:T(8,128)(2,1)} async-done(((bf16[16,256,512]{2,1,0:T(8,128)(2,1)}), bf16[16,256,512]{2,1,0:T(8,128)(2,1)}, u32[]{:S(2)}, u32[]{:S(2)}) %all-to-all-start.4) | async-done | bytes 4194336 | tf_op jit(solution)/shard_map/all_to_all | solution.py:254
  473.9 4.9 all-to-all-start.3
  478.8 0.0 copy-start
  478.8 2.2 copy-done
  481.0 4.9 combine.2
  485.8 85.4 %all-to-all-done.3.back_ref = bf16[16,256,512]{2,1,0:T(8,128)(2,1)} async-done(((bf16[16,256,512]{2,1,0:T(8,128)(2,1)}), bf16[16,256,512]{2,1,0:T(8,128)(2,1)}, u32[]{:S(2)}, u32[]{:S(2)}) %all-to-all-start.3) | async-done | bytes 4194336 | tf_op jit(solution)/shard_map/all_to_all | solution.py:254
  571.3 0.0 copy-start.1
  571.3 2.2 copy-done.1
  573.5 4.9 combine.3
Async XLA Ops:
  141.7 136.2 %all-to-all-start.2 = ((bf16[16,256,512]{2,1,0:T(8,128)(2,1)}), bf16[16,256,512]{2,1,0:T(8,128)(2,1)}, u32[]{:S(2)}, u32[]{:S(2)}) async-start(bf16[16,256,512]{2,1,0:T(8,128)(2,1)} %gather_blocks.3), calls=%async_computation.2 | async-start | bytes 8388608 | tf_op jit(solution)/shard_map/all_to_all | solution.py:254
  277.8 6.3 %copy-start.2 = (bf16[1024,1024]{1,0:T(8,128)(2,1)S(1)}, bf16[1024,1024]{1,0:T(8,128)(2,1)}, u32[]{:S(2)}) copy-start(bf16[1024,1024]{1,0:T(8,128)(2,1)} %q_ref.3) | copy-start | bytes 6291460
  277.8 98.7 %all-to-all-start.1 = ((bf16[16,256,512]{2,1,0:T(8,128)(2,1)}), bf16[16,256,512]{2,1,0:T(8,128)(2,1)}, u32[]{:S(2)}, u32[]{:S(2)}) async-start(bf16[16,256,512]{2,1,0:T(8,128)(2,1)} %gather_blocks.2), calls=%async_computation.1 | async-start | bytes 8388608 | tf_op jit(solution)/shard_map/all_to_all | solution.py:254
  284.1 1.6 copy-start.3
  376.5 97.4 %all-to-all-start.4 = ((bf16[16,256,512]{2,1,0:T(8,128)(2,1)}), bf16[16,256,512]{2,1,0:T(8,128)(2,1)}, u32[]{:S(2)}, u32[]{:S(2)}) async-start(bf16[16,256,512]{2,1,0:T(8,128)(2,1)} %get-tuple-element.18), calls=%async_computation.4 | async-start | bytes 8388608 | tf_op jit(solution)/shard_map/all_to_all | solution.py:254
  381.4 1.6 copy-start.4
  473.9 97.4 %all-to-all-start.3 = ((bf16[16,256,512]{2,1,0:T(8,128)(2,1)}), bf16[16,256,512]{2,1,0:T(8,128)(2,1)}, u32[]{:S(2)}, u32[]{:S(2)}) async-start(bf16[16,256,512]{2,1,0:T(8,128)(2,1)} %get-tuple-element.16), calls=%async_computation.3 | async-start | bytes 8388608 | tf_op jit(solution)/shard_map/all_to_all | solution.py:254
  478.8 2.2 copy-start
  571.3 2.2 copy-start.1

commit v2 on v1

--- a/solution.py
+++ b/solution.py
@@ -23,36 +23,25 @@
     return lax.dot_general(a, b, (((1,), (0,)), ((), ())), preferred_element_type=jnp.float32)
 
 
-def gather_kernel(peers, chunk_width, chunk, ids_ref, k_ref, v_ref, out_ref, sems):
-    cols = pl.ds(chunk * chunk_width, chunk_width)
-
-    def copies(p):
-        rows = pl.ds(pl.multiple_of(ids_ref[p] * TILE, TILE), TILE)
-        return (
-            pltpu.make_async_copy(k_ref.at[rows, cols], out_ref.at[p, pl.ds(0, TILE)], sems.at[0, p]),
-            pltpu.make_async_copy(v_ref.at[rows, cols], out_ref.at[p, pl.ds(TILE, TILE)], sems.at[1, p]),
-        )
-
-    for p in range(peers):
-        for copy in copies(p):
-            copy.start()
-    for p in range(peers):
-        for copy in copies(p):
-            copy.wait()
+def gather_kernel(ids_ref, k_ref, v_ref, out_ref):
+    rows = pl.ds(pl.multiple_of(ids_ref[pl.program_id(0)] * TILE, TILE), TILE)
+    out_ref[0, :TILE, :] = k_ref[rows, :]
+    out_ref[0, TILE:, :] = v_ref[rows, :]
 
 
 def gather_blocks(ids, key_rows, value_rows, chunk, chunk_width):
     peers = ids.shape[0]
+    rows_spec = pl.BlockSpec((key_rows.shape[0], chunk_width), lambda p, s: (0, chunk))
     return pl.pallas_call(
-        functools.partial(gather_kernel, peers, chunk_width, chunk),
+        gather_kernel,
         grid_spec=pltpu.PrefetchScalarGridSpec(
             num_scalar_prefetch=1,
-            grid=(),
-            in_specs=[pl.BlockSpec(memory_space=pl.ANY)] * 2,
-            out_specs=pl.BlockSpec(memory_space=pl.ANY),
-            scratch_shapes=[pltpu.SemaphoreType.DMA((2, peers))],
+            grid=(peers,),
+            in_specs=[rows_spec, rows_spec],
+            out_specs=pl.BlockSpec((1, 2 * TILE, chunk_width), lambda p, s: (p, 0, 0)),
         ),
         out_shape=jax.ShapeDtypeStruct((peers, 2 * TILE, chunk_width), jnp.bfloat16),
+        compiler_params=pltpu.CompilerParams(vmem_limit_bytes=VMEM_LIMIT),
         name="gather_blocks",
     )(ids, key_rows, value_rows)
 

time: 579 us -> 421 us (0.73)
  Pallas kernels: 389 us -> 144 us
  waiting for transfers between devices: 146 us -> 227 us
  local copies, waits for them, and re-layouts: 7.72 us -> 15.7 us
    pallas_call x2, Pallas kernels: 258 us -> 13.2 us  [gather_blocks(): pl.pallas_call(gather_kernel, grid_spec=pltpu.PrefetchScalarGridSpec(num_...]
    all_to_all x4, waiting for transfers between devices: 146 us -> 227 us  [exchange(): return lax.all_to_all(x, 'ctx', split_axis=0, concat_axis=0, tiled=True)]
    unnamed x10 -> x20, local copies, waits for them, and re-layouts: 7.56 us -> 15.5 us
  transfers between devices with their start and end apart: 4 -> 4, of which waited for: 3 -> 4; matrix products, arithmetic and copies ran while one was open for 0% -> 0% of each run, Pallas kernels for 44% -> 31%
where the time goes in v2:
time: 421 us
  waiting for transfers between devices  227 us (54%)
  Pallas kernels  144 us (34%)
  starting transfers between devices  21.9 us (5%)
  local copies, waits for them, and re-layouts  15.7 us (4%)
  blocking collectives  10.1 us (2%)
    all_to_all x4, waiting for transfers between devices, exchange(): return lax.all_to_all(x, 'ctx', split_axis=0, concat_axis=0, tiled=True)  227 us
    pallas_call x2, Pallas kernels, attend(): pl.pallas_call(functools.partial(attend_kernel, peers, blocks, picks, pre...  121 us
    all_to_all x4, starting transfers between devices, exchange(): return lax.all_to_all(x, 'ctx', split_axis=0, concat_axis=0, tiled=True)  21.9 us
    unnamed x20, local copies, waits for them, and re-layouts  15.5 us
    pallas_call x2, Pallas kernels, gather_blocks(): pl.pallas_call(gather_kernel, grid_spec=pltpu.PrefetchScalarGridSpec(num_...  13.2 us
    all_to_all x1, blocking collectives, exchange(): return lax.all_to_all(x, 'ctx', split_axis=0, concat_axis=0, tiled=True)  10.1 us
    pallas_call x2, Pallas kernels, combine(): pl.pallas_call(functools.partial(combine_kernel, peers, blocks, previous...  9.73 us
  transfers between devices with their start and end apart: 4, of which 4 were waited for; matrix products, arithmetic and copies ran while one was open for 0% of the time, Pallas kernels for 31%

profile of v2, /device:TPU:13, one launch (start us, length us, event | category | flops | bytes accessed | tf_op | source)
XLA Modules:
  0.0 420.6 jit_solution(9743219509320253860)
XLA Ops:
  0.6 0.7 add_select_fusion
  1.3 0.1 select_reduce_fusion
  1.4 0.1 copy.13
  1.5 10.1 %all_to_all.31 = s32[16,1,1]{2,1,0:T(1,128)S(1)} all-to-all(s32[16,1,1]{2,1,0:T(1,128)S(1)} %copy.13), channel_id=1, replica_groups=mesh['groups'=2,'ctx'=16] {'ctx'}, dimensions={0} | all-to-all | bytes 128 | tf_op jit(solution)/shard_map/all_to_all | solution.py:243
  11.7 0.4 reduce.ids_ref
  12.0 0.0 copy-start
  12.1 1.6 copy-done
  13.6 1.6 copy-done.2
  15.2 6.6 %gather_blocks.3 = bf16[16,256,512]{2,1,0:T(8,128)(2,1)} custom-call(s32[16]{0:T(128)S(1)} %broadcast_maximum_fusion.ids_ref, bf16[1024,1024]{1,0:T(8,128)(2,1)S(1)} %copy-done, bf16[1024,1024]{1,0:T(8,128)(2,1)S(1)} %copy-done.2), custom_call_target="tpu_custom_call" | custom-call | tf_op jit(solution)/shard_map/gather_blocks/pallas_call | solution.py:35
  21.8 7.2 %all-to-all-start.2 = ((bf16[16,256,512]{2,1,0:T(8,128)(2,1)}), bf16[16,256,512]{2,1,0:T(8,128)(2,1)}, u32[]{:S(2)}, u32[]{:S(2)}) async-start(bf16[16,256,512]{2,1,0:T(8,128)(2,1)} %gather_blocks.3), calls=%async_computation.2 | async-start | bytes 8388608 | tf_op jit(solution)/shard_map/all_to_all | solution.py:243
  29.0 0.0 copy-done.1
  29.0 0.0 copy-start.3
  29.0 1.6 copy-done.3
  30.6 6.6 %gather_blocks.2 = bf16[16,256,512]{2,1,0:T(8,128)(2,1)} custom-call(s32[16]{0:T(128)S(1)} %broadcast_maximum_fusion.ids_ref, bf16[1024,1024]{1,0:T(8,128)(2,1)S(1)} %copy-done.1, bf16[1024,1024]{1,0:T(8,128)(2,1)S(1)} %copy-done.3), custom_call_target="tpu_custom_call" | custom-call | tf_op jit(solution)/shard_map/gather_blocks/pallas_call | solution.py:35
  37.2 84.3 %all-to-all-done.2.recv_ref = bf16[16,256,512]{2,1,0:T(8,128)(2,1)} async-done(((bf16[16,256,512]{2,1,0:T(8,128)(2,1)}), bf16[16,256,512]{2,1,0:T(8,128)(2,1)}, u32[]{:S(2)}, u32[]{:S(2)}) %all-to-all-start.2) | async-done | bytes 4194336 | tf_op jit(solution)/shard_map/all_to_all | solution.py:243
  121.5 4.9 %all-to-all-start.1 = ((bf16[16,256,512]{2,1,0:T(8,128)(2,1)}), bf16[16,256,512]{2,1,0:T(8,128)(2,1)}, u32[]{:S(2)}, u32[]{:S(2)}) async-start(bf16[16,256,512]{2,1,0:T(8,128)(2,1)} %gather_blocks.2), calls=%async_computation.1 | async-start | bytes 8388608 | tf_op jit(solution)/shard_map/all_to_all | solution.py:243
  126.3 0.1 reshape.13.slots_ref
  126.4 1.6 copy-done.6
  128.0 1.6 copy-done.8
  129.6 60.4 %attend.2 = (bf16[1024,1024]{1,0:T(8,128)(2,1)}, f32[2,1024,512]{2,1,0:T(8,128)}, bf16[16,256,512]{2,1,0:T(8,128)(2,1)}) custom-call(s32[64]{0:T(128)S(1)} %reshape.13.slots_ref, bf16[1024,1024]{1,0:T(8,128)(2,1)S(1)} %copy-done.6, bf16[1024,1024]{1,0:T(8,128)(2,1)S(1)} %copy-done.8, bf16[1024,1024]{1,0:T(8,128)(2,1)} %k_ref.7, bf16[1024,1024]{1,0:T(8,128)(2,1)} %v_ref.7, ...), custom_call_target="tpu_custom_call" | custom-call | flops 12079595520 | bytes 25165824 | tf_op jit(solution)/shard_map/attend/pallas_call | solution.py:150
  190.0 28.8 %all-to-all-done.1.recv_ref = bf16[16,256,512]{2,1,0:T(8,128)(2,1)} async-done(((bf16[16,256,512]{2,1,0:T(8,128)(2,1)}), bf16[16,256,512]{2,1,0:T(8,128)(2,1)}, u32[]{:S(2)}, u32[]{:S(2)}) %all-to-all-start.1) | async-done | bytes 4194336 | tf_op jit(solution)/shard_map/all_to_all | solution.py:243
  218.8 4.9 %all-to-all-start.4 = ((bf16[16,256,512]{2,1,0:T(8,128)(2,1)}), bf16[16,256,512]{2,1,0:T(8,128)(2,1)}, u32[]{:S(2)}, u32[]{:S(2)}) async-start(bf16[16,256,512]{2,1,0:T(8,128)(2,1)} %get-tuple-element.18), calls=%async_computation.4 | async-start | bytes 8388608 | tf_op jit(solution)/shard_map/all_to_all | solution.py:243
  223.7 1.6 copy-done.7
  225.3 1.6 copy-done.9
  226.9 60.5 %attend.3 = (bf16[1024,1024]{1,0:T(8,128)(2,1)}, f32[2,1024,512]{2,1,0:T(8,128)}, bf16[16,256,512]{2,1,0:T(8,128)(2,1)}) custom-call(s32[64]{0:T(128)S(1)} %reshape.13.slots_ref, bf16[1024,1024]{1,0:T(8,128)(2,1)S(1)} %copy-done.7, bf16[1024,1024]{1,0:T(8,128)(2,1)S(1)} %copy-done.9, bf16[1024,1024]{1,0:T(8,128)(2,1)} %k_ref.7, ...), custom_call_target="tpu_custom_call", output_to_operand_aliasing={{0}: (6, {})} | custom-call | flops 12079595520 | bytes 25165824 | tf_op jit(solution)/shard_map/attend/pallas_call | solution.py:150
  287.4 28.7 %all-to-all-done.4.back_ref = bf16[16,256,512]{2,1,0:T(8,128)(2,1)} async-done(((bf16[16,256,512]{2,1,0:T(8,128)(2,1)}), bf16[16,256,512]{2,1,0:T(8,128)(2,1)}, u32[]{:S(2)}, u32[]{:S(2)}) %all-to-all-start.4) | async-done | bytes 4194336 | tf_op jit(solution)/shard_map/all_to_all | solution.py:243
  316.2 4.9 %all-to-all-start.3 = ((bf16[16,256,512]{2,1,0:T(8,128)(2,1)}), bf16[16,256,512]{2,1,0:T(8,128)(2,1)}, u32[]{:S(2)}, u32[]{:S(2)}) async-start(bf16[16,256,512]{2,1,0:T(8,128)(2,1)} %get-tuple-element.16), calls=%async_computation.3 | async-start | bytes 8388608 | tf_op jit(solution)/shard_map/all_to_all | solution.py:243
  321.1 2.2 copy-done.4
  323.3 4.9 %combine.2 = (bf16[1024,1024]{1,0:T(8,128)(2,1)}, bf16[1024,1024]{1,0:T(8,128)(2,1)}) custom-call(s32[16]{0:T(128)S(1)} %reduce.ids_ref, f32[2,1024,512]{2,1,0:T(8,128)S(1)} %copy-done.4, bf16[16,256,512]{2,1,0:T(8,128)(2,1)} %all-to-all-done.4.back_ref), custom_call_target="tpu_custom_call" | custom-call | bytes 12582912 | tf_op jit(solution)/shard_map/combine/pallas_call | solution.py:225
  328.1 85.4 %all-to-all-done.3.back_ref = bf16[16,256,512]{2,1,0:T(8,128)(2,1)} async-done(((bf16[16,256,512]{2,1,0:T(8,128)(2,1)}), bf16[16,256,512]{2,1,0:T(8,128)(2,1)}, u32[]{:S(2)}, u32[]{:S(2)}) %all-to-all-start.3) | async-done | bytes 4194336 | tf_op jit(solution)/shard_map/all_to_all | solution.py:243
  413.6 2.2 copy-done.5
  415.7 4.9 %combine.3 = (bf16[1024,1024]{1,0:T(8,128)(2,1)}, bf16[1024,1024]{1,0:T(8,128)(2,1)}) custom-call(s32[16]{0:T(128)S(1)} %reduce.ids_ref, f32[2,1024,512]{2,1,0:T(8,128)S(1)} %copy-done.5, bf16[16,256,512]{2,1,0:T(8,128)(2,1)} %all-to-all-done.3.back_ref, bf16[1024,1024]{1,0:T(8,128)(2,1)} %get-tuple-element.19.rest_0_, ...), custom_call_target="tpu_custom_call", output_to_operand_aliasing={{0}: (3, {}), {1}: (4, {})} | custom-call | bytes 12582912 | tf_op jit(solution)/shard_map/combine/pallas_call | solution.py:225
  (9 shorter events, 0.0 us)
Async XLA Ops:
  12.0 1.6 copy-start
  13.6 1.6 copy-start.2
  21.8 7.2 %copy-start.1 = (bf16[1024,1024]{1,0:T(8,128)(2,1)S(1)}, bf16[1024,1024]{1,0:T(8,128)(2,1)}, u32[]{:S(2)}) copy-start(bf16[1024,1024]{1,0:T(8,128)(2,1)} %k_ref.7) | copy-start | bytes 6291460
  21.8 99.6 %all-to-all-start.2 = ((bf16[16,256,512]{2,1,0:T(8,128)(2,1)}), bf16[16,256,512]{2,1,0:T(8,128)(2,1)}, u32[]{:S(2)}, u32[]{:S(2)}) async-start(bf16[16,256,512]{2,1,0:T(8,128)(2,1)} %gather_blocks.3), calls=%async_computation.2 | async-start | bytes 8388608 | tf_op jit(solution)/shard_map/all_to_all | solution.py:243
  29.0 1.6 copy-start.3
  121.5 97.4 %all-to-all-start.1 = ((bf16[16,256,512]{2,1,0:T(8,128)(2,1)}), bf16[16,256,512]{2,1,0:T(8,128)(2,1)}, u32[]{:S(2)}, u32[]{:S(2)}) async-start(bf16[16,256,512]{2,1,0:T(8,128)(2,1)} %gather_blocks.2), calls=%async_computation.1 | async-start | bytes 8388608 | tf_op jit(solution)/shard_map/all_to_all | solution.py:243
  126.4 1.6 copy-start.6
  128.0 1.6 copy-start.8
  218.8 97.4 %all-to-all-start.4 = ((bf16[16,256,512]{2,1,0:T(8,128)(2,1)}), bf16[16,256,512]{2,1,0:T(8,128)(2,1)}, u32[]{:S(2)}, u32[]{:S(2)}) async-start(bf16[16,256,512]{2,1,0:T(8,128)(2,1)} %get-tuple-element.18), calls=%async_computation.4 | async-start | bytes 8388608 | tf_op jit(solution)/shard_map/all_to_all | solution.py:243
  223.7 1.6 copy-start.7
  225.3 1.6 copy-start.9
  316.2 97.4 %all-to-all-start.3 = ((bf16[16,256,512]{2,1,0:T(8,128)(2,1)}), bf16[16,256,512]{2,1,0:T(8,128)(2,1)}, u32[]{:S(2)}, u32[]{:S(2)}) async-start(bf16[16,256,512]{2,1,0:T(8,128)(2,1)} %get-tuple-element.16), calls=%async_computation.3 | async-start | bytes 8388608 | tf_op jit(solution)/shard_map/all_to_all | solution.py:243
  321.1 2.2 copy-start.4
  413.6 2.2 copy-start.5

commit v3 on v1

--- a/solution.py
+++ b/solution.py
@@ -12,7 +12,7 @@
 PAIR = 2 * HD
 LOG2E = 1.4426950408889634
 CHUNKS = 2
-VMEM_LIMIT = 48 * 1024 * 1024
+VMEM_LIMIT = 60 * 1024 * 1024
 
 
 def dot_nt(a, b):
@@ -23,14 +23,12 @@
     return lax.dot_general(a, b, (((1,), (0,)), ((), ())), preferred_element_type=jnp.float32)
 
 
-def gather_kernel(peers, chunk_width, chunk, ids_ref, k_ref, v_ref, out_ref, sems):
-    cols = pl.ds(chunk * chunk_width, chunk_width)
-
+def gather_kernel(peers, ids_ref, k_ref, v_ref, out_ref, sems):
     def copies(p):
-        rows = pl.ds(pl.multiple_of(ids_ref[p] * TILE, TILE), TILE)
+        rows = pl.ds(pl.multiple_of(jnp.maximum(ids_ref[p], 0) * TILE, TILE), TILE)
         return (
-            pltpu.make_async_copy(k_ref.at[rows, cols], out_ref.at[p, pl.ds(0, TILE)], sems.at[0, p]),
-            pltpu.make_async_copy(v_ref.at[rows, cols], out_ref.at[p, pl.ds(TILE, TILE)], sems.at[1, p]),
+            pltpu.make_async_copy(k_ref.at[rows], out_ref.at[p, pl.ds(0, TILE)], sems.at[0, p]),
+            pltpu.make_async_copy(v_ref.at[rows], out_ref.at[p, pl.ds(TILE, TILE)], sems.at[1, p]),
         )
 
     for p in range(peers):
@@ -43,16 +41,18 @@
 
 def gather_blocks(ids, key_rows, value_rows, chunk, chunk_width):
     peers = ids.shape[0]
+    rows_spec = pl.BlockSpec((key_rows.shape[0], chunk_width), lambda i, s: (0, chunk))
     return pl.pallas_call(
-        functools.partial(gather_kernel, peers, chunk_width, chunk),
+        functools.partial(gather_kernel, peers),
         grid_spec=pltpu.PrefetchScalarGridSpec(
             num_scalar_prefetch=1,
-            grid=(),
-            in_specs=[pl.BlockSpec(memory_space=pl.ANY)] * 2,
+            grid=(1,),
+            in_specs=[rows_spec, rows_spec],
             out_specs=pl.BlockSpec(memory_space=pl.ANY),
             scratch_shapes=[pltpu.SemaphoreType.DMA((2, peers))],
         ),
         out_shape=jax.ShapeDtypeStruct((peers, 2 * TILE, chunk_width), jnp.bfloat16),
+        compiler_params=pltpu.CompilerParams(vmem_limit_bytes=VMEM_LIMIT),
         name="gather_blocks",
     )(ids, key_rows, value_rows)
 
@@ -220,7 +220,7 @@
     peers, _, chunk_width = returned.shape
     rows = own.shape[1]
     blocks = rows // TILE
-    step = 2 * PAIR
+    step = PAIR
     base = chunk * (chunk_width // step)
     in_specs = [
         pl.BlockSpec((2, rows, step), lambda i, s: (0, 0, i)),
@@ -264,12 +264,11 @@
     matches = owners[:, :, None] == peer_range[None, None, :]
     wanted = jnp.max(jnp.where(matches, local_ids[:, :, None], -1), axis=(0, 1))
     requested = exchange(wanted)
-    serve_ids = jnp.maximum(requested, 0)
     slots = owners.reshape(-1)
     chunk_width = width // CHUNKS
 
     received = [
-        exchange(gather_blocks(serve_ids, key_rows, value_rows, c, chunk_width)) for c in range(CHUNKS)
+        exchange(gather_blocks(requested, key_rows, value_rows, c, chunk_width)) for c in range(CHUNKS)
     ]
     grad_queries = None
     owns, backs = [], []

time: 579 us -> 416 us (0.72)
  Pallas kernels: 389 us -> 142 us
  waiting for transfers between devices: 146 us -> 238 us
  local copies, waits for them, and re-layouts: 7.72 us -> 0.68 us
    pallas_call x2, Pallas kernels: 258 us -> 8.85 us  [gather_blocks(): pl.pallas_call(functools.partial(gather_kernel, peers), grid_spec=pltpu.P...]
    all_to_all x4, waiting for transfers between devices: 146 us -> 238 us  [exchange(): return lax.all_to_all(x, 'ctx', split_axis=0, concat_axis=0, tiled=True)]
    unnamed x10 -> x0, local copies, waits for them, and re-layouts: 7.56 us -> none
  transfers between devices with their start and end apart: 4 -> 4, of which waited for: 3 -> 4; matrix products, arithmetic and copies ran while one was open for 0% -> 0% of each run, Pallas kernels for 44% -> 32%
where the time goes in v3:
time: 416 us; the launch traced here: 415 us
  waiting for transfers between devices  238 us (57%)
  Pallas kernels  142 us (34%)
  starting transfers between devices  21.7 us (5%)
  blocking collectives  10.1 us (2%)
    all_to_all x4, waiting for transfers between devices, exchange(): return lax.all_to_all(x, 'ctx', split_axis=0, concat_axis=0, tiled=True)  238 us
    pallas_call x2, Pallas kernels, attend(): pl.pallas_call(functools.partial(attend_kernel, peers, blocks, picks, pre...  120 us
    all_to_all x4, starting transfers between devices, exchange(): return lax.all_to_all(x, 'ctx', split_axis=0, concat_axis=0, tiled=True)  21.7 us
    pallas_call x2, Pallas kernels, combine(): pl.pallas_call(functools.partial(combine_kernel, peers, blocks, previous...  13.6 us
    all_to_all x1, blocking collectives, exchange(): return lax.all_to_all(x, 'ctx', split_axis=0, concat_axis=0, tiled=True)  10.1 us
    pallas_call x2, Pallas kernels, gather_blocks(): pl.pallas_call(functools.partial(gather_kernel, peers), grid_spec=pltpu.P...  8.85 us
  transfers between devices with their start and end apart: 4, of which 4 were waited for; matrix products, arithmetic and copies ran while one was open for 0% of the time, Pallas kernels for 32%

profile of v3, /device:TPU:13, one launch (start us, length us, event | category | flops | bytes accessed | tf_op | source)
XLA Modules:
  0.0 415.4 jit_solution(12103108128837894067)
XLA Ops:
  0.6 0.7 add_select_fusion
  1.3 0.1 select_reduce_fusion
  1.4 0.1 copy.13
  1.5 10.1 %all_to_all.31 = s32[16,1,1]{2,1,0:T(1,128)S(1)} all-to-all(s32[16,1,1]{2,1,0:T(1,128)S(1)} %copy.13), channel_id=1, replica_groups=mesh['groups'=2,'ctx'=16] {'ctx'}, dimensions={0} | all-to-all | bytes 128 | tf_op jit(solution)/shard_map/all_to_all | solution.py:254
  11.7 0.9 reduce.ids_ref
  12.6 4.4 %gather_blocks.3 = bf16[16,256,512]{2,1,0:T(8,128)(2,1)} custom-call(s32[16]{0:T(128)} %reduce.ids_ref, bf16[1024,1024]{1,0:T(8,128)(2,1)} %k_ref.7, bf16[1024,1024]{1,0:T(8,128)(2,1)} %v_ref.7), custom_call_target="tpu_custom_call" | custom-call | tf_op jit(solution)/shard_map/gather_blocks/pallas_call | solution.py:45
  17.0 7.0 %all-to-all-start.2 = ((bf16[16,256,512]{2,1,0:T(8,128)(2,1)}), bf16[16,256,512]{2,1,0:T(8,128)(2,1)}, u32[]{:S(2)}, u32[]{:S(2)}) async-start(bf16[16,256,512]{2,1,0:T(8,128)(2,1)} %gather_blocks.3), calls=%async_computation.2 | async-start | bytes 8388608 | tf_op jit(solution)/shard_map/all_to_all | solution.py:254
  24.1 4.4 %gather_blocks.2 = bf16[16,256,512]{2,1,0:T(8,128)(2,1)} custom-call(s32[16]{0:T(128)} %reduce.ids_ref, bf16[1024,1024]{1,0:T(8,128)(2,1)} %k_ref.7, bf16[1024,1024]{1,0:T(8,128)(2,1)} %v_ref.7), custom_call_target="tpu_custom_call" | custom-call | tf_op jit(solution)/shard_map/gather_blocks/pallas_call | solution.py:45
  28.5 88.0 %all-to-all-done.2.recv_ref = bf16[16,256,512]{2,1,0:T(8,128)(2,1)} async-done(((bf16[16,256,512]{2,1,0:T(8,128)(2,1)}), bf16[16,256,512]{2,1,0:T(8,128)(2,1)}, u32[]{:S(2)}, u32[]{:S(2)}) %all-to-all-start.2) | async-done | bytes 4194336 | tf_op jit(solution)/shard_map/all_to_all | solution.py:254
  116.5 4.9 %all-to-all-start.1 = ((bf16[16,256,512]{2,1,0:T(8,128)(2,1)}), bf16[16,256,512]{2,1,0:T(8,128)(2,1)}, u32[]{:S(2)}, u32[]{:S(2)}) async-start(bf16[16,256,512]{2,1,0:T(8,128)(2,1)} %gather_blocks.2), calls=%async_computation.1 | async-start | bytes 8388608 | tf_op jit(solution)/shard_map/all_to_all | solution.py:254
  121.4 0.6 reshape.13.slots_ref
  122.0 59.9 %attend.2 = (bf16[1024,1024]{1,0:T(8,128)(2,1)}, f32[2,1024,512]{2,1,0:T(8,128)}, bf16[16,256,512]{2,1,0:T(8,128)(2,1)}) custom-call(s32[64]{0:T(128)} %reshape.13.slots_ref, bf16[1024,1024]{1,0:T(8,128)(2,1)} %q_ref.3, bf16[1024,1024]{1,0:T(8,128)(2,1)} %g_ref.3, bf16[1024,1024]{1,0:T(8,128)(2,1)} %k_ref.7, bf16[1024,1024]{1,0:T(8,128)(2,1)} %v_ref.7, ...), custom_call_target="tpu_custom_call" | custom-call | flops 12079595520 | bytes 25165824 | tf_op jit(solution)/shard_map/attend/pallas_call | solution.py:161
  181.9 32.0 %all-to-all-done.1.recv_ref = bf16[16,256,512]{2,1,0:T(8,128)(2,1)} async-done(((bf16[16,256,512]{2,1,0:T(8,128)(2,1)}), bf16[16,256,512]{2,1,0:T(8,128)(2,1)}, u32[]{:S(2)}, u32[]{:S(2)}) %all-to-all-start.1) | async-done | bytes 4194336 | tf_op jit(solution)/shard_map/all_to_all | solution.py:254
  213.9 4.9 %all-to-all-start.4 = ((bf16[16,256,512]{2,1,0:T(8,128)(2,1)}), bf16[16,256,512]{2,1,0:T(8,128)(2,1)}, u32[]{:S(2)}, u32[]{:S(2)}) async-start(bf16[16,256,512]{2,1,0:T(8,128)(2,1)} %get-tuple-element.18), calls=%async_computation.4 | async-start | bytes 8388608 | tf_op jit(solution)/shard_map/all_to_all | solution.py:254
  218.8 60.0 %attend.3 = (bf16[1024,1024]{1,0:T(8,128)(2,1)}, f32[2,1024,512]{2,1,0:T(8,128)}, bf16[16,256,512]{2,1,0:T(8,128)(2,1)}) custom-call(s32[64]{0:T(128)} %reshape.13.slots_ref, bf16[1024,1024]{1,0:T(8,128)(2,1)} %q_ref.3, bf16[1024,1024]{1,0:T(8,128)(2,1)} %g_ref.3, bf16[1024,1024]{1,0:T(8,128)(2,1)} %k_ref.7, ...), custom_call_target="tpu_custom_call", output_to_operand_aliasing={{0}: (6, {})} | custom-call | flops 12079595520 | bytes 25165824 | tf_op jit(solution)/shard_map/attend/pallas_call | solution.py:161
  278.8 32.5 %all-to-all-done.4.back_ref = bf16[16,256,512]{2,1,0:T(8,128)(2,1)} async-done(((bf16[16,256,512]{2,1,0:T(8,128)(2,1)}), bf16[16,256,512]{2,1,0:T(8,128)(2,1)}, u32[]{:S(2)}, u32[]{:S(2)}) %all-to-all-start.4) | async-done | bytes 4194336 | tf_op jit(solution)/shard_map/all_to_all | solution.py:254
  311.3 4.9 %all-to-all-start.3 = ((bf16[16,256,512]{2,1,0:T(8,128)(2,1)}), bf16[16,256,512]{2,1,0:T(8,128)(2,1)}, u32[]{:S(2)}, u32[]{:S(2)}) async-start(bf16[16,256,512]{2,1,0:T(8,128)(2,1)} %get-tuple-element.16), calls=%async_computation.3 | async-start | bytes 8388608 | tf_op jit(solution)/shard_map/all_to_all | solution.py:254
  316.2 6.8 %combine.2 = (bf16[1024,1024]{1,0:T(8,128)(2,1)}, bf16[1024,1024]{1,0:T(8,128)(2,1)}) custom-call(s32[16]{0:T(128)} %reduce.ids_ref, f32[2,1024,512]{2,1,0:T(8,128)} %get-tuple-element.17.own_ref, bf16[16,256,512]{2,1,0:T(8,128)(2,1)} %all-to-all-done.4.back_ref), custom_call_target="tpu_custom_call" | custom-call | bytes 12582912 | tf_op jit(solution)/shard_map/combine/pallas_call | solution.py:236
  323.0 85.7 %all-to-all-done.3.back_ref = bf16[16,256,512]{2,1,0:T(8,128)(2,1)} async-done(((bf16[16,256,512]{2,1,0:T(8,128)(2,1)}), bf16[16,256,512]{2,1,0:T(8,128)(2,1)}, u32[]{:S(2)}, u32[]{:S(2)}) %all-to-all-start.3) | async-done | bytes 4194336 | tf_op jit(solution)/shard_map/all_to_all | solution.py:254
  408.7 6.8 %combine.3 = (bf16[1024,1024]{1,0:T(8,128)(2,1)}, bf16[1024,1024]{1,0:T(8,128)(2,1)}) custom-call(s32[16]{0:T(128)} %reduce.ids_ref, f32[2,1024,512]{2,1,0:T(8,128)} %get-tuple-element.15.own_ref, bf16[16,256,512]{2,1,0:T(8,128)(2,1)} %all-to-all-done.3.back_ref, ...), custom_call_target="tpu_custom_call", output_to_operand_aliasing={{0}: (3, {}), {1}: (4, {})} | custom-call | bytes 12582912 | tf_op jit(solution)/shard_map/combine/pallas_call | solution.py:236
Async XLA Ops:
  17.0 99.5 %all-to-all-start.2 = ((bf16[16,256,512]{2,1,0:T(8,128)(2,1)}), bf16[16,256,512]{2,1,0:T(8,128)(2,1)}, u32[]{:S(2)}, u32[]{:S(2)}) async-start(bf16[16,256,512]{2,1,0:T(8,128)(2,1)} %gather_blocks.3), calls=%async_computation.2 | async-start | bytes 8388608 | tf_op jit(solution)/shard_map/all_to_all | solution.py:254
  116.5 97.4 %all-to-all-start.1 = ((bf16[16,256,512]{2,1,0:T(8,128)(2,1)}), bf16[16,256,512]{2,1,0:T(8,128)(2,1)}, u32[]{:S(2)}, u32[]{:S(2)}) async-start(bf16[16,256,512]{2,1,0:T(8,128)(2,1)} %gather_blocks.2), calls=%async_computation.1 | async-start | bytes 8388608 | tf_op jit(solution)/shard_map/all_to_all | solution.py:254
  213.9 97.4 %all-to-all-start.4 = ((bf16[16,256,512]{2,1,0:T(8,128)(2,1)}), bf16[16,256,512]{2,1,0:T(8,128)(2,1)}, u32[]{:S(2)}, u32[]{:S(2)}) async-start(bf16[16,256,512]{2,1,0:T(8,128)(2,1)} %get-tuple-element.18), calls=%async_computation.4 | async-start | bytes 8388608 | tf_op jit(solution)/shard_map/all_to_all | solution.py:254
  311.3 97.4 %all-to-all-start.3 = ((bf16[16,256,512]{2,1,0:T(8,128)(2,1)}), bf16[16,256,512]{2,1,0:T(8,128)(2,1)}, u32[]{:S(2)}, u32[]{:S(2)}) async-start(bf16[16,256,512]{2,1,0:T(8,128)(2,1)} %get-tuple-element.16), calls=%async_computation.3 | async-start | bytes 8388608 | tf_op jit(solution)/shard_map/all_to_all | solution.py:254

commit v4 on v3

--- a/solution.py
+++ b/solution.py
@@ -254,7 +254,271 @@
     return lax.all_to_all(x, "ctx", split_axis=0, concat_axis=0, tiled=True)
 
 
-def on_device(queries, key_rows, value_rows, grad_out, tile_keys):
+def merge_lanes(a, b):
+    low = jnp.concatenate([a[:, :HD], b[:, :HD]], axis=1)
+    high = jnp.concatenate([a[:, HD:], b[:, HD:]], axis=1)
+    return low, high
+
+
+def pack_kernel(a_ref, b_ref, out_ref):
+    out_ref[0], out_ref[1] = merge_lanes(a_ref[...], b_ref[...])
+
+
+def pack_heads(a, b, start, count):
+    rows, width = a.shape
+    tokens = count * TILE
+    first = start // count
+    spec = pl.BlockSpec((tokens, PAIR), lambda i: (first, i))
+    return pl.pallas_call(
+        pack_kernel,
+        grid=(width // PAIR,),
+        in_specs=[spec, spec],
+        out_specs=pl.BlockSpec((2, tokens, PAIR), lambda i: (i, 0, 0)),
+        out_shape=jax.ShapeDtypeStruct((width // HD, tokens, PAIR), jnp.bfloat16),
+        cost_estimate=pl.CostEstimate(
+            flops=0, bytes_accessed=8 * tokens * width, transcendentals=0
+        ),
+        compiler_params=pltpu.CompilerParams(vmem_limit_bytes=VMEM_LIMIT),
+        name="pack_heads",
+    )(a, b)
+
+
+def turn_kernel(kv_ref, out_ref):
+    for j in range(kv_ref.shape[0] // TILE):
+        out_ref[j] = kv_ref[j * TILE : (j + 1) * TILE, :].T[:HD, :]
+
+
+def turn_keys(kv):
+    total = kv.shape[0] // TILE
+    step = 8
+    return pl.pallas_call(
+        turn_kernel,
+        grid=(total // step,),
+        in_specs=[pl.BlockSpec((step * TILE, PAIR), lambda i: (i, 0))],
+        out_specs=pl.BlockSpec((step, HD, TILE), lambda i: (i, 0, 0)),
+        out_shape=jax.ShapeDtypeStruct((total, HD, TILE), jnp.bfloat16),
+        compiler_params=pltpu.CompilerParams(vmem_limit_bytes=VMEM_LIMIT),
+        name="turn_keys",
+    )(kv)
+
+
+def head_kernel(dims, *refs):
+    blocks, picks, start, count, last = dims
+    if last:
+        table_ref, qg_ref, kv_ref, kt_ref, before_ref, out_ref, acc_ref, before_scr, sem = refs[:9]
+        scratch = refs[9:]
+    else:
+        table_ref, qg_ref, kv_ref, kt_ref, out_ref, acc_ref = refs[:6]
+        scratch = refs[6:]
+    source = pl.program_id(0)
+    sources = pl.num_programs(0)
+    width = TILE * (picks + 1)
+    lane = lax.broadcasted_iota(jnp.int32, (TILE, PAIR), 1)
+    low = lane < HD
+
+    @pl.when(source == 0)
+    def _():
+        acc_ref[...] = jnp.zeros_like(acc_ref)
+        if last:
+            pltpu.make_async_copy(before_ref, before_scr, sem).start()
+
+    def fold(x, op):
+        return op(x.reshape(-1, 8, x.shape[-1]), axis=0)
+
+    def spans(block):
+        named = [table_ref[block * picks + j] for j in range(picks)] + [block]
+        return named, [pl.ds(pl.multiple_of(n * TILE, TILE), TILE) for n in named]
+
+    def one_block(local, raw_scr, pair_scr):
+        block = source * blocks + start + local
+        named, rows = spans(block)
+        qg = qg_ref[0, pl.ds(pl.multiple_of(local * TILE, TILE), TILE), :].astype(jnp.float32)
+        zero = jnp.zeros_like(qg)
+        both = jnp.concatenate(
+            [jnp.where(low, qg * (HD**-0.5), zero), jnp.where(low, zero, qg)], axis=0
+        )
+        keys = jnp.concatenate([kv_ref[r, :] for r in rows], axis=0)
+        raw = dot_nt(keys, both.astype(jnp.bfloat16))
+        raw_scr[...] = raw
+        top = jnp.max(fold(raw[:, :TILE], jnp.max), axis=0, keepdims=True)
+        total = jnp.zeros((8, TILE), jnp.float32)
+        inner = jnp.zeros((8, TILE), jnp.float32)
+        for j in range(picks + 1):
+            part = slice(j * TILE, (j + 1) * TILE)
+            p = jnp.exp2((raw_scr[part, :TILE] - top) * LOG2E)
+            raw_scr[part, :TILE] = p
+            pair_scr[part, TILE:] = p.astype(jnp.bfloat16)
+            total += fold(p, jnp.sum)
+            inner += fold(p * raw_scr[part, TILE:], jnp.sum)
+        recip = 1.0 / jnp.sum(total, axis=0, keepdims=True)
+        delta = jnp.sum(inner, axis=0, keepdims=True) * recip
+        for j in range(picks + 1):
+            part = slice(j * TILE, (j + 1) * TILE)
+            ds = raw_scr[part, :TILE] * (raw_scr[part, TILE:] - delta)
+            pair_scr[part, :TILE] = ds.astype(jnp.bfloat16)
+        column = jnp.broadcast_to(recip, (TILE, TILE)).T
+        scaled = jnp.concatenate([both[:TILE] * column, both[TILE:] * column], axis=0)
+        grads = dot_nn(pair_scr[...], scaled.astype(jnp.bfloat16))
+        for j in range(picks + 1):
+            acc_ref[rows[j], :] += grads[j * TILE : (j + 1) * TILE, :]
+        turned = jnp.concatenate([kt_ref[n] for n in named], axis=1)
+        dqt = dot_nn(turned, pair_scr[:, :TILE])
+        return dqt * (recip * (HD**-0.5))
+
+    offset = blocks * TILE if last else 0
+
+    def two_blocks(m, carry):
+        first = one_block(2 * m, scratch[0], scratch[1])
+        second = one_block(2 * m + 1, scratch[2], scratch[3])
+        both = jnp.concatenate([first, second], axis=0).T.astype(jnp.bfloat16)
+        if last:
+            out_ref[source, pl.ds(pl.multiple_of(offset + m * TILE, TILE), TILE), :] = both
+        else:
+            out_ref[0, pl.ds(pl.multiple_of(m * TILE, TILE), TILE), :] = both
+        return carry
+
+    lax.fori_loop(0, count // 2, two_blocks, 0)
+
+    if last:
+
+        @pl.when(source == sources - 1)
+        def _():
+            pltpu.make_async_copy(before_ref, before_scr, sem).wait()
+
+            def finish(s, carry):
+                rows = pl.ds(pl.multiple_of(s * blocks * TILE, TILE), blocks * TILE)
+                out_ref[s, : blocks * TILE, :] = (acc_ref[rows, :] + before_scr[rows, :]).astype(
+                    jnp.bfloat16
+                )
+                return carry
+
+            lax.fori_loop(0, sources, finish, 0)
+
+
+def attend_head(table, qg, kv, turned, before, blocks, start):
+    peers, tokens, _ = qg.shape
+    total = kv.shape[0]
+    count = tokens // TILE
+    picks = table.shape[0] // (total // TILE)
+    last = before is not None
+    keys = TILE * (picks + 1)
+    in_specs = [
+        pl.BlockSpec((1, tokens, PAIR), lambda i, t: (i, 0, 0)),
+        pl.BlockSpec((total, PAIR), lambda i, t: (0, 0)),
+        pl.BlockSpec(turned.shape, lambda i, t: (0, 0, 0)),
+    ]
+    operands = [table, qg, kv, turned]
+    acc_shape = (total, PAIR)
+    scratch = [
+        pltpu.VMEM((keys, 2 * TILE), jnp.float32),
+        pltpu.VMEM((keys, 2 * TILE), jnp.bfloat16),
+        pltpu.VMEM((keys, 2 * TILE), jnp.float32),
+        pltpu.VMEM((keys, 2 * TILE), jnp.bfloat16),
+    ]
+    if last:
+        in_specs.append(pl.BlockSpec(memory_space=pl.ANY))
+        operands.append(before)
+        packed = (peers, (blocks + count // 2) * TILE, PAIR)
+        out_specs = pl.BlockSpec(packed, lambda i, t: (0, 0, 0))
+        out_shape = jax.ShapeDtypeStruct(packed, jnp.bfloat16)
+        scratch = [
+            pltpu.VMEM(acc_shape, jnp.float32),
+            pltpu.VMEM(acc_shape, jnp.float32),
+            pltpu.SemaphoreType.DMA,
+        ] + scratch
+    else:
+        out_specs = [
+            pl.BlockSpec((1, tokens // 2, PAIR), lambda i, t: (i, 0, 0)),
+            pl.BlockSpec(acc_shape, lambda i, t: (0, 0)),
+        ]
+        out_shape = [
+            jax.ShapeDtypeStruct((peers, tokens // 2, PAIR), jnp.bfloat16),
+            jax.ShapeDtypeStruct(acc_shape, jnp.float32),
+        ]
+    return pl.pallas_call(
+        functools.partial(head_kernel, (blocks, picks, start, count, last)),
+        grid_spec=pltpu.PrefetchScalarGridSpec(
+            num_scalar_prefetch=1,
+            grid=(peers,),
+            in_specs=in_specs,
+            out_specs=out_specs,
+            scratch_shapes=scratch,
+        ),
+        out_shape=out_shape,
+        cost_estimate=pl.CostEstimate(
+            flops=5 * 2 * 2 * TILE * PAIR * keys * peers * count // 2,
+            bytes_accessed=24 * 1024 * 1024,
+            transcendentals=peers * count * keys * TILE,
+        ),
+        compiler_params=pltpu.CompilerParams(vmem_limit_bytes=VMEM_LIMIT),
+        name="attend_head",
+    )(*operands)
+
+
+def unpack_kernel(blocks, start, count, last, in_ref, *refs):
+    refs = refs[-3:] if last else refs[-1:]
+    gq_ref = refs[0]
+    offset = 0
+    if last:
+        offset = blocks * TILE
+        refs[1][...], refs[2][...] = merge_lanes(in_ref[0, :offset, :], in_ref[1, :offset, :])
+    for m in range(count // 2):
+        rows = slice(offset + m * TILE, offset + (m + 1) * TILE)
+        even, odd = merge_lanes(in_ref[0, rows, :], in_ref[1, rows, :])
+        gq_ref[2 * m * TILE : (2 * m + 1) * TILE, :] = even
+        gq_ref[(2 * m + 1) * TILE : (2 * m + 2) * TILE, :] = odd
+
+
+def unpack_heads(back, previous, blocks, start, count):
+    heads, tokens, _ = back.shape
+    width = heads * HD
+    last = previous is not None
+    rows = blocks * TILE
+    first = start // count
+    in_specs = [pl.BlockSpec((2, tokens, PAIR), lambda i: (i, 0, 0))]
+    operands = [back]
+    out_specs = [pl.BlockSpec((count * TILE, PAIR), lambda i: (first, i))]
+    out_shape = [jax.ShapeDtypeStruct((rows, width), jnp.bfloat16)]
+    aliases = {}
+    if last:
+        in_specs.append(pl.BlockSpec(memory_space=pl.ANY))
+        operands.append(previous)
+        aliases = {1: 0}
+        out_specs += [pl.BlockSpec((rows, PAIR), lambda i: (0, i))] * 2
+        out_shape += [out_shape[0]] * 2
+    return pl.pallas_call(
+        functools.partial(unpack_kernel, blocks, start, count, last),
+        grid=(heads // 2,),
+        in_specs=in_specs,
+        out_specs=out_specs,
+        out_shape=out_shape,
+        input_output_aliases=aliases,
+        cost_estimate=pl.CostEstimate(
+            flops=0, bytes_accessed=4 * heads * tokens * PAIR, transcendentals=0
+        ),
+        compiler_params=pltpu.CompilerParams(vmem_limit_bytes=VMEM_LIMIT),
+        name="unpack_heads",
+    )(*operands)
+
+
+def by_heads(queries, key_rows, value_rows, grad_out, tile_keys):
+    rows, _ = queries.shape
+    blocks = rows // TILE
+    half = blocks // 2
+    table = lax.all_gather(tile_keys, "ctx", tiled=True).reshape(-1)
+    kv = exchange(pack_heads(key_rows, value_rows, 0, blocks))
+    qg = [exchange(pack_heads(queries, grad_out, c * half, half)) for c in range(2)]
+    kv = kv.reshape(-1, PAIR)
+    turned = turn_keys(kv)
+    dq, before = attend_head(table, qg[0], kv, turned, None, blocks, 0)
+    back = exchange(dq)
+    packed = attend_head(table, qg[1], kv, turned, before, blocks, half)
+    final = exchange(packed)
+    grad_queries = unpack_heads(back, None, blocks, 0, half)[0]
+    return unpack_heads(final, grad_queries, blocks, half, half)
+
+
+def by_blocks(queries, key_rows, value_rows, grad_out, tile_keys):
     rows, width = queries.shape
     blocks = rows // TILE
     peers = lax.axis_size("ctx")
@@ -284,6 +548,12 @@
     return grad_queries, result[0], result[1]
 
 
+def on_device(queries, key_rows, value_rows, grad_out, tile_keys):
+    split_evenly = lax.axis_size("ctx") * HD == queries.shape[1]
+    plan = by_heads if split_evenly and queries.shape[0] % (4 * TILE) == 0 else by_blocks
+    return tuple(plan(queries, key_rows, value_rows, grad_out, tile_keys))
+
+
 def solution(mesh):
     spec = P(("groups", "ctx"), None)
     return jax.shard_map(

time: 416 us -> 539 us (1.30)
  Pallas kernels: 142 us -> 214 us
  blocking collectives: 10.1 us -> 57 us
  starting transfers between devices: 21.7 us -> 27.4 us
    pallas_call x6 -> x8, Pallas kernels: 142 us -> 214 us  [the longest x2 171 us: attend_head(): pl.pallas_call(functools.partial(head_kernel, (blocks, picks, start, coun...]
    all_gather x0 -> x1, blocking collectives: none -> 57 us  [by_heads(): table = lax.all_gather(tile_keys, 'ctx', tiled=True).reshape(-1)]
    all_to_all x1 -> x0, blocking collectives: 10.1 us -> none  [exchange(): return lax.all_to_all(x, 'ctx', split_axis=0, concat_axis=0, tiled=True)]
    all_to_all x4 -> x5, starting transfers between devices: 21.7 us -> 27.4 us  [exchange(): return lax.all_to_all(x, 'ctx', split_axis=0, concat_axis=0, tiled=True)]
    all_to_all x4 -> x5, waiting for transfers between devices: 238 us -> 236 us  [exchange(): return lax.all_to_all(x, 'ctx', split_axis=0, concat_axis=0, tiled=True)]
  transfers between devices with their start and end apart: 4 -> 5, of which waited for: 4 -> 3; matrix products, arithmetic and copies ran while one was open for 0% -> 0% of each run, Pallas kernels for 32% -> 37%
where the time goes in v4:
time: 539 us; the launch traced here: 538 us
  waiting for transfers between devices  236 us (44%)
  Pallas kernels  214 us (40%)
  blocking collectives  57 us (11%)
  starting transfers between devices  27.4 us (5%)
    all_to_all x5, waiting for transfers between devices, exchange(): return lax.all_to_all(x, 'ctx', split_axis=0, concat_axis=0, tiled=True)  236 us
    pallas_call x2, Pallas kernels, attend_head(): pl.pallas_call(functools.partial(head_kernel, (blocks, picks, start, coun...  171 us
    all_gather x1, blocking collectives, by_heads(): table = lax.all_gather(tile_keys, 'ctx', tiled=True).reshape(-1)  57 us
    all_to_all x5, starting transfers between devices, exchange(): return lax.all_to_all(x, 'ctx', split_axis=0, concat_axis=0, tiled=True)  27.4 us
    pallas_call x3, Pallas kernels, pack_heads(): pl.pallas_call(pack_kernel, grid=(width // PAIR,), in_specs=[spec, spec],...  19.6 us
    pallas_call x2, Pallas kernels, unpack_heads(): pl.pallas_call(functools.partial(unpack_kernel, blocks, start, count, las...  12.9 us
  transfers between devices with their start and end apart: 5, of which 3 were waited for; matrix products, arithmetic and copies ran while one was open for 0% of the time, Pallas kernels for 37%

profile of v4, /device:TPU:13, one launch (start us, length us, event | category | flops | bytes accessed | tf_op | source)
XLA Modules:
  0.0 537.8 jit_solution(17017283734459280493)
XLA Ops:
  0.6 6.2 %pack_heads.5 = bf16[16,512,128]{2,1,0:T(8,128)(2,1)} custom-call(bf16[1024,1024]{1,0:T(8,128)(2,1)} %a_ref.5, bf16[1024,1024]{1,0:T(8,128)(2,1)} %b_ref.5), custom_call_target="tpu_custom_call" | custom-call | bytes 4194304 | tf_op jit(solution)/shard_map/pack_heads/pallas_call | solution.py:272
  6.8 6.6 %all-to-all-start.2 = ((bf16[16,512,128]{2,1,0:T(8,128)(2,1)}), bf16[16,512,128]{2,1,0:T(8,128)(2,1)S(1)}, u32[]{:S(2)}, u32[]{:S(2)}) async-start(bf16[16,512,128]{2,1,0:T(8,128)(2,1)} %pack_heads.5), calls=%async_computation.2 | async-start | bytes 4194304 | tf_op jit(solution)/shard_map/all_to_all | solution.py:254
  13.4 7.2 %pack_heads.4 = bf16[16,1024,128]{2,1,0:T(8,128)(2,1)} custom-call(bf16[1024,1024]{1,0:T(8,128)(2,1)} %a_ref.4, bf16[1024,1024]{1,0:T(8,128)(2,1)} %b_ref.4), custom_call_target="tpu_custom_call" | custom-call | bytes 8388608 | tf_op jit(solution)/shard_map/pack_heads/pallas_call | solution.py:272
  20.6 40.2 %all-to-all-done.2.refs_1_ = bf16[16,512,128]{2,1,0:T(8,128)(2,1)S(1)} async-done(((bf16[16,512,128]{2,1,0:T(8,128)(2,1)}), bf16[16,512,128]{2,1,0:T(8,128)(2,1)S(1)}, u32[]{:S(2)}, u32[]{:S(2)}) %all-to-all-start.2) | async-done | bytes 2097184 | tf_op jit(solution)/shard_map/all_to_all | solution.py:254
  60.8 0.0 copy-start.1
  60.8 1.3 copy-done.1
  62.1 4.9 all-to-all-start.1
  67.0 6.2 %pack_heads.3 = bf16[16,512,128]{2,1,0:T(8,128)(2,1)} custom-call(bf16[1024,1024]{1,0:T(8,128)(2,1)} %a_ref.5, bf16[1024,1024]{1,0:T(8,128)(2,1)} %b_ref.5), custom_call_target="tpu_custom_call" | custom-call | bytes 4194304 | tf_op jit(solution)/shard_map/pack_heads/pallas_call | solution.py:272
  73.2 0.0 copy-start.3
  73.2 86.3 %all-to-all-done.1 = bf16[16,1024,128]{2,1,0:T(8,128)(2,1)} async-done(((bf16[16,1024,128]{2,1,0:T(8,128)(2,1)}), bf16[16,1024,128]{2,1,0:T(8,128)(2,1)}, u32[]{:S(2)}, u32[]{:S(2)}) %all-to-all-start.1) | async-done | bytes 4194336 | tf_op jit(solution)/shard_map/all_to_all | solution.py:254
  159.5 4.9 all-to-all-start
  164.4 0.0 copy-done.3
  164.4 57.0 %all_gather.3 = s32[128,8]{1,0:T(8,128)S(1)} all-gather(s32[8,8]{1,0:T(8,128)S(1)} %copy-done.3), channel_id=1, replica_groups=mesh['groups'=2,'ctx'=16] {'ctx'}, dimensions={0}, use_global_device_ids=true | all-gather | bytes 4352 | tf_op jit(solution)/shard_map/all_gather | solution.py:508
  221.4 0.7 reshape.12.refs_0_
  222.1 10.4 %turn_keys.1.refs_3_ = bf16[128,64,128]{2,1,0:T(8,128)(2,1)} custom-call(bf16[16384,128]{1,0:T(8,128)(2,1)} %bitcast.kv_ref.refs_2_), custom_call_target="tpu_custom_call" | custom-call | tf_op jit(solution)/shard_map/turn_keys/pallas_call | solution.py:294
  232.5 85.4 %attend_head.2 = (bf16[16,256,128]{2,1,0:T(8,128)(2,1)}, f32[16384,128]{1,0:T(8,128)}) custom-call(s32[1024]{0:T(1024)} %reshape.12.refs_0_, bf16[16,512,128]{2,1,0:T(8,128)(2,1)} %copy-done.1, bf16[16384,128]{1,0:T(8,128)(2,1)} %bitcast.kv_ref.refs_2_, bf16[128,64,128]{2,1,0:T(8,128)(2,1)} %turn_keys.1.refs_3_), custom_call_target="tpu_custom_call" | custom-call | flops 12079595520 | bytes 25165824 | tf_op jit(solution)/shard_map/attend_head/pallas_call | solution.py:438
  317.9 0.0 all-to-all-done.refs_1_
  317.9 0.0 copy-start.2
  317.9 5.0 all-to-all-start.4
  323.0 0.0 copy-done.2
  323.0 85.4 %attend_head.3 = bf16[16,1280,128]{2,1,0:T(8,128)(2,1)} custom-call(s32[1024]{0:T(1024)} %reshape.12.refs_0_, bf16[16,512,128]{2,1,0:T(8,128)(2,1)} %copy-done.2, bf16[16384,128]{1,0:T(8,128)(2,1)} %bitcast.kv_ref.refs_2_, bf16[128,64,128]{2,1,0:T(8,128)(2,1)} %turn_keys.1.refs_3_, f32[16384,128]{1,0:T(8,128)} %get-tuple-element.5.refs_4_), custom_call_target="tpu_custom_call" | custom-call | flops 12079595520 | bytes 25165824 | tf_op jit(solution)/shard_map/attend_head/pallas_call | solution.py:438
  408.4 0.0 all-to-all-done.4.in_ref
  408.4 0.0 copy-start
  408.4 1.0 copy-done
  409.4 6.0 %all-to-all-start.3 = ((bf16[16,1280,128]{2,1,0:T(8,128)(2,1)}), bf16[16,1280,128]{2,1,0:T(8,128)(2,1)}, u32[]{:S(2)}, u32[]{:S(2)}) async-start(bf16[16,1280,128]{2,1,0:T(8,128)(2,1)} %attend_head.3), calls=%async_computation.3 | async-start | bytes 10485760 | tf_op jit(solution)/shard_map/all_to_all | solution.py:254
  415.4 5.5 %unpack_heads.2.refs_0_ = bf16[1024,1024]{1,0:T(8,128)(2,1)} custom-call(bf16[16,256,128]{2,1,0:T(8,128)(2,1)} %copy-done), custom_call_target="tpu_custom_call" | custom-call | bytes 2097152 | tf_op jit(solution)/shard_map/unpack_heads/pallas_call | solution.py:489
  420.9 109.4 %all-to-all-done.3.in_ref = bf16[16,1280,128]{2,1,0:T(8,128)(2,1)} async-done(((bf16[16,1280,128]{2,1,0:T(8,128)(2,1)}), bf16[16,1280,128]{2,1,0:T(8,128)(2,1)}, u32[]{:S(2)}, u32[]{:S(2)}) %all-to-all-start.3) | async-done | bytes 5242912 | tf_op jit(solution)/shard_map/all_to_all | solution.py:254
  530.3 7.4 %unpack_heads.3 = (bf16[1024,1024]{1,0:T(8,128)(2,1)}, bf16[1024,1024]{1,0:T(8,128)(2,1)}, bf16[1024,1024]{1,0:T(8,128)(2,1)}) custom-call(bf16[16,1280,128]{2,1,0:T(8,128)(2,1)} %all-to-all-done.3.in_ref, bf16[1024,1024]{1,0:T(8,128)(2,1)} %unpack_heads.2.refs_0_), custom_call_target="tpu_custom_call", output_to_operand_aliasing={{0}: (1, {})} | custom-call | bytes 10485760 | tf_op jit(solution)/shard_map/unpack_heads/pallas_call | solution.py:489
Async XLA Ops:
  6.8 54.0 %all-to-all-start.2 = ((bf16[16,512,128]{2,1,0:T(8,128)(2,1)}), bf16[16,512,128]{2,1,0:T(8,128)(2,1)S(1)}, u32[]{:S(2)}, u32[]{:S(2)}) async-start(bf16[16,512,128]{2,1,0:T(8,128)(2,1)} %pack_heads.5), calls=%async_computation.2 | async-start | bytes 4194304 | tf_op jit(solution)/shard_map/all_to_all | solution.py:254
  60.8 1.3 copy-start.1
  62.1 97.4 %all-to-all-start.1 = ((bf16[16,1024,128]{2,1,0:T(8,128)(2,1)}), bf16[16,1024,128]{2,1,0:T(8,128)(2,1)}, u32[]{:S(2)}, u32[]{:S(2)}) async-start(bf16[16,1024,128]{2,1,0:T(8,128)(2,1)} %pack_heads.4), calls=%async_computation.1 | async-start | bytes 8388608 | tf_op jit(solution)/shard_map/all_to_all | solution.py:254
  73.2 91.2 %copy-start.3 = (s32[8,8]{1,0:T(8,128)S(1)}, s32[8,8]{1,0:T(8,128)}, u32[]{:S(2)}) copy-start(s32[8,8]{1,0:T(8,128)} %param.9) | copy-start | bytes 772
  159.5 158.4 %all-to-all-start = ((bf16[16,512,128]{2,1,0:T(8,128)(2,1)}), bf16[16,512,128]{2,1,0:T(8,128)(2,1)S(1)}, u32[]{:S(2)}, u32[]{:S(2)}) async-start(bf16[16,512,128]{2,1,0:T(8,128)(2,1)} %pack_heads.3), calls=%async_computation | async-start | bytes 4194304 | tf_op jit(solution)/shard_map/all_to_all | solution.py:254
  317.9 5.0 copy-start.2
  317.9 90.4 %all-to-all-start.4 = ((bf16[16,256,128]{2,1,0:T(8,128)(2,1)}), bf16[16,256,128]{2,1,0:T(8,128)(2,1)S(1)}, u32[]{:S(2)}, u32[]{:S(2)}) async-start(bf16[16,256,128]{2,1,0:T(8,128)(2,1)} %get-tuple-element.6), calls=%async_computation.4 | async-start | bytes 2097152 | tf_op jit(solution)/shard_map/all_to_all | solution.py:254
  408.4 1.0 copy-start
  409.4 121.0 %all-to-all-start.3 = ((bf16[16,1280,128]{2,1,0:T(8,128)(2,1)}), bf16[16,1280,128]{2,1,0:T(8,128)(2,1)}, u32[]{:S(2)}, u32[]{:S(2)}) async-start(bf16[16,1280,128]{2,1,0:T(8,128)(2,1)} %attend_head.3), calls=%async_computation.3 | async-start | bytes 10485760 | tf_op jit(solution)/shard_map/all_to_all | solution.py:254

commit v5 on v4

--- a/solution.py
+++ b/solution.py
@@ -12,6 +12,7 @@
 PAIR = 2 * HD
 LOG2E = 1.4426950408889634
 CHUNKS = 2
+DEPTH = 4
 VMEM_LIMIT = 60 * 1024 * 1024
 
 
@@ -260,27 +261,39 @@
     return low, high
 
 
-def pack_kernel(a_ref, b_ref, out_ref):
-    out_ref[0], out_ref[1] = merge_lanes(a_ref[...], b_ref[...])
-
-
-def pack_heads(a, b, start, count):
-    rows, width = a.shape
+def pack_kernel(tokens, a_ref, b_ref, *refs):
+    out_ref = refs[-1]
+    low, high = merge_lanes(a_ref[...], b_ref[...])
+    out_ref[0, :tokens, :] = low
+    out_ref[1, :tokens, :] = high
+    if len(refs) > 1:
+        out_ref[0, tokens:, :] = refs[0][...]
+        out_ref[1, tokens:, :] = refs[0][...]
+
+
+def pack_heads(a, b, start, count, extra=None):
+    _, width = a.shape
     tokens = count * TILE
     first = start // count
     spec = pl.BlockSpec((tokens, PAIR), lambda i: (first, i))
+    in_specs, operands = [spec, spec], [a, b]
+    length = tokens
+    if extra is not None:
+        length += extra.shape[0]
+        in_specs.append(pl.BlockSpec(extra.shape, lambda i: (0, 0)))
+        operands.append(extra)
     return pl.pallas_call(
-        pack_kernel,
+        functools.partial(pack_kernel, tokens),
         grid=(width // PAIR,),
-        in_specs=[spec, spec],
-        out_specs=pl.BlockSpec((2, tokens, PAIR), lambda i: (i, 0, 0)),
-        out_shape=jax.ShapeDtypeStruct((width // HD, tokens, PAIR), jnp.bfloat16),
+        in_specs=in_specs,
+        out_specs=pl.BlockSpec((2, length, PAIR), lambda i: (i, 0, 0)),
+        out_shape=jax.ShapeDtypeStruct((width // HD, length, PAIR), jnp.bfloat16),
         cost_estimate=pl.CostEstimate(
             flops=0, bytes_accessed=8 * tokens * width, transcendentals=0
         ),
         compiler_params=pltpu.CompilerParams(vmem_limit_bytes=VMEM_LIMIT),
         name="pack_heads",
-    )(a, b)
+    )(*operands)
 
 
 def turn_kernel(kv_ref, out_ref):
@@ -305,148 +318,182 @@
 def head_kernel(dims, *refs):
     blocks, picks, start, count, last = dims
     if last:
-        table_ref, qg_ref, kv_ref, kt_ref, before_ref, out_ref, acc_ref, before_scr, sem = refs[:9]
-        scratch = refs[9:]
+        table_ref, qg_ref, kv_ref, kt_ref, before_ref, out_ref, acc_ref, sem = refs[:8]
+        buffers = refs[8:]
     else:
         table_ref, qg_ref, kv_ref, kt_ref, out_ref, acc_ref = refs[:6]
-        scratch = refs[6:]
-    source = pl.program_id(0)
-    sources = pl.num_programs(0)
-    width = TILE * (picks + 1)
+        buffers = refs[6:]
+    raws, pairs = buffers[:DEPTH], buffers[DEPTH:]
+    sources = out_ref.shape[0]
     lane = lax.broadcasted_iota(jnp.int32, (TILE, PAIR), 1)
     low = lane < HD
-
-    @pl.when(source == 0)
-    def _():
-        acc_ref[...] = jnp.zeros_like(acc_ref)
-        if last:
-            pltpu.make_async_copy(before_ref, before_scr, sem).start()
+    parts = [slice(j * TILE, (j + 1) * TILE) for j in range(picks + 1)]
+    final = sources * count - 1
 
     def fold(x, op):
         return op(x.reshape(-1, 8, x.shape[-1]), axis=0)
 
-    def spans(block):
+    def load_block(index):
+        index = jnp.minimum(index, final)
+        source, local = index // count, index % count
+        block = source * blocks + start + local
         named = [table_ref[block * picks + j] for j in range(picks)] + [block]
-        return named, [pl.ds(pl.multiple_of(n * TILE, TILE), TILE) for n in named]
-
-    def one_block(local, raw_scr, pair_scr):
-        block = source * blocks + start + local
-        named, rows = spans(block)
-        qg = qg_ref[0, pl.ds(pl.multiple_of(local * TILE, TILE), TILE), :].astype(jnp.float32)
+        rows = [pl.ds(pl.multiple_of(n * TILE, TILE), TILE) for n in named]
+        local_rows = pl.ds(pl.multiple_of(local * TILE, TILE), TILE)
+        qg = qg_ref[source, local_rows, :].astype(jnp.float32)
         zero = jnp.zeros_like(qg)
         both = jnp.concatenate(
             [jnp.where(low, qg * (HD**-0.5), zero), jnp.where(low, zero, qg)], axis=0
         )
-        keys = jnp.concatenate([kv_ref[r, :] for r in rows], axis=0)
-        raw = dot_nt(keys, both.astype(jnp.bfloat16))
-        raw_scr[...] = raw
-        top = jnp.max(fold(raw[:, :TILE], jnp.max), axis=0, keepdims=True)
+        return named, rows, both
+
+    def stage_raw(state, slot):
+        _, rows, both = state
+        low_both = both.astype(jnp.bfloat16)
+        top = None
+        for j in range(picks + 1):
+            raw = dot_nt(kv_ref[rows[j], :], low_both)
+            raws[slot][parts[j]] = raw
+            part = fold(raw[:, :TILE], jnp.max)
+            top = part if top is None else jnp.maximum(top, part)
+            yield
+        yield jnp.max(top, axis=0, keepdims=True)
+
+    def stage_exp(top, slot):
+        raw_scr, pair_scr = raws[slot], pairs[slot]
         total = jnp.zeros((8, TILE), jnp.float32)
         inner = jnp.zeros((8, TILE), jnp.float32)
         for j in range(picks + 1):
-            part = slice(j * TILE, (j + 1) * TILE)
-            p = jnp.exp2((raw_scr[part, :TILE] - top) * LOG2E)
-            raw_scr[part, :TILE] = p
-            pair_scr[part, TILE:] = p.astype(jnp.bfloat16)
+            p = jnp.exp2((raw_scr[parts[j], :TILE] - top) * LOG2E)
+            raw_scr[parts[j], :TILE] = p
+            pair_scr[parts[j], TILE:] = p.astype(jnp.bfloat16)
             total += fold(p, jnp.sum)
-            inner += fold(p * raw_scr[part, TILE:], jnp.sum)
+            inner += fold(p * raw_scr[parts[j], TILE:], jnp.sum)
+            yield
         recip = 1.0 / jnp.sum(total, axis=0, keepdims=True)
         delta = jnp.sum(inner, axis=0, keepdims=True) * recip
-        for j in range(picks + 1):
-            part = slice(j * TILE, (j + 1) * TILE)
-            ds = raw_scr[part, :TILE] * (raw_scr[part, TILE:] - delta)
-            pair_scr[part, :TILE] = ds.astype(jnp.bfloat16)
+        yield recip, delta
+
+    def stage_grad(state, recip, delta, slot):
+        named, rows, both = state
+        raw_scr, pair_scr = raws[slot], pairs[slot]
         column = jnp.broadcast_to(recip, (TILE, TILE)).T
         scaled = jnp.concatenate([both[:TILE] * column, both[TILE:] * column], axis=0)
-        grads = dot_nn(pair_scr[...], scaled.astype(jnp.bfloat16))
+        scaled = scaled.astype(jnp.bfloat16)
         for j in range(picks + 1):
-            acc_ref[rows[j], :] += grads[j * TILE : (j + 1) * TILE, :]
+            ds = raw_scr[parts[j], :TILE] * (raw_scr[parts[j], TILE:] - delta)
+            pair_scr[parts[j], :TILE] = ds.astype(jnp.bfloat16)
+            acc_ref[rows[j], :] += dot_nn(pair_scr[parts[j]], scaled)
+            yield
         turned = jnp.concatenate([kt_ref[n] for n in named], axis=1)
         dqt = dot_nn(turned, pair_scr[:, :TILE])
-        return dqt * (recip * (HD**-0.5))
-
+        yield dqt * (recip * (HD**-0.5))
+
+    def together(*stages):
+        results = [None] * len(stages)
+        live = list(range(len(stages)))
+        while live:
+            for n in list(live):
+                try:
+                    value = next(stages[n])
+                    if value is not None:
+                        results[n] = value
+                except StopIteration:
+                    live.remove(n)
+        return results
+
+    if last:
+        fill = pltpu.make_async_copy(before_ref, acc_ref, sem)
+        fill.start()
+    else:
+
+        def clear(n, carry):
+            rows = pl.ds(pl.multiple_of(n * 8 * TILE, TILE), 8 * TILE)
+            acc_ref[rows, :] = jnp.zeros((8 * TILE, PAIR), jnp.float32)
+            return carry
+
+        lax.fori_loop(0, acc_ref.shape[0] // (8 * TILE), clear, 0)
+
+    (top0,) = together(stage_raw(load_block(0), 0))
+    top1, stats0 = together(stage_raw(load_block(1), 1), stage_exp(top0, 0))
+    if last:
+        fill.wait()
     offset = blocks * TILE if last else 0
 
-    def two_blocks(m, carry):
-        first = one_block(2 * m, scratch[0], scratch[1])
-        second = one_block(2 * m + 1, scratch[2], scratch[3])
-        both = jnp.concatenate([first, second], axis=0).T.astype(jnp.bfloat16)
-        if last:
-            out_ref[source, pl.ds(pl.multiple_of(offset + m * TILE, TILE), TILE), :] = both
-        else:
-            out_ref[0, pl.ds(pl.multiple_of(m * TILE, TILE), TILE), :] = both
-        return carry
-
-    lax.fori_loop(0, count // 2, two_blocks, 0)
+    def round_of_blocks(m, carry):
+        top, recip, delta = carry
+        base = m * DEPTH
+        held = None
+        for n in range(DEPTH):
+            index = base + n
+            top, (next_recip, next_delta), dqt = together(
+                stage_raw(load_block(index + 2), (n + 2) % DEPTH),
+                stage_exp(top, (n + 1) % DEPTH),
+                stage_grad(load_block(index), recip, delta, n),
+            )
+            recip, delta = next_recip, next_delta
+            if n % 2 == 0:
+                held = dqt
+            else:
+                both = jnp.concatenate([held, dqt], axis=0).T.astype(jnp.bfloat16)
+                source, local = index // count, index % count
+                rows = pl.ds(pl.multiple_of(offset + local // 2 * TILE, TILE), TILE)
+                out_ref[source, rows, :] = both
+        return top, recip, delta
+
+    lax.fori_loop(0, sources * count // DEPTH, round_of_blocks, (top1, *stats0))
 
     if last:
 
-        @pl.when(source == sources - 1)
-        def _():
-            pltpu.make_async_copy(before_ref, before_scr, sem).wait()
-
-            def finish(s, carry):
-                rows = pl.ds(pl.multiple_of(s * blocks * TILE, TILE), blocks * TILE)
-                out_ref[s, : blocks * TILE, :] = (acc_ref[rows, :] + before_scr[rows, :]).astype(
-                    jnp.bfloat16
-                )
-                return carry
-
-            lax.fori_loop(0, sources, finish, 0)
-
-
-def attend_head(table, qg, kv, turned, before, blocks, start):
-    peers, tokens, _ = qg.shape
+        def finish(s, carry):
+            rows = pl.ds(pl.multiple_of(s * blocks * TILE, TILE), blocks * TILE)
+            out_ref[s, : blocks * TILE, :] = acc_ref[rows, :].astype(jnp.bfloat16)
+            return carry
+
+        lax.fori_loop(0, sources, finish, 0)
+
+
+def attend_head(table, qg, kv, turned, before, blocks, start, count):
+    peers = qg.shape[0]
     total = kv.shape[0]
-    count = tokens // TILE
     picks = table.shape[0] // (total // TILE)
     last = before is not None
     keys = TILE * (picks + 1)
-    in_specs = [
-        pl.BlockSpec((1, tokens, PAIR), lambda i, t: (i, 0, 0)),
-        pl.BlockSpec((total, PAIR), lambda i, t: (0, 0)),
-        pl.BlockSpec(turned.shape, lambda i, t: (0, 0, 0)),
-    ]
+
+    def whole(shape):
+        return pl.BlockSpec(shape, lambda i, t: (0,) * len(shape))
+
+    in_specs = [whole((peers, count * TILE, PAIR)), whole(kv.shape), whole(turned.shape)]
     operands = [table, qg, kv, turned]
     acc_shape = (total, PAIR)
-    scratch = [
-        pltpu.VMEM((keys, 2 * TILE), jnp.float32),
-        pltpu.VMEM((keys, 2 * TILE), jnp.bfloat16),
-        pltpu.VMEM((keys, 2 * TILE), jnp.float32),
-        pltpu.VMEM((keys, 2 * TILE), jnp.bfloat16),
-    ]
+    buffers = [pltpu.VMEM((keys, 2 * TILE), jnp.float32)] * DEPTH
+    buffers += [pltpu.VMEM((keys, 2 * TILE), jnp.bfloat16)] * DEPTH
     if last:
         in_specs.append(pl.BlockSpec(memory_space=pl.ANY))
         operands.append(before)
         packed = (peers, (blocks + count // 2) * TILE, PAIR)
-        out_specs = pl.BlockSpec(packed, lambda i, t: (0, 0, 0))
+        out_specs = whole(packed)
         out_shape = jax.ShapeDtypeStruct(packed, jnp.bfloat16)
-        scratch = [
-            pltpu.VMEM(acc_shape, jnp.float32),
-            pltpu.VMEM(acc_shape, jnp.float32),
-            pltpu.SemaphoreType.DMA,
-        ] + scratch
+        buffers = [pltpu.VMEM(acc_shape, jnp.float32), pltpu.SemaphoreType.DMA] + buffers
     else:
-        out_specs = [
-            pl.BlockSpec((1, tokens // 2, PAIR), lambda i, t: (i, 0, 0)),
-            pl.BlockSpec(acc_shape, lambda i, t: (0, 0)),
-        ]
+        dq_shape = (peers, count // 2 * TILE, PAIR)
+        out_specs = [whole(dq_shape), whole(acc_shape)]
         out_shape = [
-            jax.ShapeDtypeStruct((peers, tokens // 2, PAIR), jnp.bfloat16),
+            jax.ShapeDtypeStruct(dq_shape, jnp.bfloat16),
             jax.ShapeDtypeStruct(acc_shape, jnp.float32),
         ]
     return pl.pallas_call(
         functools.partial(head_kernel, (blocks, picks, start, count, last)),
         grid_spec=pltpu.PrefetchScalarGridSpec(
             num_scalar_prefetch=1,
-            grid=(peers,),
+            grid=(1,),
             in_specs=in_specs,
             out_specs=out_specs,
-            scratch_shapes=scratch,
+            scratch_shapes=buffers,
         ),
         out_shape=out_shape,
         cost_estimate=pl.CostEstimate(
-            flops=5 * 2 * 2 * TILE * PAIR * keys * peers * count // 2,
+            flops=5 * 2 * TILE * PAIR * keys * peers * count,
             bytes_accessed=24 * 1024 * 1024,
             transcendentals=peers * count * keys * TILE,
         ),
@@ -503,16 +550,24 @@
 
 def by_heads(queries, key_rows, value_rows, grad_out, tile_keys):
     rows, _ = queries.shape
-    blocks = rows // TILE
+    blocks, picks = tile_keys.shape
     half = blocks // 2
-    table = lax.all_gather(tile_keys, "ctx", tiled=True).reshape(-1)
-    kv = exchange(pack_heads(key_rows, value_rows, 0, blocks))
-    qg = [exchange(pack_heads(queries, grad_out, c * half, half)) for c in range(2)]
+    tokens = half * TILE
+    extra = jnp.pad(tile_keys.astype(jnp.bfloat16), ((0, 16 - blocks), (0, PAIR - picks)))
+    kv = pack_heads(key_rows, value_rows, 0, blocks)
+    qg0 = pack_heads(queries, grad_out, 0, half, extra)
+    qg1 = pack_heads(queries, grad_out, half, half)
+    kv = exchange(kv)
+    kv, qg0 = lax.optimization_barrier((kv, qg0))
+    qg0 = exchange(qg0)
     kv = kv.reshape(-1, PAIR)
     turned = turn_keys(kv)
-    dq, before = attend_head(table, qg[0], kv, turned, None, blocks, 0)
+    qg0, qg1, turned = lax.optimization_barrier((qg0, qg1, turned))
+    qg1 = exchange(qg1)
+    table = qg0[:, tokens : tokens + blocks, :picks].astype(jnp.int32).reshape(-1)
+    dq, before = attend_head(table, qg0, kv, turned, None, blocks, 0, half)
     back = exchange(dq)
-    packed = attend_head(table, qg[1], kv, turned, before, blocks, half)
+    packed = attend_head(table, qg1, kv, turned, before, blocks, half, half)
     final = exchange(packed)
     grad_queries = unpack_heads(back, None, blocks, 0, half)[0]
     return unpack_heads(final, grad_queries, blocks, half, half)
@@ -549,8 +604,11 @@
 
 
 def on_device(queries, key_rows, value_rows, grad_out, tile_keys):
-    split_evenly = lax.axis_size("ctx") * HD == queries.shape[1]
-    plan = by_heads if split_evenly and queries.shape[0] % (4 * TILE) == 0 else by_blocks
+    peers = lax.axis_size("ctx")
+    blocks = tile_keys.shape[0]
+    one_head_each = peers * HD == queries.shape[1]
+    fits = one_head_each and blocks % 4 == 0 and blocks <= 16 and peers * blocks <= 256
+    plan = by_heads if fits else by_blocks
     return tuple(plan(queries, key_rows, value_rows, grad_out, tile_keys))
 
 

time: 539 us -> 403 us (0.75)
  Pallas kernels: 214 us -> 143 us
  blocking collectives: 57 us -> 0 us
  waiting for transfers between devices: 236 us -> 227 us
    pallas_call x2, Pallas kernels: 171 us -> 99.5 us  [attend_head(): pl.pallas_call(functools.partial(head_kernel, (blocks, picks, start, coun...]
    all_gather x1 -> x0, blocking collectives: 57 us -> none  [by_heads(): table = lax.all_gather(tile_keys, 'ctx', tiled=True).reshape(-1)]
    all_to_all x5, waiting for transfers between devices: 236 us -> 227 us  [exchange(): return lax.all_to_all(x, 'ctx', split_axis=0, concat_axis=0, tiled=True)]
  transfers between devices with their start and end apart: 5 -> 5, of which waited for: 3 -> 3; matrix products, arithmetic and copies ran while one was open for 0% -> 0% of each run, Pallas kernels for 37% -> 32%
where the time goes in v5:
time: 403 us; the launch traced here: 401 us
  waiting for transfers between devices  227 us (56%)
  Pallas kernels  143 us (35%)
  starting transfers between devices  28.5 us (7%)
    all_to_all x5, waiting for transfers between devices, exchange(): return lax.all_to_all(x, 'ctx', split_axis=0, concat_axis=0, tiled=True)  227 us
    pallas_call x2, Pallas kernels, attend_head(): pl.pallas_call(functools.partial(head_kernel, (blocks, picks, start, coun...  99.5 us
    all_to_all x5, starting transfers between devices, exchange(): return lax.all_to_all(x, 'ctx', split_axis=0, concat_axis=0, tiled=True)  28.5 us
    pallas_call x3, Pallas kernels, pack_heads(): pl.pallas_call(functools.partial(pack_kernel, tokens), grid=(width // PAI...  19.7 us
    pallas_call x2, Pallas kernels, unpack_heads(): pl.pallas_call(functools.partial(unpack_kernel, blocks, start, count, las...  12.9 us
    pallas_call x1, Pallas kernels, turn_keys(): pl.pallas_call(turn_kernel, grid=(total // step,), in_specs=[pl.BlockSpec...  10.4 us
  transfers between devices with their start and end apart: 5, of which 3 were waited for; matrix products, arithmetic and copies ran while one was open for 0% of the time, Pallas kernels for 32%

profile of v5, /device:TPU:13, one launch (start us, length us, event | category | flops | bytes accessed | tf_op | source)
XLA Modules:
  0.0 401.3 jit_solution(8210971311009019079)
XLA Ops:
  0.6 7.2 %pack_heads.3 = bf16[16,1024,128]{2,1,0:T(8,128)(2,1)} custom-call(bf16[1024,1024]{1,0:T(8,128)(2,1)} %a_ref.3, bf16[1024,1024]{1,0:T(8,128)(2,1)} %b_ref.3), custom_call_target="tpu_custom_call" | custom-call | bytes 8388608 | tf_op jit(solution)/shard_map/pack_heads/pallas_call | solution.py:285
  7.9 0.0 copy-start.2
  7.9 6.7 %all-to-all-start = ((bf16[16,1024,128]{2,1,0:T(8,128)(2,1)}), bf16[16,1024,128]{2,1,0:T(8,128)(2,1)}, u32[]{:S(2)}, u32[]{:S(2)}) async-start(bf16[16,1024,128]{2,1,0:T(8,128)(2,1)} %pack_heads.3), calls=%async_computation | async-start | bytes 8388608 | tf_op jit(solution)/shard_map/all_to_all | solution.py:255
  14.6 0.0 copy-done.2
  14.6 0.6 pad.4.refs_0_
  15.2 6.3 %pack_heads.4 = bf16[16,528,128]{2,1,0:T(8,128)(2,1)} custom-call(bf16[1024,1024]{1,0:T(8,128)(2,1)} %a_ref.5, bf16[1024,1024]{1,0:T(8,128)(2,1)} %b_ref.5, bf16[16,128]{1,0:T(8,128)(2,1)} %pad.4.refs_0_), custom_call_target="tpu_custom_call" | custom-call | bytes 4194304 | tf_op jit(solution)/shard_map/pack_heads/pallas_call | solution.py:285
  21.4 85.6 %all-to-all-done = bf16[16,1024,128]{2,1,0:T(8,128)(2,1)} async-done(((bf16[16,1024,128]{2,1,0:T(8,128)(2,1)}), bf16[16,1024,128]{2,1,0:T(8,128)(2,1)}, u32[]{:S(2)}, u32[]{:S(2)}) %all-to-all-start) | async-done | bytes 4194336 | tf_op jit(solution)/shard_map/all_to_all | solution.py:255
  107.0 4.9 %all-to-all-start.1 = ((bf16[16,528,128]{2,1,0:T(8,128)(2,1)}), bf16[16,528,128]{2,1,0:T(8,128)(2,1)S(1)}, u32[]{:S(2)}, u32[]{:S(2)}) async-start(bf16[16,528,128]{2,1,0:T(8,128)(2,1)} %pack_heads.4), calls=%async_computation.1 | async-start | bytes 4325376 | tf_op jit(solution)/shard_map/all_to_all | solution.py:255
  111.9 6.2 %pack_heads.5 = bf16[16,512,128]{2,1,0:T(8,128)(2,1)} custom-call(bf16[1024,1024]{1,0:T(8,128)(2,1)} %a_ref.5, bf16[1024,1024]{1,0:T(8,128)(2,1)} %b_ref.5), custom_call_target="tpu_custom_call" | custom-call | bytes 4194304 | tf_op jit(solution)/shard_map/pack_heads/pallas_call | solution.py:285
  118.1 10.4 %turn_keys.1.refs_3_ = bf16[128,64,128]{2,1,0:T(8,128)(2,1)} custom-call(bf16[16384,128]{1,0:T(8,128)(2,1)} %bitcast.kv_ref.refs_2_), custom_call_target="tpu_custom_call" | custom-call | tf_op jit(solution)/shard_map/turn_keys/pallas_call | solution.py:307
  128.5 32.2 %all-to-all-done.1.refs_1_ = bf16[16,528,128]{2,1,0:T(8,128)(2,1)S(1)} async-done(((bf16[16,528,128]{2,1,0:T(8,128)(2,1)}), bf16[16,528,128]{2,1,0:T(8,128)(2,1)S(1)}, u32[]{:S(2)}, u32[]{:S(2)}) %all-to-all-start.1) | async-done | bytes 2162720 | tf_op jit(solution)/shard_map/all_to_all | solution.py:255
  160.8 0.0 copy-start.1
  160.8 4.9 %all-to-all-start.2 = ((bf16[16,512,128]{2,1,0:T(8,128)(2,1)}), bf16[16,512,128]{2,1,0:T(8,128)(2,1)}, u32[]{:S(2)}, u32[]{:S(2)}) async-start(bf16[16,512,128]{2,1,0:T(8,128)(2,1)} %pack_heads.5), calls=%async_computation.2 | async-start | bytes 4194304 | tf_op jit(solution)/shard_map/all_to_all | solution.py:255
  165.7 0.0 copy-done.1
  165.7 0.7 reshape.18.refs_0_
  166.4 48.9 %attend_head.2 = (bf16[16,256,128]{2,1,0:T(8,128)(2,1)}, f32[16384,128]{1,0:T(8,128)}) custom-call(s32[1024]{0:T(1024)} %reshape.18.refs_0_, bf16[16,528,128]{2,1,0:T(8,128)(2,1)} %copy-done.1, bf16[16384,128]{1,0:T(8,128)(2,1)} %bitcast.kv_ref.refs_2_, bf16[128,64,128]{2,1,0:T(8,128)(2,1)} %turn_keys.1.refs_3_), custom_call_target="tpu_custom_call" | custom-call | flops 12079595520 | bytes 25165824 | tf_op jit(solution)/shard_map/attend_head/pallas_call | solution.py:485
  215.3 0.0 all-to-all-done.2.refs_1_
  215.3 6.0 %all-to-all-start.4 = ((bf16[16,256,128]{2,1,0:T(8,128)(2,1)}), bf16[16,256,128]{2,1,0:T(8,128)(2,1)S(1)}, u32[]{:S(2)}, u32[]{:S(2)}) async-start(bf16[16,256,128]{2,1,0:T(8,128)(2,1)} %get-tuple-element.16), calls=%async_computation.4 | async-start | bytes 2097152 | tf_op jit(solution)/shard_map/all_to_all | solution.py:255
  221.3 50.6 %attend_head.3 = bf16[16,1280,128]{2,1,0:T(8,128)(2,1)} custom-call(s32[1024]{0:T(1024)} %reshape.18.refs_0_, bf16[16,512,128]{2,1,0:T(8,128)(2,1)} %all-to-all-done.2.refs_1_, bf16[16384,128]{1,0:T(8,128)(2,1)} %bitcast.kv_ref.refs_2_, bf16[128,64,128]{2,1,0:T(8,128)(2,1)} %turn_keys.1.refs_3_, f32[16384,128]{1,0:T(8,128)} %get-tuple-element.15.refs_4_), custom_call_target="tpu_custom_call" | custom-call | flops 12079595520 | bytes 25165824 | tf_op jit(solution)/shard_map/attend_head/pallas_call | solution.py:485
  271.9 0.0 all-to-all-done.4.in_ref
  272.0 0.0 copy-start
  272.0 1.0 copy-done
  272.9 6.0 %all-to-all-start.3 = ((bf16[16,1280,128]{2,1,0:T(8,128)(2,1)}), bf16[16,1280,128]{2,1,0:T(8,128)(2,1)}, u32[]{:S(2)}, u32[]{:S(2)}) async-start(bf16[16,1280,128]{2,1,0:T(8,128)(2,1)} %attend_head.3), calls=%async_computation.3 | async-start | bytes 10485760 | tf_op jit(solution)/shard_map/all_to_all | solution.py:255
  278.9 5.5 %unpack_heads.2.refs_0_ = bf16[1024,1024]{1,0:T(8,128)(2,1)} custom-call(bf16[16,256,128]{2,1,0:T(8,128)(2,1)} %copy-done), custom_call_target="tpu_custom_call" | custom-call | bytes 2097152 | tf_op jit(solution)/shard_map/unpack_heads/pallas_call | solution.py:536
  284.5 109.4 %all-to-all-done.3.in_ref = bf16[16,1280,128]{2,1,0:T(8,128)(2,1)} async-done(((bf16[16,1280,128]{2,1,0:T(8,128)(2,1)}), bf16[16,1280,128]{2,1,0:T(8,128)(2,1)}, u32[]{:S(2)}, u32[]{:S(2)}) %all-to-all-start.3) | async-done | bytes 5242912 | tf_op jit(solution)/shard_map/all_to_all | solution.py:255
  393.9 7.4 %unpack_heads.3 = (bf16[1024,1024]{1,0:T(8,128)(2,1)}, bf16[1024,1024]{1,0:T(8,128)(2,1)}, bf16[1024,1024]{1,0:T(8,128)(2,1)}) custom-call(bf16[16,1280,128]{2,1,0:T(8,128)(2,1)} %all-to-all-done.3.in_ref, bf16[1024,1024]{1,0:T(8,128)(2,1)} %unpack_heads.2.refs_0_), custom_call_target="tpu_custom_call", output_to_operand_aliasing={{0}: (1, {})} | custom-call | bytes 10485760 | tf_op jit(solution)/shard_map/unpack_heads/pallas_call | solution.py:536
  (2 shorter events, 0.0 us)
Async XLA Ops:
  7.9 6.7 %copy-start.2 = (s32[8,8]{1,0:T(8,128)S(1)}, s32[8,8]{1,0:T(8,128)}, u32[]{:S(2)}) copy-start(s32[8,8]{1,0:T(8,128)} %param.9) | copy-start | bytes 772
  7.9 99.2 %all-to-all-start = ((bf16[16,1024,128]{2,1,0:T(8,128)(2,1)}), bf16[16,1024,128]{2,1,0:T(8,128)(2,1)}, u32[]{:S(2)}, u32[]{:S(2)}) async-start(bf16[16,1024,128]{2,1,0:T(8,128)(2,1)} %pack_heads.3), calls=%async_computation | async-start | bytes 8388608 | tf_op jit(solution)/shard_map/all_to_all | solution.py:255
  107.0 53.7 %all-to-all-start.1 = ((bf16[16,528,128]{2,1,0:T(8,128)(2,1)}), bf16[16,528,128]{2,1,0:T(8,128)(2,1)S(1)}, u32[]{:S(2)}, u32[]{:S(2)}) async-start(bf16[16,528,128]{2,1,0:T(8,128)(2,1)} %pack_heads.4), calls=%async_computation.1 | async-start | bytes 4325376 | tf_op jit(solution)/shard_map/all_to_all | solution.py:255
  160.8 4.9 %copy-start.1 = (bf16[16,528,128]{2,1,0:T(8,128)(2,1)}, bf16[16,528,128]{2,1,0:T(8,128)(2,1)S(1)}, u32[]{:S(2)}) copy-start(bf16[16,528,128]{2,1,0:T(8,128)(2,1)S(1)} %all-to-all-done.1.refs_1_) | copy-start | bytes 6488068
  160.8 54.5 %all-to-all-start.2 = ((bf16[16,512,128]{2,1,0:T(8,128)(2,1)}), bf16[16,512,128]{2,1,0:T(8,128)(2,1)}, u32[]{:S(2)}, u32[]{:S(2)}) async-start(bf16[16,512,128]{2,1,0:T(8,128)(2,1)} %pack_heads.5), calls=%async_computation.2 | async-start | bytes 4194304 | tf_op jit(solution)/shard_map/all_to_all | solution.py:255
  215.3 56.7 %all-to-all-start.4 = ((bf16[16,256,128]{2,1,0:T(8,128)(2,1)}), bf16[16,256,128]{2,1,0:T(8,128)(2,1)S(1)}, u32[]{:S(2)}, u32[]{:S(2)}) async-start(bf16[16,256,128]{2,1,0:T(8,128)(2,1)} %get-tuple-element.16), calls=%async_computation.4 | async-start | bytes 2097152 | tf_op jit(solution)/shard_map/all_to_all | solution.py:255
  272.0 1.0 copy-start
  272.9 121.0 %all-to-all-start.3 = ((bf16[16,1280,128]{2,1,0:T(8,128)(2,1)}), bf16[16,1280,128]{2,1,0:T(8,128)(2,1)}, u32[]{:S(2)}, u32[]{:S(2)}) async-start(bf16[16,1280,128]{2,1,0:T(8,128)(2,1)} %attend_head.3), calls=%async_computation.3 | async-start | bytes 10485760 | tf_op jit(solution)/shard_map/all_to_all | solution.py:255

commit v6 on v3

--- a/solution.py
+++ b/solution.py
@@ -12,6 +12,8 @@
 PAIR = 2 * HD
 LOG2E = 1.4426950408889634
 CHUNKS = 2
+DEPTH = 4
+PHASES = 2
 VMEM_LIMIT = 60 * 1024 * 1024
 
 
@@ -254,7 +256,335 @@
     return lax.all_to_all(x, "ctx", split_axis=0, concat_axis=0, tiled=True)
 
 
-def on_device(queries, key_rows, value_rows, grad_out, tile_keys):
+def merge_lanes(a, b):
+    low = jnp.concatenate([a[:, :HD], b[:, :HD]], axis=1)
+    high = jnp.concatenate([a[:, HD:], b[:, HD:]], axis=1)
+    return low, high
+
+
+def pack_kernel(tokens, k_ref, v_ref, q_ref, g_ref, *refs):
+    out_ref = refs[-1]
+    kv = merge_lanes(k_ref[...], v_ref[...])
+    qg = merge_lanes(q_ref[...], g_ref[...])
+    for head in range(2):
+        for core in range(2):
+            part = slice(core * tokens, (core + 1) * tokens)
+            out_ref[2 * head + core, :tokens, :] = kv[head][part]
+            out_ref[2 * head + core, tokens : 2 * tokens, :] = qg[head][part]
+            if len(refs) > 1:
+                out_ref[2 * head + core, 2 * tokens :, :] = refs[0][core]
+
+
+def pack_phase(key_rows, value_rows, queries, grad_out, phase, extra=None):
+    rows, width = queries.shape
+    slabs = width // PAIR // PHASES
+    spec = pl.BlockSpec((rows, PAIR), lambda j: (0, phase * slabs + j))
+    in_specs, operands = [spec] * 4, [key_rows, value_rows, queries, grad_out]
+    length = rows
+    if extra is not None:
+        length += extra.shape[1]
+        in_specs.append(pl.BlockSpec(extra.shape, lambda j: (0, 0, 0)))
+        operands.append(extra)
+    return pl.pallas_call(
+        functools.partial(pack_kernel, rows // 2),
+        grid=(slabs,),
+        in_specs=in_specs,
+        out_specs=pl.BlockSpec((4, length, PAIR), lambda j: (j, 0, 0)),
+        out_shape=jax.ShapeDtypeStruct((4 * slabs, length, PAIR), jnp.bfloat16),
+        cost_estimate=pl.CostEstimate(
+            flops=0, bytes_accessed=8 * rows * width, transcendentals=0
+        ),
+        compiler_params=pltpu.CompilerParams(vmem_limit_bytes=VMEM_LIMIT),
+        name="pack_phase",
+    )(*operands)
+
+
+def head_kernel(picks, table_ref, qg_ref, mine_ref, other_ref, out_ref, sum_ref, give_ref, *scratch):
+    kv_scr, kt_scr, acc_ref, sems = scratch[:4]
+    raws, pairs = scratch[4 : 4 + DEPTH], scratch[4 + DEPTH :]
+    sources, tokens, _ = qg_ref.shape
+    half = tokens // TILE
+    lane = lax.broadcasted_iota(jnp.int32, (TILE, PAIR), 1)
+    low = lane < HD
+    parts = [slice(j * TILE, (j + 1) * TILE) for j in range(picks + 1)]
+    final = sources * half - 1
+
+    loads = [
+        pltpu.make_async_copy(
+            mine_ref.at[:, pl.ds(0, tokens)], kv_scr.at[pl.ds(0, sources)], sems.at[0]
+        ),
+        pltpu.make_async_copy(other_ref, kv_scr.at[pl.ds(sources, sources)], sems.at[1]),
+    ]
+    for load in loads:
+        load.start()
+
+    def clear(n, carry):
+        rows = pl.ds(pl.multiple_of(n * tokens, tokens), tokens)
+        acc_ref[rows, :] = jnp.zeros((tokens, PAIR), jnp.float32)
+        return carry
+
+    lax.fori_loop(0, 2 * sources, clear, 0)
+    for load in loads:
+        load.wait()
+
+    def turn(n, carry):
+        for j in range(half):
+            kt_scr[n * half + j] = kv_scr[n, j * TILE : (j + 1) * TILE, :].T[:HD, :]
+        return carry
+
+    lax.fori_loop(0, 2 * sources, turn, 0)
+
+    def tile_rows(n):
+        return pl.ds(pl.multiple_of(n * TILE, TILE), TILE)
+
+    def fold(x, op):
+        return op(x.reshape(-1, 8, x.shape[-1]), axis=0)
+
+    def load_block(index):
+        block = jnp.minimum(index, final)
+        named = [table_ref[block * picks + j] for j in range(picks)] + [block]
+        rows = [tile_rows(n) for n in named]
+        qg = qg_ref[block // half, tile_rows(block % half), :].astype(jnp.float32)
+        zero = jnp.zeros_like(qg)
+        both = jnp.concatenate(
+            [jnp.where(low, qg * (HD**-0.5), zero), jnp.where(low, zero, qg)], axis=0
+        )
+        return named, rows, both
+
+    def stage_raw(state, slot):
+        named, _, both = state
+        low_both = both.astype(jnp.bfloat16)
+        top = None
+        for j in range(picks + 1):
+            n = named[j]
+            raw = dot_nt(kv_scr[n // half, tile_rows(n % half), :], low_both)
+            raws[slot][parts[j]] = raw
+            part = fold(raw[:, :TILE], jnp.max)
+            top = part if top is None else jnp.maximum(top, part)
+            yield
+        yield jnp.max(top, axis=0, keepdims=True)
+
+    def stage_exp(top, slot):
+        raw_scr, pair_scr = raws[slot], pairs[slot]
+        total = jnp.zeros((8, TILE), jnp.float32)
+        inner = jnp.zeros((8, TILE), jnp.float32)
+        for j in range(picks + 1):
+            p = jnp.exp2((raw_scr[parts[j], :TILE] - top) * LOG2E)
+            raw_scr[parts[j], :TILE] = p
+            pair_scr[parts[j], TILE:] = p.astype(jnp.bfloat16)
+            total += fold(p, jnp.sum)
+            inner += fold(p * raw_scr[parts[j], TILE:], jnp.sum)
+            yield
+        recip = 1.0 / jnp.sum(total, axis=0, keepdims=True)
+        delta = jnp.sum(inner, axis=0, keepdims=True) * recip
+        yield recip, delta
+
+    def stage_grad(state, recip, delta, slot):
+        named, rows, both = state
+        raw_scr, pair_scr = raws[slot], pairs[slot]
+        column = jnp.broadcast_to(recip, (TILE, TILE)).T
+        scaled = jnp.concatenate([both[:TILE] * column, both[TILE:] * column], axis=0)
+        scaled = scaled.astype(jnp.bfloat16)
+        for j in range(picks + 1):
+            ds = raw_scr[parts[j], :TILE] * (raw_scr[parts[j], TILE:] - delta)
+            pair_scr[parts[j], :TILE] = ds.astype(jnp.bfloat16)
+            acc_ref[rows[j], :] += dot_nn(pair_scr[parts[j]], scaled)
+            yield
+        turned = jnp.concatenate([kt_scr[n] for n in named], axis=1)
+        dqt = dot_nn(turned, pair_scr[:, :TILE])
+        yield dqt * (recip * (HD**-0.5))
+
+    def together(*stages):
+        results = [None] * len(stages)
+        live = list(range(len(stages)))
+        while live:
+            for n in list(live):
+                try:
+                    value = next(stages[n])
+                    if value is not None:
+                        results[n] = value
+                except StopIteration:
+                    live.remove(n)
+        return results
+
+    (top0,) = together(stage_raw(load_block(0), 0))
+    top1, stats0 = together(stage_raw(load_block(1), 1), stage_exp(top0, 0))
+
+    def round_of_blocks(m, carry):
+        top, recip, delta = carry
+        held = None
+        for n in range(DEPTH):
+            index = m * DEPTH + n
+            top, (next_recip, next_delta), dqt = together(
+                stage_raw(load_block(index + 2), (n + 2) % DEPTH),
+                stage_exp(top, (n + 1) % DEPTH),
+                stage_grad(load_block(index), recip, delta, n),
+            )
+            recip, delta = next_recip, next_delta
+            if n % 2 == 0:
+                held = dqt
+            else:
+                both = jnp.concatenate([held, dqt], axis=0).T.astype(jnp.bfloat16)
+                out_ref[index // half, tile_rows(index % half // 2), :] = both
+        return top, recip, delta
+
+    lax.fori_loop(0, sources * half // DEPTH, round_of_blocks, (top1, *stats0))
+
+    store = pltpu.make_async_copy(acc_ref.at[pl.ds(0, sources * tokens)], sum_ref, sems.at[2])
+    store.start()
+
+    def finish(s, carry):
+        rows = pl.ds(pl.multiple_of((sources + s) * tokens, tokens), tokens)
+        give_ref[s] = acc_ref[rows, :].astype(jnp.bfloat16)
+        return carry
+
+    lax.fori_loop(0, sources, finish, 0)
+    store.wait()
+
+
+def attend_head(table, received, other):
+    peers, tokens, _ = other.shape
+    half = tokens // TILE
+    total = 2 * peers * tokens
+    picks = table.shape[0] // (peers * half)
+    keys = TILE * (picks + 1)
+    any_spec = pl.BlockSpec(memory_space=pl.ANY)
+    scratch = [
+        pltpu.VMEM((2 * peers, tokens, PAIR), jnp.bfloat16),
+        pltpu.VMEM((2 * peers * half, HD, TILE), jnp.bfloat16),
+        pltpu.VMEM((total, PAIR), jnp.float32),
+        pltpu.SemaphoreType.DMA((3,)),
+    ]
+    scratch += [pltpu.VMEM((keys, 2 * TILE), jnp.float32)] * DEPTH
+    scratch += [pltpu.VMEM((keys, 2 * TILE), jnp.bfloat16)] * DEPTH
+    return pl.pallas_call(
+        functools.partial(head_kernel, picks),
+        grid_spec=pltpu.PrefetchScalarGridSpec(
+            num_scalar_prefetch=1,
+            grid=(1,),
+            in_specs=[
+                pl.BlockSpec((peers, tokens, PAIR), lambda i, t: (0, 1, 0)),
+                any_spec,
+                any_spec,
+            ],
+            out_specs=[
+                pl.BlockSpec((peers, tokens // 2, PAIR), lambda i, t: (0, 2, 0)),
+                any_spec,
+                pl.BlockSpec((peers, tokens, PAIR), lambda i, t: (0, 0, 0)),
+            ],
+            scratch_shapes=scratch,
+        ),
+        out_shape=[
+            jax.ShapeDtypeStruct((peers, 3 * tokens // 2, PAIR), jnp.bfloat16),
+            jax.ShapeDtypeStruct((peers * tokens, PAIR), jnp.float32),
+            jax.ShapeDtypeStruct((peers, tokens, PAIR), jnp.bfloat16),
+        ],
+        cost_estimate=pl.CostEstimate(
+            flops=5 * 2 * TILE * PAIR * keys * peers * half,
+            bytes_accessed=24 * 1024 * 1024,
+            transcendentals=peers * half * keys * TILE,
+        ),
+        compiler_params=pltpu.CompilerParams(vmem_limit_bytes=VMEM_LIMIT),
+        name="attend_head",
+    )(table, received, received, other)
+
+
+def merge_kernel(sum_ref, given_ref, before_ref, out_ref):
+    out_ref[...] = (sum_ref[...] + given_ref[...].astype(jnp.float32)).astype(jnp.bfloat16)
+
+
+def merge_sums(sums, given, payload):
+    peers, tokens, _ = given.shape
+    step = 4
+    spec = pl.BlockSpec((step, tokens, PAIR), lambda i: (i, 0, 0))
+    return pl.pallas_call(
+        merge_kernel,
+        grid=(peers // step,),
+        in_specs=[spec, spec, pl.BlockSpec(memory_space=pl.ANY)],
+        out_specs=spec,
+        out_shape=jax.ShapeDtypeStruct(payload.shape, jnp.bfloat16),
+        input_output_aliases={2: 0},
+        cost_estimate=pl.CostEstimate(
+            flops=0, bytes_accessed=8 * peers * tokens * PAIR, transcendentals=0
+        ),
+        compiler_params=pltpu.CompilerParams(vmem_limit_bytes=VMEM_LIMIT),
+        name="merge_sums",
+    )(sums.reshape(given.shape), given, payload)
+
+
+def unpack_kernel(tokens, in_ref, *refs):
+    gq_ref, gk_ref, gv_ref = refs[-3:]
+    for core in range(2):
+        part = slice(core * tokens, (core + 1) * tokens)
+        gk_ref[part, :], gv_ref[part, :] = merge_lanes(
+            in_ref[core, :tokens, :], in_ref[2 + core, :tokens, :]
+        )
+        for m in range(tokens // TILE // 2):
+            rows = slice(tokens + m * TILE, tokens + (m + 1) * TILE)
+            even, odd = merge_lanes(in_ref[core, rows, :], in_ref[2 + core, rows, :])
+            base = core * tokens + 2 * m * TILE
+            gq_ref[base : base + TILE, :] = even
+            gq_ref[base + TILE : base + 2 * TILE, :] = odd
+
+
+def unpack_phase(back, previous, phase, rows, width):
+    slabs = width // PAIR // PHASES
+    in_specs = [pl.BlockSpec((4, back.shape[1], PAIR), lambda j: (j, 0, 0))]
+    operands = [back]
+    aliases = {}
+    if previous is not None:
+        in_specs += [pl.BlockSpec(memory_space=pl.ANY)] * 3
+        operands += list(previous)
+        aliases = {1: 0, 2: 1, 3: 2}
+    return pl.pallas_call(
+        functools.partial(unpack_kernel, rows // 2),
+        grid=(slabs,),
+        in_specs=in_specs,
+        out_specs=[pl.BlockSpec((rows, PAIR), lambda j: (0, phase * slabs + j))] * 3,
+        out_shape=[jax.ShapeDtypeStruct((rows, width), jnp.bfloat16)] * 3,
+        input_output_aliases=aliases,
+        cost_estimate=pl.CostEstimate(
+            flops=0, bytes_accessed=6 * rows * width, transcendentals=0
+        ),
+        compiler_params=pltpu.CompilerParams(vmem_limit_bytes=VMEM_LIMIT),
+        name="unpack_phase",
+    )(*operands)
+
+
+def by_heads(queries, key_rows, value_rows, grad_out, tile_keys):
+    rows, width = queries.shape
+    blocks, picks = tile_keys.shape
+    peers = lax.axis_size("ctx")
+    half = blocks // 2
+    tokens = half * TILE
+    core = lax.axis_index("ctx") % 2
+
+    def swap(x):
+        return lax.ppermute(x, "ctx", [(i, i ^ 1) for i in range(peers)])
+
+    extra = tile_keys.astype(jnp.bfloat16).reshape(2, half, picks)
+    extra = jnp.pad(extra, ((0, 0), (0, 16 - half), (0, PAIR - picks)))
+    received = [
+        exchange(
+            pack_phase(key_rows, value_rows, queries, grad_out, p, extra if p == 0 else None)
+        )
+        for p in range(PHASES)
+    ]
+    table = received[0][:, 2 * tokens : 2 * tokens + half, :picks].astype(jnp.int32)
+    local = table % blocks
+    side = (local // half + core) % 2
+    table = (side * (peers * half) + table // blocks * half + local % half).reshape(-1)
+    backs = []
+    for p in range(PHASES):
+        payload, sums, give = attend_head(table, received[p], swap(received[p][:, :tokens]))
+        backs.append(exchange(merge_sums(sums, swap(give), payload)))
+    result = None
+    for p in range(PHASES):
+        result = unpack_phase(backs[p], result, p, rows, width)
+    return result
+
+
+def by_blocks(queries, key_rows, value_rows, grad_out, tile_keys):
     rows, width = queries.shape
     blocks = rows // TILE
     peers = lax.axis_size("ctx")
@@ -284,6 +614,16 @@
     return grad_queries, result[0], result[1]
 
 
+def on_device(queries, key_rows, value_rows, grad_out, tile_keys):
+    peers = lax.axis_size("ctx")
+    blocks = tile_keys.shape[0]
+    one_head_each = peers * HD == queries.shape[1]
+    even = peers % 4 == 0 and blocks % 4 == 0 and blocks <= 32
+    fits = one_head_each and even and peers * blocks <= 256
+    plan = by_heads if fits else by_blocks
+    return tuple(plan(queries, key_rows, value_rows, grad_out, tile_keys))
+
+
 def solution(mesh):
     spec = P(("groups", "ctx"), None)
     return jax.shard_map(

time: 416 us -> 362 us (0.87)
  waiting for transfers between devices: 238 us -> 196 us
  blocking collectives: 10.1 us -> 0 us
  Pallas kernels: 142 us -> 132 us
  local copies, waits for them, and re-layouts: 0.68 us -> 7.77 us
    all_to_all x4, waiting for transfers between devices: 238 us -> 181 us  [exchange(): return lax.all_to_all(x, 'ctx', split_axis=0, concat_axis=0, tiled=True)]
    ppermute x0 -> x4, waiting for transfers between devices: none -> 14.4 us  [swap(): return lax.ppermute(x, 'ctx', [(i, i ^ 1) for i in range(peers)])]
    all_to_all x1 -> x0, blocking collectives: 10.1 us -> none  [exchange(): return lax.all_to_all(x, 'ctx', split_axis=0, concat_axis=0, tiled=True)]
    pallas_call x6 -> x8, Pallas kernels: 142 us -> 132 us  [the longest x2 103 us: attend_head(): pl.pallas_call(functools.partial(head_kernel, picks), grid_spec=pltpu.Pre...]
  transfers between devices with their start and end apart: 4 -> 8, of which waited for: 4 -> 8; matrix products, arithmetic and copies ran while one was open for 0% -> 1% of each run, Pallas kernels for 32% -> 34%
where the time goes in v6:
time: 362 us; the launch traced here: 361 us
  waiting for transfers between devices  196 us (54%)
  Pallas kernels  132 us (36%)
  starting transfers between devices  23 us (6%)
  local copies, waits for them, and re-layouts  7.77 us (2%)
    all_to_all x4, waiting for transfers between devices, exchange(): return lax.all_to_all(x, 'ctx', split_axis=0, concat_axis=0, tiled=True)  181 us
    pallas_call x2, Pallas kernels, attend_head(): pl.pallas_call(functools.partial(head_kernel, picks), grid_spec=pltpu.Pre...  103 us
    all_to_all x4, starting transfers between devices, exchange(): return lax.all_to_all(x, 'ctx', split_axis=0, concat_axis=0, tiled=True)  21.3 us
    ppermute x4, waiting for transfers between devices, swap(): return lax.ppermute(x, 'ctx', [(i, i ^ 1) for i in range(peers)])  14.4 us
    pallas_call x2, Pallas kernels, pack_phase(): pl.pallas_call(functools.partial(pack_kernel, rows // 2), grid=(slabs,),...  10.7 us
    pallas_call x2, Pallas kernels, merge_sums(): pl.pallas_call(merge_kernel, grid=(peers // step,), in_specs=[spec, spec,...  9.31 us
    pallas_call x2, Pallas kernels, unpack_phase(): pl.pallas_call(functools.partial(unpack_kernel, rows // 2), grid=(slabs,)...  8.97 us
  transfers between devices with their start and end apart: 8, of which 8 were waited for; matrix products, arithmetic and copies ran while one was open for 1% of the time, Pallas kernels for 34%

profile of v6, /device:TPU:13, one launch (start us, length us, event | category | flops | bytes accessed | tf_op | source)
XLA Modules:
  0.0 361.0 jit_solution(3633077660512959463)
XLA Ops:
  0.6 0.7 convert_element_type.8
  1.3 0.6 pad.4.refs_0_
  1.9 5.4 %pack_phase.2 = bf16[16,1040,128]{2,1,0:T(8,128)(2,1)} custom-call(bf16[1024,1024]{1,0:T(8,128)(2,1)} %k_ref.3, bf16[1024,1024]{1,0:T(8,128)(2,1)} %v_ref.3, bf16[1024,1024]{1,0:T(8,128)(2,1)} %q_ref.3, bf16[1024,1024]{1,0:T(8,128)(2,1)} %g_ref.3, bf16[2,16,128]{2,1,0:T(8,128)(2,1)} %pad.4.refs_0_), custom_call_target="tpu_custom_call" | custom-call | bytes 8388608 | tf_op jit(solution)/shard_map/pack_phase/pallas_call | solution.py:288
  7.3 6.6 %all-to-all-start = ((bf16[16,1040,128]{2,1,0:T(8,128)(2,1)}), bf16[16,1040,128]{2,1,0:T(8,128)(2,1)}, u32[]{:S(2)}, u32[]{:S(2)}) async-start(bf16[16,1040,128]{2,1,0:T(8,128)(2,1)} %pack_phase.2), calls=%async_computation | async-start | bytes 8519680 | tf_op jit(solution)/shard_map/all_to_all | solution.py:256
  13.9 5.3 %pack_phase.3 = bf16[16,1024,128]{2,1,0:T(8,128)(2,1)} custom-call(bf16[1024,1024]{1,0:T(8,128)(2,1)} %k_ref.3, bf16[1024,1024]{1,0:T(8,128)(2,1)} %v_ref.3, bf16[1024,1024]{1,0:T(8,128)(2,1)} %q_ref.3, bf16[1024,1024]{1,0:T(8,128)(2,1)} %g_ref.3), custom_call_target="tpu_custom_call" | custom-call | bytes 8388608 | tf_op jit(solution)/shard_map/pack_phase/pallas_call | solution.py:288
  19.2 88.6 %all-to-all-done.qg_ref.mine_ref = bf16[16,1040,128]{2,1,0:T(8,128)(2,1)} async-done(((bf16[16,1040,128]{2,1,0:T(8,128)(2,1)}), bf16[16,1040,128]{2,1,0:T(8,128)(2,1)}, u32[]{:S(2)}, u32[]{:S(2)}) %all-to-all-start) | async-done | bytes 4259872 | tf_op jit(solution)/shard_map/all_to_all | solution.py:256
  107.8 4.9 %all-to-all-start.1 = ((bf16[16,1024,128]{2,1,0:T(8,128)(2,1)}), bf16[16,1024,128]{2,1,0:T(8,128)(2,1)}, u32[]{:S(2)}, u32[]{:S(2)}) async-start(bf16[16,1024,128]{2,1,0:T(8,128)(2,1)} %pack_phase.3), calls=%async_computation.1 | async-start | bytes 8388608 | tf_op jit(solution)/shard_map/all_to_all | solution.py:256
  112.7 1.7 slice.14
  114.4 0.4 collective-permute-start.2
  114.8 0.9 fusion.4
  115.8 0.7 reshape.19.table_ref
  116.4 2.3 collective-permute-done.2.other_ref
  118.8 51.6 %attend_head.3 = (bf16[16,768,128]{2,1,0:T(8,128)(2,1)}, f32[8192,128]{1,0:T(8,128)}, bf16[16,512,128]{2,1,0:T(8,128)(2,1)}) custom-call(s32[512]{0:T(512)} %reshape.19.table_ref, bf16[16,1040,128]{2,1,0:T(8,128)(2,1)} %all-to-all-done.qg_ref.mine_ref, bf16[16,1040,128]{2,1,0:T(8,128)(2,1)} %all-to-all-done.qg_ref.mine_ref, ...), custom_call_target="tpu_custom_call" | custom-call | flops 12079595520 | bytes 25165824 | tf_op jit(solution)/shard_map/attend_head/pallas_call | solution.py:460
  170.4 0.4 collective-permute-start.3
  170.8 4.0 %collective-permute-done.3.given_ref = bf16[16,512,128]{2,1,0:T(8,128)(2,1)S(1)} collective-permute-done((bf16[16,512,128]{2,1,0:T(8,128)(2,1)}, bf16[16,512,128]{2,1,0:T(8,128)(2,1)S(1)}, u32[]{:S(2)}, u32[]{:S(2)}) %collective-permute-start.3) | collective-permute-done | bytes 2097184 | tf_op jit(solution)/shard_map/ppermute | solution.py:563
  174.8 1.3 copy-done.1
  176.1 4.7 %merge_sums.3 = bf16[16,768,128]{2,1,0:T(8,128)(2,1)} custom-call(f32[16,512,128]{2,1,0:T(8,128)} %bitcast.4, bf16[16,512,128]{2,1,0:T(8,128)(2,1)} %copy-done.1, bf16[16,768,128]{2,1,0:T(8,128)(2,1)} %get-tuple-element.17.before_ref), custom_call_target="tpu_custom_call", output_to_operand_aliasing={{}: (2, {})} | custom-call | bytes 8388608 | tf_op jit(solution)/shard_map/merge_sums/pallas_call | solution.py:500
  180.8 24.3 %all-to-all-done.1.qg_ref.mine_ref = bf16[16,1024,128]{2,1,0:T(8,128)(2,1)} async-done(((bf16[16,1024,128]{2,1,0:T(8,128)(2,1)}), bf16[16,1024,128]{2,1,0:T(8,128)(2,1)}, u32[]{:S(2)}, u32[]{:S(2)}) %all-to-all-start.1) | async-done | bytes 4194336 | tf_op jit(solution)/shard_map/all_to_all | solution.py:256
  205.1 4.9 %all-to-all-start.3 = ((bf16[16,768,128]{2,1,0:T(8,128)(2,1)}), bf16[16,768,128]{2,1,0:T(8,128)(2,1)S(1)}, u32[]{:S(2)}, u32[]{:S(2)}) async-start(bf16[16,768,128]{2,1,0:T(8,128)(2,1)} %merge_sums.3), calls=%async_computation.3 | async-start | bytes 6291456 | tf_op jit(solution)/shard_map/all_to_all | solution.py:256
  210.0 1.7 slice.13
  211.8 0.4 collective-permute-start
  212.2 3.9 %collective-permute-done.other_ref = bf16[16,512,128]{2,1,0:T(8,128)(2,1)} collective-permute-done((bf16[16,512,128]{2,1,0:T(8,128)(2,1)S(1)}, bf16[16,512,128]{2,1,0:T(8,128)(2,1)}, u32[]{:S(2)}, u32[]{:S(2)}) %collective-permute-start) | collective-permute-done | bytes 2097184 | tf_op jit(solution)/shard_map/ppermute | solution.py:563
  216.1 51.7 %attend_head.2 = (bf16[16,768,128]{2,1,0:T(8,128)(2,1)}, f32[8192,128]{1,0:T(8,128)}, bf16[16,512,128]{2,1,0:T(8,128)(2,1)}) custom-call(s32[512]{0:T(512)} %reshape.19.table_ref, bf16[16,1024,128]{2,1,0:T(8,128)(2,1)} %all-to-all-done.1.qg_ref.mine_ref, bf16[16,1024,128]{2,1,0:T(8,128)(2,1)} %all-to-all-done.1.qg_ref.mine_ref, ...), custom_call_target="tpu_custom_call" | custom-call | flops 12079595520 | bytes 25165824 | tf_op jit(solution)/shard_map/attend_head/pallas_call | solution.py:460
  267.8 0.4 collective-permute-start.1
  268.3 4.1 %collective-permute-done.1.given_ref = bf16[16,512,128]{2,1,0:T(8,128)(2,1)} collective-permute-done((bf16[16,512,128]{2,1,0:T(8,128)(2,1)}, bf16[16,512,128]{2,1,0:T(8,128)(2,1)}, u32[]{:S(2)}, u32[]{:S(2)}) %collective-permute-start.1) | collective-permute-done | bytes 2097184 | tf_op jit(solution)/shard_map/ppermute | solution.py:563
  272.4 4.7 %merge_sums.2 = bf16[16,768,128]{2,1,0:T(8,128)(2,1)} custom-call(f32[16,512,128]{2,1,0:T(8,128)} %bitcast.3, bf16[16,512,128]{2,1,0:T(8,128)(2,1)} %collective-permute-done.1.given_ref, bf16[16,768,128]{2,1,0:T(8,128)(2,1)} %get-tuple-element.14.before_ref), custom_call_target="tpu_custom_call", output_to_operand_aliasing={{}: (2, {})} | custom-call | bytes 8388608 | tf_op jit(solution)/shard_map/merge_sums/pallas_call | solution.py:500
  277.1 2.9 all-to-all-done.3.in_ref
  279.9 1.7 copy-done
  281.6 4.9 %all-to-all-start.2 = ((bf16[16,768,128]{2,1,0:T(8,128)(2,1)}), bf16[16,768,128]{2,1,0:T(8,128)(2,1)}, u32[]{:S(2)}, u32[]{:S(2)}) async-start(bf16[16,768,128]{2,1,0:T(8,128)(2,1)} %merge_sums.2), calls=%async_computation.2 | async-start | bytes 6291456 | tf_op jit(solution)/shard_map/all_to_all | solution.py:256
  286.5 4.5 %unpack_phase.2 = (bf16[1024,1024]{1,0:T(8,128)(2,1)}, bf16[1024,1024]{1,0:T(8,128)(2,1)}, bf16[1024,1024]{1,0:T(8,128)(2,1)}) custom-call(bf16[16,768,128]{2,1,0:T(8,128)(2,1)} %copy-done), custom_call_target="tpu_custom_call" | custom-call | bytes 6291456 | tf_op jit(solution)/shard_map/unpack_phase/pallas_call | solution.py:539
  291.0 65.5 %all-to-all-done.2.in_ref = bf16[16,768,128]{2,1,0:T(8,128)(2,1)} async-done(((bf16[16,768,128]{2,1,0:T(8,128)(2,1)}), bf16[16,768,128]{2,1,0:T(8,128)(2,1)}, u32[]{:S(2)}, u32[]{:S(2)}) %all-to-all-start.2) | async-done | bytes 3145760 | tf_op jit(solution)/shard_map/all_to_all | solution.py:256
  356.5 4.5 %unpack_phase.3 = (bf16[1024,1024]{1,0:T(8,128)(2,1)}, bf16[1024,1024]{1,0:T(8,128)(2,1)}, bf16[1024,1024]{1,0:T(8,128)(2,1)}) custom-call(bf16[16,768,128]{2,1,0:T(8,128)(2,1)} %all-to-all-done.2.in_ref, bf16[1024,1024]{1,0:T(8,128)(2,1)} %get-tuple-element.18.refs_0_, ...), custom_call_target="tpu_custom_call", output_to_operand_aliasing={{0}: (1, {}), {1}: (2, {}), {2}: (3, {})} | custom-call | bytes 6291456 | tf_op jit(solution)/shard_map/unpack_phase/pallas_call | solution.py:539
  (2 shorter events, 0.0 us)
Async XLA Ops:
  7.3 100.4 %all-to-all-start = ((bf16[16,1040,128]{2,1,0:T(8,128)(2,1)}), bf16[16,1040,128]{2,1,0:T(8,128)(2,1)}, u32[]{:S(2)}, u32[]{:S(2)}) async-start(bf16[16,1040,128]{2,1,0:T(8,128)(2,1)} %pack_phase.2), calls=%async_computation | async-start | bytes 8519680 | tf_op jit(solution)/shard_map/all_to_all | solution.py:256
  107.8 97.4 %all-to-all-start.1 = ((bf16[16,1024,128]{2,1,0:T(8,128)(2,1)}), bf16[16,1024,128]{2,1,0:T(8,128)(2,1)}, u32[]{:S(2)}, u32[]{:S(2)}) async-start(bf16[16,1024,128]{2,1,0:T(8,128)(2,1)} %pack_phase.3), calls=%async_computation.1 | async-start | bytes 8388608 | tf_op jit(solution)/shard_map/all_to_all | solution.py:256
  114.4 4.4 %collective-permute-start.2 = (bf16[16,512,128]{2,1,0:T(8,128)(2,1)S(1)}, bf16[16,512,128]{2,1,0:T(8,128)(2,1)}, u32[]{:S(2)}, u32[]{:S(2)}) collective-permute-start(bf16[16,512,128]{2,1,0:T(8,128)(2,1)S(1)} %slice.14), channel_id=1, source_target_pairs={{0,1},{1,0},{2,3},{3,2},{4,5},{5,4},{6,7},{7,6},{8,9},{9,8},{10,11... | collective-permute-start | bytes 6291464 | tf_op jit(solution)/shard_map/ppermute | solution.py:563
  170.4 4.4 %collective-permute-start.3 = (bf16[16,512,128]{2,1,0:T(8,128)(2,1)}, bf16[16,512,128]{2,1,0:T(8,128)(2,1)S(1)}, u32[]{:S(2)}, u32[]{:S(2)}) collective-permute-start(bf16[16,512,128]{2,1,0:T(8,128)(2,1)} %get-tuple-element.16), channel_id=1, source_target_pairs={{0,1},{1,0},{2,3},{3,2},{4,5},{5,4},{6,7},{7,6},{8,9},{9,8},{10,11... | collective-permute-start | bytes 6291464 | tf_op jit(solution)/shard_map/ppermute | solution.py:563
  174.8 1.3 copy-start.1
  205.1 74.8 %all-to-all-start.3 = ((bf16[16,768,128]{2,1,0:T(8,128)(2,1)}), bf16[16,768,128]{2,1,0:T(8,128)(2,1)S(1)}, u32[]{:S(2)}, u32[]{:S(2)}) async-start(bf16[16,768,128]{2,1,0:T(8,128)(2,1)} %merge_sums.3), calls=%async_computation.3 | async-start | bytes 6291456 | tf_op jit(solution)/shard_map/all_to_all | solution.py:256
  211.8 4.4 %collective-permute-start = (bf16[16,512,128]{2,1,0:T(8,128)(2,1)S(1)}, bf16[16,512,128]{2,1,0:T(8,128)(2,1)}, u32[]{:S(2)}, u32[]{:S(2)}) collective-permute-start(bf16[16,512,128]{2,1,0:T(8,128)(2,1)S(1)} %slice.13), channel_id=1, source_target_pairs={{0,1},{1,0},{2,3},{3,2},{4,5},{5,4},{6,7},{7,6},{8,9},{9,8},{10,11... | collective-permute-start | bytes 6291464 | tf_op jit(solution)/shard_map/ppermute | solution.py:563
  267.8 4.6 %collective-permute-start.1 = (bf16[16,512,128]{2,1,0:T(8,128)(2,1)}, bf16[16,512,128]{2,1,0:T(8,128)(2,1)}, u32[]{:S(2)}, u32[]{:S(2)}) collective-permute-start(bf16[16,512,128]{2,1,0:T(8,128)(2,1)} %get-tuple-element.13), channel_id=1, source_target_pairs={{0,1},{1,0},{2,3},{3,2},{4,5},{5,4},{6,7},{7,6},{8,9},{9,8},{10,11... | collective-permute-start | bytes 6291464 | tf_op jit(solution)/shard_map/ppermute | solution.py:563
  279.9 1.7 copy-start
  281.6 74.9 %all-to-all-start.2 = ((bf16[16,768,128]{2,1,0:T(8,128)(2,1)}), bf16[16,768,128]{2,1,0:T(8,128)(2,1)}, u32[]{:S(2)}, u32[]{:S(2)}) async-start(bf16[16,768,128]{2,1,0:T(8,128)(2,1)} %merge_sums.2), calls=%async_computation.2 | async-start | bytes 6291456 | tf_op jit(solution)/shard_map/all_to_all | solution.py:256

commit v7 on v6

--- a/solution.py
+++ b/solution.py
@@ -14,6 +14,8 @@
 CHUNKS = 2
 DEPTH = 4
 PHASES = 2
+EXTRA = 16
+SMALL_LIMIT = 16 * 1024 * 1024
 VMEM_LIMIT = 60 * 1024 * 1024
 
 
@@ -267,36 +269,44 @@
     kv = merge_lanes(k_ref[...], v_ref[...])
     qg = merge_lanes(q_ref[...], g_ref[...])
     for head in range(2):
-        for core in range(2):
-            part = slice(core * tokens, (core + 1) * tokens)
-            out_ref[2 * head + core, :tokens, :] = kv[head][part]
-            out_ref[2 * head + core, tokens : 2 * tokens, :] = qg[head][part]
-            if len(refs) > 1:
-                out_ref[2 * head + core, 2 * tokens :, :] = refs[0][core]
+        out_ref[head, 0, :tokens, :] = kv[head]
+        out_ref[head, 0, tokens : 2 * tokens, :] = qg[head]
+    if len(refs) > 1:
+        table = refs[0][...].astype(jnp.float32)
+        table = jnp.concatenate(
+            [table, jnp.zeros((table.shape[0], PAIR - table.shape[1]), jnp.float32)], axis=1
+        )
+        table = jnp.concatenate(
+            [table, jnp.zeros((EXTRA - table.shape[0], PAIR), jnp.float32)], axis=0
+        ).astype(jnp.bfloat16)
+        for head in range(2):
+            out_ref[head, 0, 2 * tokens :, :] = table
 
 
 def pack_phase(key_rows, value_rows, queries, grad_out, phase, extra=None):
     rows, width = queries.shape
+    tokens = rows // 2
     slabs = width // PAIR // PHASES
-    spec = pl.BlockSpec((rows, PAIR), lambda j: (0, phase * slabs + j))
+    spec = pl.BlockSpec((tokens, PAIR), lambda j, c: (c, phase * slabs + j))
     in_specs, operands = [spec] * 4, [key_rows, value_rows, queries, grad_out]
     length = rows
     if extra is not None:
-        length += extra.shape[1]
-        in_specs.append(pl.BlockSpec(extra.shape, lambda j: (0, 0, 0)))
+        length += EXTRA
+        in_specs.append(pl.BlockSpec(extra.shape, lambda j, c: (0, 0)))
         operands.append(extra)
-    return pl.pallas_call(
-        functools.partial(pack_kernel, rows // 2),
-        grid=(slabs,),
+    packed = pl.pallas_call(
+        functools.partial(pack_kernel, tokens),
+        grid=(slabs, 2),
         in_specs=in_specs,
-        out_specs=pl.BlockSpec((4, length, PAIR), lambda j: (j, 0, 0)),
-        out_shape=jax.ShapeDtypeStruct((4 * slabs, length, PAIR), jnp.bfloat16),
+        out_specs=pl.BlockSpec((2, 1, length, PAIR), lambda j, c: (j, c, 0, 0)),
+        out_shape=jax.ShapeDtypeStruct((2 * slabs, 2, length, PAIR), jnp.bfloat16),
         cost_estimate=pl.CostEstimate(
             flops=0, bytes_accessed=8 * rows * width, transcendentals=0
         ),
         compiler_params=pltpu.CompilerParams(vmem_limit_bytes=VMEM_LIMIT),
         name="pack_phase",
     )(*operands)
+    return packed.reshape(4 * slabs, length, PAIR)
 
 
 def head_kernel(picks, table_ref, qg_ref, mine_ref, other_ref, out_ref, sum_ref, give_ref, *scratch):
@@ -514,39 +524,35 @@
 
 def unpack_kernel(tokens, in_ref, *refs):
     gq_ref, gk_ref, gv_ref = refs[-3:]
-    for core in range(2):
-        part = slice(core * tokens, (core + 1) * tokens)
-        gk_ref[part, :], gv_ref[part, :] = merge_lanes(
-            in_ref[core, :tokens, :], in_ref[2 + core, :tokens, :]
-        )
-        for m in range(tokens // TILE // 2):
-            rows = slice(tokens + m * TILE, tokens + (m + 1) * TILE)
-            even, odd = merge_lanes(in_ref[core, rows, :], in_ref[2 + core, rows, :])
-            base = core * tokens + 2 * m * TILE
-            gq_ref[base : base + TILE, :] = even
-            gq_ref[base + TILE : base + 2 * TILE, :] = odd
+    gk_ref[...], gv_ref[...] = merge_lanes(in_ref[0, 0, :tokens, :], in_ref[1, 0, :tokens, :])
+    for m in range(tokens // TILE // 2):
+        rows = slice(tokens + m * TILE, tokens + (m + 1) * TILE)
+        even, odd = merge_lanes(in_ref[0, 0, rows, :], in_ref[1, 0, rows, :])
+        gq_ref[2 * m * TILE : (2 * m + 1) * TILE, :] = even
+        gq_ref[(2 * m + 1) * TILE : (2 * m + 2) * TILE, :] = odd
 
 
 def unpack_phase(back, previous, phase, rows, width):
     slabs = width // PAIR // PHASES
-    in_specs = [pl.BlockSpec((4, back.shape[1], PAIR), lambda j: (j, 0, 0))]
-    operands = [back]
+    tokens = rows // 2
+    in_specs = [pl.BlockSpec((2, 1, back.shape[1], PAIR), lambda j, c: (j, c, 0, 0))]
+    operands = [back.reshape(2 * slabs, 2, back.shape[1], PAIR)]
     aliases = {}
     if previous is not None:
         in_specs += [pl.BlockSpec(memory_space=pl.ANY)] * 3
         operands += list(previous)
         aliases = {1: 0, 2: 1, 3: 2}
     return pl.pallas_call(
-        functools.partial(unpack_kernel, rows // 2),
-        grid=(slabs,),
+        functools.partial(unpack_kernel, tokens),
+        grid=(slabs, 2),
         in_specs=in_specs,
-        out_specs=[pl.BlockSpec((rows, PAIR), lambda j: (0, phase * slabs + j))] * 3,
+        out_specs=[pl.BlockSpec((tokens, PAIR), lambda j, c: (c, phase * slabs + j))] * 3,
         out_shape=[jax.ShapeDtypeStruct((rows, width), jnp.bfloat16)] * 3,
         input_output_aliases=aliases,
         cost_estimate=pl.CostEstimate(
             flops=0, bytes_accessed=6 * rows * width, transcendentals=0
         ),
-        compiler_params=pltpu.CompilerParams(vmem_limit_bytes=VMEM_LIMIT),
+        compiler_params=pltpu.CompilerParams(vmem_limit_bytes=SMALL_LIMIT),
         name="unpack_phase",
     )(*operands)
 
@@ -562,15 +568,16 @@
     def swap(x):
         return lax.ppermute(x, "ctx", [(i, i ^ 1) for i in range(peers)])
 
-    extra = tile_keys.astype(jnp.bfloat16).reshape(2, half, picks)
-    extra = jnp.pad(extra, ((0, 0), (0, 16 - half), (0, PAIR - picks)))
     received = [
         exchange(
-            pack_phase(key_rows, value_rows, queries, grad_out, p, extra if p == 0 else None)
+            pack_phase(
+                key_rows, value_rows, queries, grad_out, p, tile_keys if p == 0 else None
+            )
         )
         for p in range(PHASES)
     ]
-    table = received[0][:, 2 * tokens : 2 * tokens + half, :picks].astype(jnp.int32)
+    table = received[0][:, 2 * tokens : 2 * tokens + blocks, :picks].astype(jnp.int32)
+    table = jnp.where(core == 0, table[:, :half], table[:, half:])
     local = table % blocks
     side = (local // half + core) % 2
     table = (side * (peers * half) + table // blocks * half + local % half).reshape(-1)
@@ -618,7 +625,7 @@
     peers = lax.axis_size("ctx")
     blocks = tile_keys.shape[0]
     one_head_each = peers * HD == queries.shape[1]
-    even = peers % 4 == 0 and blocks % 4 == 0 and blocks <= 32
+    even = peers % 4 == 0 and blocks % 4 == 0 and blocks <= EXTRA
     fits = one_head_each and even and peers * blocks <= 256
     plan = by_heads if fits else by_blocks
     return tuple(plan(queries, key_rows, value_rows, grad_out, tile_keys))

time: 362 us -> 363 us (level)
  Pallas kernels: 132 us -> 138 us
    pallas_call x4, Pallas kernels: 19.6 us -> 25 us  [the longest x2 14.8 us: pack_phase(): pl.pallas_call(functools.partial(pack_kernel, tokens), grid=(slabs, 2), i...]
where the time goes in v7:
time: 363 us; the launch traced here: 362 us
  waiting for transfers between devices  194 us (53%)
  Pallas kernels  138 us (38%)
  starting transfers between devices  23 us (6%)
  local copies, waits for them, and re-layouts  5.48 us (2%)
    all_to_all x4, waiting for transfers between devices, exchange(): return lax.all_to_all(x, 'ctx', split_axis=0, concat_axis=0, tiled=True)  180 us
    pallas_call x2, Pallas kernels, attend_head(): pl.pallas_call(functools.partial(head_kernel, picks), grid_spec=pltpu.Pre...  103 us
    all_to_all x4, starting transfers between devices, exchange(): return lax.all_to_all(x, 'ctx', split_axis=0, concat_axis=0, tiled=True)  21.3 us
    pallas_call x2, Pallas kernels, pack_phase(): pl.pallas_call(functools.partial(pack_kernel, tokens), grid=(slabs, 2), i...  14.8 us
    ppermute x4, waiting for transfers between devices, swap(): return lax.ppermute(x, 'ctx', [(i, i ^ 1) for i in range(peers)])  14.4 us
    pallas_call x2, Pallas kernels, unpack_phase(): pl.pallas_call(functools.partial(unpack_kernel, tokens), grid=(slabs, 2),...  10.1 us
    pallas_call x2, Pallas kernels, merge_sums(): pl.pallas_call(merge_kernel, grid=(peers // step,), in_specs=[spec, spec,...  9.28 us
  transfers between devices with their start and end apart: 8, of which 8 were waited for; matrix products, arithmetic and copies ran while one was open for 1% of the time, Pallas kernels for 34%

profile of v7, /device:TPU:13, one launch (start us, length us, event | category | flops | bytes accessed | tf_op | source)
XLA Modules:
  0.0 361.9 jit_solution(6324453748144018508)
XLA Ops:
  0.6 7.4 %pack_phase.2 = bf16[8,2,1040,128]{3,2,1,0:T(8,128)(2,1)} custom-call(bf16[1024,1024]{1,0:T(8,128)(2,1)} %k_ref.3, bf16[1024,1024]{1,0:T(8,128)(2,1)} %v_ref.3, bf16[1024,1024]{1,0:T(8,128)(2,1)} %q_ref.3, bf16[1024,1024]{1,0:T(8,128)(2,1)} %g_ref.3, s32[8,8]{1,0:T(8,128)} %refs_0_.1), custom_call_target="tpu_custom_call" | custom-call | bytes 8388608 | tf_op jit(solution)/shard_map/pack_phase/pallas_call | solution.py:297
  8.0 6.6 %all-to-all-start = ((bf16[16,1040,128]{2,1,0:T(8,128)(2,1)}), bf16[16,1040,128]{2,1,0:T(8,128)(2,1)}, u32[]{:S(2)}, u32[]{:S(2)}) async-start(bf16[16,1040,128]{2,1,0:T(8,128)(2,1)} %bitcast.7), calls=%async_computation | async-start | bytes 8519680 | tf_op jit(solution)/shard_map/all_to_all | solution.py:258
  14.6 7.4 %pack_phase.3 = bf16[8,2,1024,128]{3,2,1,0:T(8,128)(2,1)} custom-call(bf16[1024,1024]{1,0:T(8,128)(2,1)} %k_ref.3, bf16[1024,1024]{1,0:T(8,128)(2,1)} %v_ref.3, bf16[1024,1024]{1,0:T(8,128)(2,1)} %q_ref.3, bf16[1024,1024]{1,0:T(8,128)(2,1)} %g_ref.3), custom_call_target="tpu_custom_call" | custom-call | bytes 8388608 | tf_op jit(solution)/shard_map/pack_phase/pallas_call | solution.py:297
  22.0 86.4 %all-to-all-done.qg_ref.mine_ref = bf16[16,1040,128]{2,1,0:T(8,128)(2,1)} async-done(((bf16[16,1040,128]{2,1,0:T(8,128)(2,1)}), bf16[16,1040,128]{2,1,0:T(8,128)(2,1)}, u32[]{:S(2)}, u32[]{:S(2)}) %all-to-all-start) | async-done | bytes 4259872 | tf_op jit(solution)/shard_map/all_to_all | solution.py:258
  108.5 4.9 %all-to-all-start.1 = ((bf16[16,1024,128]{2,1,0:T(8,128)(2,1)}), bf16[16,1024,128]{2,1,0:T(8,128)(2,1)}, u32[]{:S(2)}, u32[]{:S(2)}) async-start(bf16[16,1024,128]{2,1,0:T(8,128)(2,1)} %bitcast.8), calls=%async_computation.1 | async-start | bytes 8388608 | tf_op jit(solution)/shard_map/all_to_all | solution.py:258
  113.4 1.7 slice.24
  115.1 0.4 collective-permute-start.2
  115.5 0.8 slice_convert_fusion
  116.3 0.2 fusion.4
  116.5 0.7 reshape.28.table_ref
  117.2 2.3 collective-permute-done.2.other_ref
  119.5 51.6 %attend_head.3 = (bf16[16,768,128]{2,1,0:T(8,128)(2,1)}, f32[8192,128]{1,0:T(8,128)}, bf16[16,512,128]{2,1,0:T(8,128)(2,1)}) custom-call(s32[512]{0:T(512)} %reshape.28.table_ref, bf16[16,1040,128]{2,1,0:T(8,128)(2,1)} %all-to-all-done.qg_ref.mine_ref, bf16[16,1040,128]{2,1,0:T(8,128)(2,1)} %all-to-all-done.qg_ref.mine_ref, ...), custom_call_target="tpu_custom_call" | custom-call | flops 12079595520 | bytes 25165824 | tf_op jit(solution)/shard_map/attend_head/pallas_call | solution.py:470
  171.1 0.4 collective-permute-start.3
  171.5 4.0 %collective-permute-done.3.given_ref = bf16[16,512,128]{2,1,0:T(8,128)(2,1)S(1)} collective-permute-done((bf16[16,512,128]{2,1,0:T(8,128)(2,1)}, bf16[16,512,128]{2,1,0:T(8,128)(2,1)S(1)}, u32[]{:S(2)}, u32[]{:S(2)}) %collective-permute-start.3) | collective-permute-done | bytes 2097184 | tf_op jit(solution)/shard_map/ppermute | solution.py:569
  175.5 0.0 copy-start
  175.5 1.3 copy-done
  176.8 4.6 %merge_sums.3 = bf16[16,768,128]{2,1,0:T(8,128)(2,1)} custom-call(f32[16,512,128]{2,1,0:T(8,128)} %bitcast.10, bf16[16,512,128]{2,1,0:T(8,128)(2,1)} %copy-done, bf16[16,768,128]{2,1,0:T(8,128)(2,1)} %get-tuple-element.17.before_ref), custom_call_target="tpu_custom_call", output_to_operand_aliasing={{}: (2, {})} | custom-call | bytes 8388608 | tf_op jit(solution)/shard_map/merge_sums/pallas_call | solution.py:510
  181.5 24.4 %all-to-all-done.1.qg_ref.mine_ref = bf16[16,1024,128]{2,1,0:T(8,128)(2,1)} async-done(((bf16[16,1024,128]{2,1,0:T(8,128)(2,1)}), bf16[16,1024,128]{2,1,0:T(8,128)(2,1)}, u32[]{:S(2)}, u32[]{:S(2)}) %all-to-all-start.1) | async-done | bytes 4194336 | tf_op jit(solution)/shard_map/all_to_all | solution.py:258
  205.8 4.9 %all-to-all-start.3 = ((bf16[16,768,128]{2,1,0:T(8,128)(2,1)}), bf16[16,768,128]{2,1,0:T(8,128)(2,1)S(1)}, u32[]{:S(2)}, u32[]{:S(2)}) async-start(bf16[16,768,128]{2,1,0:T(8,128)(2,1)} %merge_sums.3), calls=%async_computation.3 | async-start | bytes 6291456 | tf_op jit(solution)/shard_map/all_to_all | solution.py:258
  210.8 1.7 slice.23
  212.5 0.4 collective-permute-start
  212.9 3.9 %collective-permute-done.other_ref = bf16[16,512,128]{2,1,0:T(8,128)(2,1)} collective-permute-done((bf16[16,512,128]{2,1,0:T(8,128)(2,1)S(1)}, bf16[16,512,128]{2,1,0:T(8,128)(2,1)}, u32[]{:S(2)}, u32[]{:S(2)}) %collective-permute-start) | collective-permute-done | bytes 2097184 | tf_op jit(solution)/shard_map/ppermute | solution.py:569
  216.9 51.7 %attend_head.2 = (bf16[16,768,128]{2,1,0:T(8,128)(2,1)}, f32[8192,128]{1,0:T(8,128)}, bf16[16,512,128]{2,1,0:T(8,128)(2,1)}) custom-call(s32[512]{0:T(512)} %reshape.28.table_ref, bf16[16,1024,128]{2,1,0:T(8,128)(2,1)} %all-to-all-done.1.qg_ref.mine_ref, bf16[16,1024,128]{2,1,0:T(8,128)(2,1)} %all-to-all-done.1.qg_ref.mine_ref, ...), custom_call_target="tpu_custom_call" | custom-call | flops 12079595520 | bytes 25165824 | tf_op jit(solution)/shard_map/attend_head/pallas_call | solution.py:470
  268.6 0.4 collective-permute-start.1
  269.0 4.1 %collective-permute-done.1.given_ref = bf16[16,512,128]{2,1,0:T(8,128)(2,1)} collective-permute-done((bf16[16,512,128]{2,1,0:T(8,128)(2,1)}, bf16[16,512,128]{2,1,0:T(8,128)(2,1)}, u32[]{:S(2)}, u32[]{:S(2)}) %collective-permute-start.1) | collective-permute-done | bytes 2097184 | tf_op jit(solution)/shard_map/ppermute | solution.py:569
  273.1 4.6 %merge_sums.2 = bf16[16,768,128]{2,1,0:T(8,128)(2,1)} custom-call(f32[16,512,128]{2,1,0:T(8,128)} %bitcast.9, bf16[16,512,128]{2,1,0:T(8,128)(2,1)} %collective-permute-done.1.given_ref, bf16[16,768,128]{2,1,0:T(8,128)(2,1)} %get-tuple-element.14.before_ref), custom_call_target="tpu_custom_call", output_to_operand_aliasing={{}: (2, {})} | custom-call | bytes 8388608 | tf_op jit(solution)/shard_map/merge_sums/pallas_call | solution.py:510
  277.8 2.9 all-to-all-done.3
  280.6 4.9 %all-to-all-start.2 = ((bf16[16,768,128]{2,1,0:T(8,128)(2,1)}), bf16[16,768,128]{2,1,0:T(8,128)(2,1)}, u32[]{:S(2)}, u32[]{:S(2)}) async-start(bf16[16,768,128]{2,1,0:T(8,128)(2,1)} %merge_sums.2), calls=%async_computation.2 | async-start | bytes 6291456 | tf_op jit(solution)/shard_map/all_to_all | solution.py:258
  285.5 3.7 %unpack_phase.2 = (bf16[1024,1024]{1,0:T(8,128)(2,1)}, bf16[1024,1024]{1,0:T(8,128)(2,1)}, bf16[1024,1024]{1,0:T(8,128)(2,1)}) custom-call(bf16[8,2,768,128]{3,2,1,0:T(8,128)(2,1)S(1)} %bitcast.6), custom_call_target="tpu_custom_call" | custom-call | bytes 6291456 | tf_op jit(solution)/shard_map/unpack_phase/pallas_call | solution.py:545
  289.3 66.3 %all-to-all-done.2 = bf16[16,768,128]{2,1,0:T(8,128)(2,1)} async-done(((bf16[16,768,128]{2,1,0:T(8,128)(2,1)}), bf16[16,768,128]{2,1,0:T(8,128)(2,1)}, u32[]{:S(2)}, u32[]{:S(2)}) %all-to-all-start.2) | async-done | bytes 3145760 | tf_op jit(solution)/shard_map/all_to_all | solution.py:258
  355.5 6.4 %unpack_phase.3 = (bf16[1024,1024]{1,0:T(8,128)(2,1)}, bf16[1024,1024]{1,0:T(8,128)(2,1)}, bf16[1024,1024]{1,0:T(8,128)(2,1)}) custom-call(bf16[8,2,768,128]{3,2,1,0:T(8,128)(2,1)} %bitcast.3.in_ref, bf16[1024,1024]{1,0:T(8,128)(2,1)} %get-tuple-element.18.refs_0_, ...), custom_call_target="tpu_custom_call", output_to_operand_aliasing={{0}: (1, {}), {1}: (2, {}), {2}: (3, {})} | custom-call | bytes 6291456 | tf_op jit(solution)/shard_map/unpack_phase/pallas_call | solution.py:545
Async XLA Ops:
  8.0 100.4 %all-to-all-start = ((bf16[16,1040,128]{2,1,0:T(8,128)(2,1)}), bf16[16,1040,128]{2,1,0:T(8,128)(2,1)}, u32[]{:S(2)}, u32[]{:S(2)}) async-start(bf16[16,1040,128]{2,1,0:T(8,128)(2,1)} %bitcast.7), calls=%async_computation | async-start | bytes 8519680 | tf_op jit(solution)/shard_map/all_to_all | solution.py:258
  108.5 97.4 %all-to-all-start.1 = ((bf16[16,1024,128]{2,1,0:T(8,128)(2,1)}), bf16[16,1024,128]{2,1,0:T(8,128)(2,1)}, u32[]{:S(2)}, u32[]{:S(2)}) async-start(bf16[16,1024,128]{2,1,0:T(8,128)(2,1)} %bitcast.8), calls=%async_computation.1 | async-start | bytes 8388608 | tf_op jit(solution)/shard_map/all_to_all | solution.py:258
  115.1 4.4 %collective-permute-start.2 = (bf16[16,512,128]{2,1,0:T(8,128)(2,1)S(1)}, bf16[16,512,128]{2,1,0:T(8,128)(2,1)}, u32[]{:S(2)}, u32[]{:S(2)}) collective-permute-start(bf16[16,512,128]{2,1,0:T(8,128)(2,1)S(1)} %slice.24), channel_id=1, source_target_pairs={{0,1},{1,0},{2,3},{3,2},{4,5},{5,4},{6,7},{7,6},{8,9},{9,8},{10,11... | collective-permute-start | bytes 6291464 | tf_op jit(solution)/shard_map/ppermute | solution.py:569
  171.1 4.4 %collective-permute-start.3 = (bf16[16,512,128]{2,1,0:T(8,128)(2,1)}, bf16[16,512,128]{2,1,0:T(8,128)(2,1)S(1)}, u32[]{:S(2)}, u32[]{:S(2)}) collective-permute-start(bf16[16,512,128]{2,1,0:T(8,128)(2,1)} %get-tuple-element.16), channel_id=1, source_target_pairs={{0,1},{1,0},{2,3},{3,2},{4,5},{5,4},{6,7},{7,6},{8,9},{9,8},{10,11... | collective-permute-start | bytes 6291464 | tf_op jit(solution)/shard_map/ppermute | solution.py:569
  175.5 1.3 copy-start
  205.8 74.8 %all-to-all-start.3 = ((bf16[16,768,128]{2,1,0:T(8,128)(2,1)}), bf16[16,768,128]{2,1,0:T(8,128)(2,1)S(1)}, u32[]{:S(2)}, u32[]{:S(2)}) async-start(bf16[16,768,128]{2,1,0:T(8,128)(2,1)} %merge_sums.3), calls=%async_computation.3 | async-start | bytes 6291456 | tf_op jit(solution)/shard_map/all_to_all | solution.py:258
  212.5 4.4 %collective-permute-start = (bf16[16,512,128]{2,1,0:T(8,128)(2,1)S(1)}, bf16[16,512,128]{2,1,0:T(8,128)(2,1)}, u32[]{:S(2)}, u32[]{:S(2)}) collective-permute-start(bf16[16,512,128]{2,1,0:T(8,128)(2,1)S(1)} %slice.23), channel_id=1, source_target_pairs={{0,1},{1,0},{2,3},{3,2},{4,5},{5,4},{6,7},{7,6},{8,9},{9,8},{10,11... | collective-permute-start | bytes 6291464 | tf_op jit(solution)/shard_map/ppermute | solution.py:569
  268.6 4.6 %collective-permute-start.1 = (bf16[16,512,128]{2,1,0:T(8,128)(2,1)}, bf16[16,512,128]{2,1,0:T(8,128)(2,1)}, u32[]{:S(2)}, u32[]{:S(2)}) collective-permute-start(bf16[16,512,128]{2,1,0:T(8,128)(2,1)} %get-tuple-element.13), channel_id=1, source_target_pairs={{0,1},{1,0},{2,3},{3,2},{4,5},{5,4},{6,7},{7,6},{8,9},{9,8},{10,11... | collective-permute-start | bytes 6291464 | tf_op jit(solution)/shard_map/ppermute | solution.py:569
  280.6 74.9 %all-to-all-start.2 = ((bf16[16,768,128]{2,1,0:T(8,128)(2,1)}), bf16[16,768,128]{2,1,0:T(8,128)(2,1)}, u32[]{:S(2)}, u32[]{:S(2)}) async-start(bf16[16,768,128]{2,1,0:T(8,128)(2,1)} %merge_sums.2), calls=%async_computation.2 | async-start | bytes 6291456 | tf_op jit(solution)/shard_map/all_to_all | solution.py:258

commit v8 on v7

--- a/solution.py
+++ b/solution.py
@@ -15,6 +15,7 @@
 DEPTH = 4
 PHASES = 2
 EXTRA = 16
+PARTS = 4
 SMALL_LIMIT = 16 * 1024 * 1024
 VMEM_LIMIT = 60 * 1024 * 1024
 
@@ -264,49 +265,97 @@
     return low, high
 
 
-def pack_kernel(tokens, k_ref, v_ref, q_ref, g_ref, *refs):
-    out_ref = refs[-1]
-    kv = merge_lanes(k_ref[...], v_ref[...])
-    qg = merge_lanes(q_ref[...], g_ref[...])
-    for head in range(2):
-        out_ref[head, 0, :tokens, :] = kv[head]
-        out_ref[head, 0, tokens : 2 * tokens, :] = qg[head]
-    if len(refs) > 1:
-        table = refs[0][...].astype(jnp.float32)
+def pack_kernel(tokens, lanes, k_ref, v_ref, q_ref, g_ref, *refs):
+    has_table = len(refs) > 5
+    table_ref = refs[0]
+    out_ref, in_scr, out_scr, in_sems, out_sems = refs[-5:]
+    step = tokens // 2
+    sources = (k_ref, v_ref, q_ref, g_ref)
+    slabs = in_scr.shape[2] // PAIR
+    loads = [
+        [
+            pltpu.make_async_copy(
+                ref.at[pl.ds(t * step, step), pl.ds(lanes, slabs * PAIR)],
+                in_scr.at[n, pl.ds(t * step, step)],
+                in_sems.at[n, t],
+            )
+            for n, ref in enumerate(sources)
+        ]
+        for t in range(PARTS)
+    ]
+    for group in loads:
+        for load in group:
+            load.start()
+    stores = []
+
+    def send(core, start, count, sem):
+        rows = pl.ds(start, count)
+        copy = pltpu.make_async_copy(
+            out_scr.at[:, core, rows], out_ref.at[:, core, rows], out_sems.at[sem]
+        )
+        copy.start()
+        stores.append(copy)
+
+    if has_table:
+        table = table_ref[...].astype(jnp.float32)
         table = jnp.concatenate(
             [table, jnp.zeros((table.shape[0], PAIR - table.shape[1]), jnp.float32)], axis=1
         )
         table = jnp.concatenate(
             [table, jnp.zeros((EXTRA - table.shape[0], PAIR), jnp.float32)], axis=0
         ).astype(jnp.bfloat16)
-        for head in range(2):
-            out_ref[head, 0, 2 * tokens :, :] = table
+        for chip in range(2 * slabs):
+            for core in range(2):
+                out_scr[chip, core, 2 * tokens :, :] = table
+        for core in range(2):
+            send(core, 2 * tokens, EXTRA, 2 * PARTS + core)
+    for t in range(PARTS):
+        for load in loads[t]:
+            load.wait()
+        core, start = divmod(t, 2)
+        start *= step
+        rows = slice(t * step, (t + 1) * step)
+        for j in range(slabs):
+            cols = slice(j * PAIR, (j + 1) * PAIR)
+            for n, place in ((0, start), (2, tokens + start)):
+                low, high = merge_lanes(in_scr[n, rows, cols], in_scr[n + 1, rows, cols])
+                out_scr[2 * j, core, place : place + step, :] = low
+                out_scr[2 * j + 1, core, place : place + step, :] = high
+        send(core, start, step, 2 * t)
+        send(core, tokens + start, step, 2 * t + 1)
+    for copy in stores:
+        copy.wait()
 
 
 def pack_phase(key_rows, value_rows, queries, grad_out, phase, extra=None):
     rows, width = queries.shape
-    tokens = rows // 2
-    slabs = width // PAIR // PHASES
-    spec = pl.BlockSpec((tokens, PAIR), lambda j, c: (c, phase * slabs + j))
-    in_specs, operands = [spec] * 4, [key_rows, value_rows, queries, grad_out]
+    part = width // PHASES
+    chips = part // HD
+    any_spec = pl.BlockSpec(memory_space=pl.ANY)
+    in_specs, operands = [any_spec] * 4, [key_rows, value_rows, queries, grad_out]
     length = rows
     if extra is not None:
         length += EXTRA
-        in_specs.append(pl.BlockSpec(extra.shape, lambda j, c: (0, 0)))
+        in_specs.append(pl.BlockSpec(memory_space=pltpu.VMEM))
         operands.append(extra)
     packed = pl.pallas_call(
-        functools.partial(pack_kernel, tokens),
-        grid=(slabs, 2),
+        functools.partial(pack_kernel, rows // 2, phase * part),
         in_specs=in_specs,
-        out_specs=pl.BlockSpec((2, 1, length, PAIR), lambda j, c: (j, c, 0, 0)),
-        out_shape=jax.ShapeDtypeStruct((2 * slabs, 2, length, PAIR), jnp.bfloat16),
+        out_specs=any_spec,
+        out_shape=jax.ShapeDtypeStruct((chips, 2, length, PAIR), jnp.bfloat16),
+        scratch_shapes=[
+            pltpu.VMEM((4, rows, part), jnp.bfloat16),
+            pltpu.VMEM((chips, 2, length, PAIR), jnp.bfloat16),
+            pltpu.SemaphoreType.DMA((4, PARTS)),
+            pltpu.SemaphoreType.DMA((2 * PARTS + 2,)),
+        ],
         cost_estimate=pl.CostEstimate(
             flops=0, bytes_accessed=8 * rows * width, transcendentals=0
         ),
         compiler_params=pltpu.CompilerParams(vmem_limit_bytes=VMEM_LIMIT),
         name="pack_phase",
     )(*operands)
-    return packed.reshape(4 * slabs, length, PAIR)
+    return packed.reshape(2 * chips, length, PAIR)
 
 
 def head_kernel(picks, table_ref, qg_ref, mine_ref, other_ref, out_ref, sum_ref, give_ref, *scratch):
@@ -522,32 +571,74 @@
     )(sums.reshape(given.shape), given, payload)
 
 
-def unpack_kernel(tokens, in_ref, *refs):
-    gq_ref, gk_ref, gv_ref = refs[-3:]
-    gk_ref[...], gv_ref[...] = merge_lanes(in_ref[0, 0, :tokens, :], in_ref[1, 0, :tokens, :])
-    for m in range(tokens // TILE // 2):
-        rows = slice(tokens + m * TILE, tokens + (m + 1) * TILE)
-        even, odd = merge_lanes(in_ref[0, 0, rows, :], in_ref[1, 0, rows, :])
-        gq_ref[2 * m * TILE : (2 * m + 1) * TILE, :] = even
-        gq_ref[(2 * m + 1) * TILE : (2 * m + 2) * TILE, :] = odd
+def unpack_kernel(tokens, lanes, in_ref, *refs):
+    gq_ref, gk_ref, gv_ref, in_scr, gq_scr, gk_scr, gv_scr, in_sems, out_sems = refs[-9:]
+    step = tokens // 2
+    slabs = gq_scr.shape[1] // PAIR
+    loads = []
+    for t in range(PARTS):
+        core, side = divmod(t, 2)
+        places = (pl.ds(side * step, step), pl.ds(tokens + side * step // 2, step // 2))
+        loads.append(
+            [
+                pltpu.make_async_copy(
+                    in_ref.at[:, core, rows], in_scr.at[:, core, rows], in_sems.at[n, t]
+                )
+                for n, rows in enumerate(places)
+            ]
+        )
+    for group in loads:
+        for load in group:
+            load.start()
+    stores = []
+    for t in range(PARTS):
+        for load in loads[t]:
+            load.wait()
+        core, side = divmod(t, 2)
+        rows = slice(t * step, (t + 1) * step)
+        for j in range(slabs):
+            cols = slice(j * PAIR, (j + 1) * PAIR)
+            place = slice(side * step, (side + 1) * step)
+            gk_scr[rows, cols], gv_scr[rows, cols] = merge_lanes(
+                in_scr[2 * j, core, place, :], in_scr[2 * j + 1, core, place, :]
+            )
+            for m in range(step // TILE // 2):
+                base = tokens + side * step // 2 + m * TILE
+                even, odd = merge_lanes(
+                    in_scr[2 * j, core, base : base + TILE, :],
+                    in_scr[2 * j + 1, core, base : base + TILE, :],
+                )
+                base = t * step + 2 * m * TILE
+                gq_scr[base : base + TILE, cols] = even
+                gq_scr[base + TILE : base + 2 * TILE, cols] = odd
+        for n, (scr, ref) in enumerate(((gq_scr, gq_ref), (gk_scr, gk_ref), (gv_scr, gv_ref))):
+            copy = pltpu.make_async_copy(
+                scr.at[pl.ds(t * step, step)],
+                ref.at[pl.ds(t * step, step), pl.ds(lanes, slabs * PAIR)],
+                out_sems.at[n, t],
+            )
+            copy.start()
+            stores.append(copy)
+    for copy in stores:
+        copy.wait()
 
 
 def unpack_phase(back, previous, phase, rows, width):
-    slabs = width // PAIR // PHASES
-    tokens = rows // 2
-    in_specs = [pl.BlockSpec((2, 1, back.shape[1], PAIR), lambda j, c: (j, c, 0, 0))]
-    operands = [back.reshape(2 * slabs, 2, back.shape[1], PAIR)]
+    part = width // PHASES
+    any_spec = pl.BlockSpec(memory_space=pl.ANY)
+    operands = [back.reshape(back.shape[0] // 2, 2, *back.shape[1:])]
     aliases = {}
     if previous is not None:
-        in_specs += [pl.BlockSpec(memory_space=pl.ANY)] * 3
         operands += list(previous)
         aliases = {1: 0, 2: 1, 3: 2}
     return pl.pallas_call(
-        functools.partial(unpack_kernel, tokens),
-        grid=(slabs, 2),
-        in_specs=in_specs,
-        out_specs=[pl.BlockSpec((tokens, PAIR), lambda j, c: (c, phase * slabs + j))] * 3,
+        functools.partial(unpack_kernel, rows // 2, phase * part),
+        in_specs=[any_spec] * len(operands),
+        out_specs=[any_spec] * 3,
         out_shape=[jax.ShapeDtypeStruct((rows, width), jnp.bfloat16)] * 3,
+        scratch_shapes=[pltpu.VMEM(operands[0].shape, jnp.bfloat16)]
+        + [pltpu.VMEM((rows, part), jnp.bfloat16)] * 3
+        + [pltpu.SemaphoreType.DMA((2, PARTS)), pltpu.SemaphoreType.DMA((3, PARTS))],
         input_output_aliases=aliases,
         cost_estimate=pl.CostEstimate(
             flops=0, bytes_accessed=6 * rows * width, transcendentals=0

time: 363 us -> 357 us (0.983)
  Pallas kernels: 138 us -> 126 us
  waiting for transfers between devices: 194 us -> 199 us
    pallas_call x4, Pallas kernels: 25 us -> 13.9 us  [the longest x2 8.29 us: pack_phase(): pl.pallas_call(functools.partial(pack_kernel, rows // 2, phase * part), i...]
    all_to_all x4, waiting for transfers between devices: 180 us -> 185 us  [exchange(): return lax.all_to_all(x, 'ctx', split_axis=0, concat_axis=0, tiled=True)]
  transfers between devices with their start and end apart: 8 -> 8, of which waited for: 8 -> 8; matrix products, arithmetic and copies ran while one was open for 1% -> 1% of each run, Pallas kernels for 34% -> 33%
where the time goes in v8:
time: 357 us; the launch traced here: 356 us
  waiting for transfers between devices  199 us (56%)
  Pallas kernels  126 us (35%)
  starting transfers between devices  23 us (6%)
  local copies, waits for them, and re-layouts  5.48 us (2%)
    all_to_all x4, waiting for transfers between devices, exchange(): return lax.all_to_all(x, 'ctx', split_axis=0, concat_axis=0, tiled=True)  185 us
    pallas_call x2, Pallas kernels, attend_head(): pl.pallas_call(functools.partial(head_kernel, picks), grid_spec=pltpu.Pre...  103 us
    all_to_all x4, starting transfers between devices, exchange(): return lax.all_to_all(x, 'ctx', split_axis=0, concat_axis=0, tiled=True)  21.3 us
    ppermute x4, waiting for transfers between devices, swap(): return lax.ppermute(x, 'ctx', [(i, i ^ 1) for i in range(peers)])  14.4 us
    pallas_call x2, Pallas kernels, merge_sums(): pl.pallas_call(merge_kernel, grid=(peers // step,), in_specs=[spec, spec,...  9.28 us
    pallas_call x2, Pallas kernels, pack_phase(): pl.pallas_call(functools.partial(pack_kernel, rows // 2, phase * part), i...  8.29 us
  transfers between devices with their start and end apart: 8, of which 8 were waited for; matrix products, arithmetic and copies ran while one was open for 1% of the time, Pallas kernels for 33%

profile of v8, /device:TPU:13, one launch (start us, length us, event | category | flops | bytes accessed | tf_op | source)
XLA Modules:
  0.0 355.9 jit_solution(7833573132803946154)
XLA Ops:
  0.6 4.5 %pack_phase.2 = bf16[8,2,1040,128]{3,2,1,0:T(8,128)(2,1)} custom-call(bf16[1024,1024]{1,0:T(8,128)(2,1)} %k_ref.3, bf16[1024,1024]{1,0:T(8,128)(2,1)} %v_ref.3, bf16[1024,1024]{1,0:T(8,128)(2,1)} %q_ref.3, bf16[1024,1024]{1,0:T(8,128)(2,1)} %g_ref.3, s32[8,8]{1,0:T(8,128)} %refs_0_.1), custom_call_target="tpu_custom_call" | custom-call | bytes 8388608 | tf_op jit(solution)/shard_map/pack_phase/pallas_call | solution.py:341
  5.1 6.6 %all-to-all-start = ((bf16[16,1040,128]{2,1,0:T(8,128)(2,1)}), bf16[16,1040,128]{2,1,0:T(8,128)(2,1)}, u32[]{:S(2)}, u32[]{:S(2)}) async-start(bf16[16,1040,128]{2,1,0:T(8,128)(2,1)} %bitcast.7), calls=%async_computation | async-start | bytes 8519680 | tf_op jit(solution)/shard_map/all_to_all | solution.py:259
  11.7 3.8 %pack_phase.3 = bf16[8,2,1024,128]{3,2,1,0:T(8,128)(2,1)} custom-call(bf16[1024,1024]{1,0:T(8,128)(2,1)} %k_ref.3, bf16[1024,1024]{1,0:T(8,128)(2,1)} %v_ref.3, bf16[1024,1024]{1,0:T(8,128)(2,1)} %q_ref.3, bf16[1024,1024]{1,0:T(8,128)(2,1)} %g_ref.3), custom_call_target="tpu_custom_call" | custom-call | bytes 8388608 | tf_op jit(solution)/shard_map/pack_phase/pallas_call | solution.py:341
  15.5 90.1 %all-to-all-done.qg_ref.mine_ref = bf16[16,1040,128]{2,1,0:T(8,128)(2,1)} async-done(((bf16[16,1040,128]{2,1,0:T(8,128)(2,1)}), bf16[16,1040,128]{2,1,0:T(8,128)(2,1)}, u32[]{:S(2)}, u32[]{:S(2)}) %all-to-all-start) | async-done | bytes 4259872 | tf_op jit(solution)/shard_map/all_to_all | solution.py:259
  105.6 4.9 %all-to-all-start.1 = ((bf16[16,1024,128]{2,1,0:T(8,128)(2,1)}), bf16[16,1024,128]{2,1,0:T(8,128)(2,1)}, u32[]{:S(2)}, u32[]{:S(2)}) async-start(bf16[16,1024,128]{2,1,0:T(8,128)(2,1)} %bitcast.8), calls=%async_computation.1 | async-start | bytes 8388608 | tf_op jit(solution)/shard_map/all_to_all | solution.py:259
  110.5 1.7 slice.24
  112.2 0.4 collective-permute-start.2
  112.7 0.8 slice_convert_fusion
  113.4 0.2 fusion.4
  113.6 0.7 reshape.28.table_ref
  114.3 2.3 collective-permute-done.2.other_ref
  116.6 51.6 %attend_head.3 = (bf16[16,768,128]{2,1,0:T(8,128)(2,1)}, f32[8192,128]{1,0:T(8,128)}, bf16[16,512,128]{2,1,0:T(8,128)(2,1)}) custom-call(s32[512]{0:T(512)} %reshape.28.table_ref, bf16[16,1040,128]{2,1,0:T(8,128)(2,1)} %all-to-all-done.qg_ref.mine_ref, bf16[16,1040,128]{2,1,0:T(8,128)(2,1)} %all-to-all-done.qg_ref.mine_ref, ...), custom_call_target="tpu_custom_call" | custom-call | flops 12079595520 | bytes 25165824 | tf_op jit(solution)/shard_map/attend_head/pallas_call | solution.py:519
  168.2 0.4 collective-permute-start.3
  168.6 4.0 %collective-permute-done.3.given_ref = bf16[16,512,128]{2,1,0:T(8,128)(2,1)S(1)} collective-permute-done((bf16[16,512,128]{2,1,0:T(8,128)(2,1)}, bf16[16,512,128]{2,1,0:T(8,128)(2,1)S(1)}, u32[]{:S(2)}, u32[]{:S(2)}) %collective-permute-start.3) | collective-permute-done | bytes 2097184 | tf_op jit(solution)/shard_map/ppermute | solution.py:660
  172.6 0.0 copy-start
  172.6 1.3 copy-done
  173.9 4.6 %merge_sums.3 = bf16[16,768,128]{2,1,0:T(8,128)(2,1)} custom-call(f32[16,512,128]{2,1,0:T(8,128)} %bitcast.10, bf16[16,512,128]{2,1,0:T(8,128)(2,1)} %copy-done, bf16[16,768,128]{2,1,0:T(8,128)(2,1)} %get-tuple-element.17.before_ref), custom_call_target="tpu_custom_call", output_to_operand_aliasing={{}: (2, {})} | custom-call | bytes 8388608 | tf_op jit(solution)/shard_map/merge_sums/pallas_call | solution.py:559
  178.6 24.4 %all-to-all-done.1.qg_ref.mine_ref = bf16[16,1024,128]{2,1,0:T(8,128)(2,1)} async-done(((bf16[16,1024,128]{2,1,0:T(8,128)(2,1)}), bf16[16,1024,128]{2,1,0:T(8,128)(2,1)}, u32[]{:S(2)}, u32[]{:S(2)}) %all-to-all-start.1) | async-done | bytes 4194336 | tf_op jit(solution)/shard_map/all_to_all | solution.py:259
  202.9 4.9 %all-to-all-start.3 = ((bf16[16,768,128]{2,1,0:T(8,128)(2,1)}), bf16[16,768,128]{2,1,0:T(8,128)(2,1)S(1)}, u32[]{:S(2)}, u32[]{:S(2)}) async-start(bf16[16,768,128]{2,1,0:T(8,128)(2,1)} %merge_sums.3), calls=%async_computation.3 | async-start | bytes 6291456 | tf_op jit(solution)/shard_map/all_to_all | solution.py:259
  207.9 1.7 slice.23
  209.6 0.4 collective-permute-start
  210.0 3.9 %collective-permute-done.other_ref = bf16[16,512,128]{2,1,0:T(8,128)(2,1)} collective-permute-done((bf16[16,512,128]{2,1,0:T(8,128)(2,1)S(1)}, bf16[16,512,128]{2,1,0:T(8,128)(2,1)}, u32[]{:S(2)}, u32[]{:S(2)}) %collective-permute-start) | collective-permute-done | bytes 2097184 | tf_op jit(solution)/shard_map/ppermute | solution.py:660
  214.0 51.7 %attend_head.2 = (bf16[16,768,128]{2,1,0:T(8,128)(2,1)}, f32[8192,128]{1,0:T(8,128)}, bf16[16,512,128]{2,1,0:T(8,128)(2,1)}) custom-call(s32[512]{0:T(512)} %reshape.28.table_ref, bf16[16,1024,128]{2,1,0:T(8,128)(2,1)} %all-to-all-done.1.qg_ref.mine_ref, bf16[16,1024,128]{2,1,0:T(8,128)(2,1)} %all-to-all-done.1.qg_ref.mine_ref, ...), custom_call_target="tpu_custom_call" | custom-call | flops 12079595520 | bytes 25165824 | tf_op jit(solution)/shard_map/attend_head/pallas_call | solution.py:519
  265.7 0.4 collective-permute-start.1
  266.1 4.1 %collective-permute-done.1.given_ref = bf16[16,512,128]{2,1,0:T(8,128)(2,1)} collective-permute-done((bf16[16,512,128]{2,1,0:T(8,128)(2,1)}, bf16[16,512,128]{2,1,0:T(8,128)(2,1)}, u32[]{:S(2)}, u32[]{:S(2)}) %collective-permute-start.1) | collective-permute-done | bytes 2097184 | tf_op jit(solution)/shard_map/ppermute | solution.py:660
  270.2 4.6 %merge_sums.2 = bf16[16,768,128]{2,1,0:T(8,128)(2,1)} custom-call(f32[16,512,128]{2,1,0:T(8,128)} %bitcast.9, bf16[16,512,128]{2,1,0:T(8,128)(2,1)} %collective-permute-done.1.given_ref, bf16[16,768,128]{2,1,0:T(8,128)(2,1)} %get-tuple-element.14.before_ref), custom_call_target="tpu_custom_call", output_to_operand_aliasing={{}: (2, {})} | custom-call | bytes 8388608 | tf_op jit(solution)/shard_map/merge_sums/pallas_call | solution.py:559
  274.9 2.9 all-to-all-done.3
  277.7 4.9 %all-to-all-start.2 = ((bf16[16,768,128]{2,1,0:T(8,128)(2,1)}), bf16[16,768,128]{2,1,0:T(8,128)(2,1)}, u32[]{:S(2)}, u32[]{:S(2)}) async-start(bf16[16,768,128]{2,1,0:T(8,128)(2,1)} %merge_sums.2), calls=%async_computation.2 | async-start | bytes 6291456 | tf_op jit(solution)/shard_map/all_to_all | solution.py:259
  282.7 2.3 unpack_phase.2
  285.0 67.6 %all-to-all-done.2 = bf16[16,768,128]{2,1,0:T(8,128)(2,1)} async-done(((bf16[16,768,128]{2,1,0:T(8,128)(2,1)}), bf16[16,768,128]{2,1,0:T(8,128)(2,1)}, u32[]{:S(2)}, u32[]{:S(2)}) %all-to-all-start.2) | async-done | bytes 3145760 | tf_op jit(solution)/shard_map/all_to_all | solution.py:259
  352.7 3.2 unpack_phase.3
Async XLA Ops:
  5.1 100.4 %all-to-all-start = ((bf16[16,1040,128]{2,1,0:T(8,128)(2,1)}), bf16[16,1040,128]{2,1,0:T(8,128)(2,1)}, u32[]{:S(2)}, u32[]{:S(2)}) async-start(bf16[16,1040,128]{2,1,0:T(8,128)(2,1)} %bitcast.7), calls=%async_computation | async-start | bytes 8519680 | tf_op jit(solution)/shard_map/all_to_all | solution.py:259
  105.6 97.4 %all-to-all-start.1 = ((bf16[16,1024,128]{2,1,0:T(8,128)(2,1)}), bf16[16,1024,128]{2,1,0:T(8,128)(2,1)}, u32[]{:S(2)}, u32[]{:S(2)}) async-start(bf16[16,1024,128]{2,1,0:T(8,128)(2,1)} %bitcast.8), calls=%async_computation.1 | async-start | bytes 8388608 | tf_op jit(solution)/shard_map/all_to_all | solution.py:259
  112.2 4.4 %collective-permute-start.2 = (bf16[16,512,128]{2,1,0:T(8,128)(2,1)S(1)}, bf16[16,512,128]{2,1,0:T(8,128)(2,1)}, u32[]{:S(2)}, u32[]{:S(2)}) collective-permute-start(bf16[16,512,128]{2,1,0:T(8,128)(2,1)S(1)} %slice.24), channel_id=1, source_target_pairs={{0,1},{1,0},{2,3},{3,2},{4,5},{5,4},{6,7},{7,6},{8,9},{9,8},{10,11... | collective-permute-start | bytes 6291464 | tf_op jit(solution)/shard_map/ppermute | solution.py:660
  168.2 4.4 %collective-permute-start.3 = (bf16[16,512,128]{2,1,0:T(8,128)(2,1)}, bf16[16,512,128]{2,1,0:T(8,128)(2,1)S(1)}, u32[]{:S(2)}, u32[]{:S(2)}) collective-permute-start(bf16[16,512,128]{2,1,0:T(8,128)(2,1)} %get-tuple-element.16), channel_id=1, source_target_pairs={{0,1},{1,0},{2,3},{3,2},{4,5},{5,4},{6,7},{7,6},{8,9},{9,8},{10,11... | collective-permute-start | bytes 6291464 | tf_op jit(solution)/shard_map/ppermute | solution.py:660
  172.6 1.3 copy-start
  202.9 74.8 %all-to-all-start.3 = ((bf16[16,768,128]{2,1,0:T(8,128)(2,1)}), bf16[16,768,128]{2,1,0:T(8,128)(2,1)S(1)}, u32[]{:S(2)}, u32[]{:S(2)}) async-start(bf16[16,768,128]{2,1,0:T(8,128)(2,1)} %merge_sums.3), calls=%async_computation.3 | async-start | bytes 6291456 | tf_op jit(solution)/shard_map/all_to_all | solution.py:259
  209.6 4.4 %collective-permute-start = (bf16[16,512,128]{2,1,0:T(8,128)(2,1)S(1)}, bf16[16,512,128]{2,1,0:T(8,128)(2,1)}, u32[]{:S(2)}, u32[]{:S(2)}) collective-permute-start(bf16[16,512,128]{2,1,0:T(8,128)(2,1)S(1)} %slice.23), channel_id=1, source_target_pairs={{0,1},{1,0},{2,3},{3,2},{4,5},{5,4},{6,7},{7,6},{8,9},{9,8},{10,11... | collective-permute-start | bytes 6291464 | tf_op jit(solution)/shard_map/ppermute | solution.py:660
  265.7 4.6 %collective-permute-start.1 = (bf16[16,512,128]{2,1,0:T(8,128)(2,1)}, bf16[16,512,128]{2,1,0:T(8,128)(2,1)}, u32[]{:S(2)}, u32[]{:S(2)}) collective-permute-start(bf16[16,512,128]{2,1,0:T(8,128)(2,1)} %get-tuple-element.13), channel_id=1, source_target_pairs={{0,1},{1,0},{2,3},{3,2},{4,5},{5,4},{6,7},{7,6},{8,9},{9,8},{10,11... | collective-permute-start | bytes 6291464 | tf_op jit(solution)/shard_map/ppermute | solution.py:660
  277.7 74.9 %all-to-all-start.2 = ((bf16[16,768,128]{2,1,0:T(8,128)(2,1)}), bf16[16,768,128]{2,1,0:T(8,128)(2,1)}, u32[]{:S(2)}, u32[]{:S(2)}) async-start(bf16[16,768,128]{2,1,0:T(8,128)(2,1)} %merge_sums.2), calls=%async_computation.2 | async-start | bytes 6291456 | tf_op jit(solution)/shard_map/all_to_all | solution.py:259

commit v9 on v8

--- a/solution.py
+++ b/solution.py
@@ -14,9 +14,8 @@
 CHUNKS = 2
 DEPTH = 4
 PHASES = 2
-EXTRA = 16
 PARTS = 4
-SMALL_LIMIT = 16 * 1024 * 1024
+SMALL_LIMIT = 8 * 1024 * 1024
 VMEM_LIMIT = 60 * 1024 * 1024
 
 
@@ -265,10 +264,8 @@
     return low, high
 
 
-def pack_kernel(tokens, lanes, k_ref, v_ref, q_ref, g_ref, *refs):
-    has_table = len(refs) > 5
-    table_ref = refs[0]
-    out_ref, in_scr, out_scr, in_sems, out_sems = refs[-5:]
+def pack_kernel(tokens, lanes, k_ref, v_ref, q_ref, g_ref, out_ref, *scratch):
+    in_scr, out_scr, in_sems, out_sems = scratch
     step = tokens // 2
     sources = (k_ref, v_ref, q_ref, g_ref)
     slabs = in_scr.shape[2] // PAIR
@@ -296,19 +293,6 @@
         copy.start()
         stores.append(copy)
 
-    if has_table:
-        table = table_ref[...].astype(jnp.float32)
-        table = jnp.concatenate(
-            [table, jnp.zeros((table.shape[0], PAIR - table.shape[1]), jnp.float32)], axis=1
-        )
-        table = jnp.concatenate(
-            [table, jnp.zeros((EXTRA - table.shape[0], PAIR), jnp.float32)], axis=0
-        ).astype(jnp.bfloat16)
-        for chip in range(2 * slabs):
-            for core in range(2):
-                out_scr[chip, core, 2 * tokens :, :] = table
-        for core in range(2):
-            send(core, 2 * tokens, EXTRA, 2 * PARTS + core)
     for t in range(PARTS):
         for load in loads[t]:
             load.wait()
@@ -327,35 +311,29 @@
         copy.wait()
 
 
-def pack_phase(key_rows, value_rows, queries, grad_out, phase, extra=None):
+def pack_phase(key_rows, value_rows, queries, grad_out, phase):
     rows, width = queries.shape
     part = width // PHASES
     chips = part // HD
     any_spec = pl.BlockSpec(memory_space=pl.ANY)
-    in_specs, operands = [any_spec] * 4, [key_rows, value_rows, queries, grad_out]
-    length = rows
-    if extra is not None:
-        length += EXTRA
-        in_specs.append(pl.BlockSpec(memory_space=pltpu.VMEM))
-        operands.append(extra)
     packed = pl.pallas_call(
         functools.partial(pack_kernel, rows // 2, phase * part),
-        in_specs=in_specs,
+        in_specs=[any_spec] * 4,
         out_specs=any_spec,
-        out_shape=jax.ShapeDtypeStruct((chips, 2, length, PAIR), jnp.bfloat16),
+        out_shape=jax.ShapeDtypeStruct((chips, 2, rows, PAIR), jnp.bfloat16),
         scratch_shapes=[
             pltpu.VMEM((4, rows, part), jnp.bfloat16),
-            pltpu.VMEM((chips, 2, length, PAIR), jnp.bfloat16),
+            pltpu.VMEM((chips, 2, rows, PAIR), jnp.bfloat16),
             pltpu.SemaphoreType.DMA((4, PARTS)),
-            pltpu.SemaphoreType.DMA((2 * PARTS + 2,)),
+            pltpu.SemaphoreType.DMA((2 * PARTS,)),
         ],
         cost_estimate=pl.CostEstimate(
             flops=0, bytes_accessed=8 * rows * width, transcendentals=0
         ),
         compiler_params=pltpu.CompilerParams(vmem_limit_bytes=VMEM_LIMIT),
         name="pack_phase",
-    )(*operands)
-    return packed.reshape(2 * chips, length, PAIR)
+    )(key_rows, value_rows, queries, grad_out)
+    return packed.reshape(2 * chips, rows, PAIR)
 
 
 def head_kernel(picks, table_ref, qg_ref, mine_ref, other_ref, out_ref, sum_ref, give_ref, *scratch):
@@ -659,19 +637,26 @@
     def swap(x):
         return lax.ppermute(x, "ctx", [(i, i ^ 1) for i in range(peers)])
 
-    received = [
-        exchange(
-            pack_phase(
-                key_rows, value_rows, queries, grad_out, p, tile_keys if p == 0 else None
-            )
+    packed = [
+        pack_phase(key_rows, value_rows, queries, grad_out, p) for p in range(PHASES)
+    ]
+    table, packed[1] = lax.optimization_barrier((tile_keys, packed[1]))
+    index = lax.axis_index("ctx")
+    bit = 1
+    while bit < peers:
+        there = lax.ppermute(table, "ctx", [(i, i ^ bit) for i in range(peers)])
+        upper = index // bit % 2 == 1
+        table = jnp.concatenate(
+            [jnp.where(upper, there, table), jnp.where(upper, table, there)], axis=0
         )
-        for p in range(PHASES)
-    ]
-    table = received[0][:, 2 * tokens : 2 * tokens + blocks, :picks].astype(jnp.int32)
+        bit *= 2
+    table = table.reshape(peers, blocks, picks)
     table = jnp.where(core == 0, table[:, :half], table[:, half:])
     local = table % blocks
     side = (local // half + core) % 2
     table = (side * (peers * half) + table // blocks * half + local % half).reshape(-1)
+    table, packed[1] = lax.optimization_barrier((table, packed[1]))
+    received = [exchange(x) for x in packed]
     backs = []
     for p in range(PHASES):
         payload, sums, give = attend_head(table, received[p], swap(received[p][:, :tokens]))
@@ -716,8 +701,8 @@
     peers = lax.axis_size("ctx")
     blocks = tile_keys.shape[0]
     one_head_each = peers * HD == queries.shape[1]
-    even = peers % 4 == 0 and blocks % 4 == 0 and blocks <= EXTRA
-    fits = one_head_each and even and peers * blocks <= 256
+    even = peers & (peers - 1) == 0 and peers % 4 == 0 and blocks % 4 == 0
+    fits = one_head_each and even
     plan = by_heads if fits else by_blocks
     return tuple(plan(queries, key_rows, value_rows, grad_out, tile_keys))
 

time: 357 us -> 357 us (level)
  waiting for transfers between devices: 199 us -> 195 us
  starting transfers between devices: 23 us -> 26.6 us
    all_to_all x4, waiting for transfers between devices: 185 us -> 94.6 us  [exchange(): return lax.all_to_all(x, 'ctx', split_axis=0, concat_axis=0, tiled=True)]
    ppermute x0 -> x4, waiting for transfers between devices: none -> 84.9 us  [by_heads(): there = lax.ppermute(table, 'ctx', [(i, i ^ bit) for i in range(peers)])]
  transfers between devices with their start and end apart: 8 -> 12, of which waited for: 8 -> 12; matrix products, arithmetic and copies ran while one was open for 1% -> 1% of each run, Pallas kernels for 33% -> 33%
where the time goes in v9:
time: 357 us
  waiting for transfers between devices  195 us (55%)
  Pallas kernels  126 us (35%)
  starting transfers between devices  26.6 us (7%)
  local copies, waits for them, and re-layouts  7.37 us (2%)
    pallas_call x2, Pallas kernels, attend_head(): pl.pallas_call(functools.partial(head_kernel, picks), grid_spec=pltpu.Pre...  103 us
    all_to_all x4, waiting for transfers between devices, exchange(): return lax.all_to_all(x, 'ctx', split_axis=0, concat_axis=0, tiled=True)  94.6 us
    ppermute x4, waiting for transfers between devices, by_heads(): there = lax.ppermute(table, 'ctx', [(i, i ^ bit) for i in range(peers)])  84.9 us
    all_to_all x4, starting transfers between devices, exchange(): return lax.all_to_all(x, 'ctx', split_axis=0, concat_axis=0, tiled=True)  23.8 us
    ppermute x4, waiting for transfers between devices, swap(): return lax.ppermute(x, 'ctx', [(i, i ^ 1) for i in range(peers)])  15.9 us
    pallas_call x2, Pallas kernels, merge_sums(): pl.pallas_call(merge_kernel, grid=(peers // step,), in_specs=[spec, spec,...  9.3 us
    pallas_call x2, Pallas kernels, pack_phase(): pl.pallas_call(functools.partial(pack_kernel, rows // 2, phase * part), i...  7.73 us
  transfers between devices with their start and end apart: 12, of which 12 were waited for; matrix products, arithmetic and copies ran while one was open for 1% of the time, Pallas kernels for 33%

profile of v9, /device:TPU:13, one launch (start us, length us, event | category | flops | bytes accessed | tf_op | source)
XLA Modules:
  0.0 356.5 jit_solution(15156377232440838718)
XLA Ops:
  0.6 3.9 %pack_phase.3 = bf16[8,2,1024,128]{3,2,1,0:T(8,128)(2,1)} custom-call(bf16[1024,1024]{1,0:T(8,128)(2,1)} %k_ref.3, bf16[1024,1024]{1,0:T(8,128)(2,1)} %v_ref.3, bf16[1024,1024]{1,0:T(8,128)(2,1)} %q_ref.3, bf16[1024,1024]{1,0:T(8,128)(2,1)} %g_ref.3), custom_call_target="tpu_custom_call" | custom-call | bytes 8388608 | tf_op jit(solution)/shard_map/pack_phase/pallas_call | solution.py:319
  4.5 6.6 %all-to-all-start.2 = ((bf16[16,1024,128]{2,1,0:T(8,128)(2,1)}), bf16[16,1024,128]{2,1,0:T(8,128)(2,1)}, u32[]{:S(2)}, u32[]{:S(2)}) async-start(bf16[16,1024,128]{2,1,0:T(8,128)(2,1)} %bitcast.10), calls=%async_computation.2 | async-start | bytes 8388608 | tf_op jit(solution)/shard_map/all_to_all | solution.py:258
  11.1 3.8 %pack_phase.2 = bf16[8,2,1024,128]{3,2,1,0:T(8,128)(2,1)} custom-call(bf16[1024,1024]{1,0:T(8,128)(2,1)} %k_ref.3, bf16[1024,1024]{1,0:T(8,128)(2,1)} %v_ref.3, bf16[1024,1024]{1,0:T(8,128)(2,1)} %q_ref.3, bf16[1024,1024]{1,0:T(8,128)(2,1)} %g_ref.3), custom_call_target="tpu_custom_call" | custom-call | bytes 8388608 | tf_op jit(solution)/shard_map/pack_phase/pallas_call | solution.py:319
  15.4 0.8 collective-permute-done
  16.6 12.8 %collective-permute-done.1 = s32[16,8]{0,1:T(8,128)S(1)} collective-permute-done((s32[16,8]{0,1:T(8,128)S(1)}, s32[16,8]{0,1:T(8,128)S(1)}, u32[]{:S(2)}, u32[]{:S(2)}) %collective-permute-start.1) | collective-permute-done | bytes 544 | tf_op jit(solution)/shard_map/ppermute | solution.py:647
  29.9 51.2 %collective-permute-done.2 = s32[32,8]{0,1:T(8,128)S(1)} collective-permute-done((s32[32,8]{0,1:T(8,128)S(1)}, s32[32,8]{0,1:T(8,128)S(1)}, u32[]{:S(2)}, u32[]{:S(2)}) %collective-permute-start.2) | collective-permute-done | bytes 1056 | tf_op jit(solution)/shard_map/ppermute | solution.py:647
  81.4 20.1 %collective-permute-done.3 = s32[64,8]{0,1:T(8,128)S(1)} collective-permute-done((s32[64,8]{0,1:T(8,128)S(1)}, s32[64,8]{0,1:T(8,128)S(1)}, u32[]{:S(2)}, u32[]{:S(2)}) %collective-permute-start.3) | collective-permute-done | bytes 2080 | tf_op jit(solution)/shard_map/ppermute | solution.py:647
  102.2 0.7 reshape.32.table_ref
  102.9 0.8 all-to-all-done.2.qg_ref.mine_ref
  103.7 7.4 %all-to-all-start = ((bf16[16,1024,128]{2,1,0:T(8,128)(2,1)}), bf16[16,1024,128]{2,1,0:T(8,128)(2,1)}, u32[]{:S(2)}, u32[]{:S(2)}) async-start(bf16[16,1024,128]{2,1,0:T(8,128)(2,1)} %bitcast.9), calls=%async_computation | async-start | bytes 8388608 | tf_op jit(solution)/shard_map/all_to_all | solution.py:258
  111.1 1.7 slice.19
  112.9 0.4 collective-permute-start.6
  113.3 3.8 %collective-permute-done.6.other_ref = bf16[16,512,128]{2,1,0:T(8,128)(2,1)S(1)} collective-permute-done((bf16[16,512,128]{2,1,0:T(8,128)(2,1)S(1)}, bf16[16,512,128]{2,1,0:T(8,128)(2,1)S(1)}, u32[]{:S(2)}, u32[]{:S(2)}) %collective-permute-start.6) | collective-permute-done | bytes 2097184 | tf_op jit(solution)/shard_map/ppermute | solution.py:638
  117.1 1.3 copy-done.2
  118.4 51.6 %attend_head.3 = (bf16[16,768,128]{2,1,0:T(8,128)(2,1)}, f32[8192,128]{1,0:T(8,128)}, bf16[16,512,128]{2,1,0:T(8,128)(2,1)}) custom-call(s32[512]{0:T(512)} %reshape.32.table_ref, bf16[16,1024,128]{2,1,0:T(8,128)(2,1)} %all-to-all-done.2.qg_ref.mine_ref, bf16[16,1024,128]{2,1,0:T(8,128)(2,1)} %all-to-all-done.2.qg_ref.mine_ref, bf16[16,512,128]{2,1,0:T(8,128)(2,1)} %copy-done.2), custom_call_target="tpu_custom_call" | custom-call | flops 12079595520 | bytes 25165824 | tf_op jit(solution)/shard_map/attend_head/pallas_call | solution.py:497
  170.0 0.4 collective-permute-start.7
  170.4 4.0 %collective-permute-done.7.given_ref = bf16[16,512,128]{2,1,0:T(8,128)(2,1)S(1)} collective-permute-done((bf16[16,512,128]{2,1,0:T(8,128)(2,1)}, bf16[16,512,128]{2,1,0:T(8,128)(2,1)S(1)}, u32[]{:S(2)}, u32[]{:S(2)}) %collective-permute-start.7) | collective-permute-done | bytes 2097184 | tf_op jit(solution)/shard_map/ppermute | solution.py:638
  174.4 1.3 copy-done
  175.8 4.7 %merge_sums.3 = bf16[16,768,128]{2,1,0:T(8,128)(2,1)} custom-call(f32[16,512,128]{2,1,0:T(8,128)} %bitcast.12, bf16[16,512,128]{2,1,0:T(8,128)(2,1)} %copy-done, bf16[16,768,128]{2,1,0:T(8,128)(2,1)} %get-tuple-element.25.before_ref), custom_call_target="tpu_custom_call", output_to_operand_aliasing={{}: (2, {})} | custom-call | bytes 8388608 | tf_op jit(solution)/shard_map/merge_sums/pallas_call | solution.py:537
  180.4 23.2 %all-to-all-done.qg_ref.mine_ref = bf16[16,1024,128]{2,1,0:T(8,128)(2,1)} async-done(((bf16[16,1024,128]{2,1,0:T(8,128)(2,1)}), bf16[16,1024,128]{2,1,0:T(8,128)(2,1)}, u32[]{:S(2)}, u32[]{:S(2)}) %all-to-all-start) | async-done | bytes 4194336 | tf_op jit(solution)/shard_map/all_to_all | solution.py:258
  203.6 4.9 %all-to-all-start.3 = ((bf16[16,768,128]{2,1,0:T(8,128)(2,1)}), bf16[16,768,128]{2,1,0:T(8,128)(2,1)S(1)}, u32[]{:S(2)}, u32[]{:S(2)}) async-start(bf16[16,768,128]{2,1,0:T(8,128)(2,1)} %merge_sums.3), calls=%async_computation.3 | async-start | bytes 6291456 | tf_op jit(solution)/shard_map/all_to_all | solution.py:258
  208.5 1.7 slice.18
  210.7 3.9 %collective-permute-done.4.other_ref = bf16[16,512,128]{2,1,0:T(8,128)(2,1)} collective-permute-done((bf16[16,512,128]{2,1,0:T(8,128)(2,1)S(1)}, bf16[16,512,128]{2,1,0:T(8,128)(2,1)}, u32[]{:S(2)}, u32[]{:S(2)}) %collective-permute-start.4) | collective-permute-done | bytes 2097184 | tf_op jit(solution)/shard_map/ppermute | solution.py:638
  214.6 51.6 %attend_head.2 = (bf16[16,768,128]{2,1,0:T(8,128)(2,1)}, f32[8192,128]{1,0:T(8,128)}, bf16[16,512,128]{2,1,0:T(8,128)(2,1)}) custom-call(s32[512]{0:T(512)} %reshape.32.table_ref, bf16[16,1024,128]{2,1,0:T(8,128)(2,1)} %all-to-all-done.qg_ref.mine_ref, bf16[16,1024,128]{2,1,0:T(8,128)(2,1)} %all-to-all-done.qg_ref.mine_ref, ...), custom_call_target="tpu_custom_call" | custom-call | flops 12079595520 | bytes 25165824 | tf_op jit(solution)/shard_map/attend_head/pallas_call | solution.py:497
  266.3 0.4 collective-permute-start.5
  266.7 4.1 %collective-permute-done.5.given_ref = bf16[16,512,128]{2,1,0:T(8,128)(2,1)} collective-permute-done((bf16[16,512,128]{2,1,0:T(8,128)(2,1)}, bf16[16,512,128]{2,1,0:T(8,128)(2,1)}, u32[]{:S(2)}, u32[]{:S(2)}) %collective-permute-start.5) | collective-permute-done | bytes 2097184 | tf_op jit(solution)/shard_map/ppermute | solution.py:638
  270.8 4.6 %merge_sums.2 = bf16[16,768,128]{2,1,0:T(8,128)(2,1)} custom-call(f32[16,512,128]{2,1,0:T(8,128)} %bitcast.11, bf16[16,512,128]{2,1,0:T(8,128)(2,1)} %collective-permute-done.5.given_ref, bf16[16,768,128]{2,1,0:T(8,128)(2,1)} %get-tuple-element.22.before_ref), custom_call_target="tpu_custom_call", output_to_operand_aliasing={{}: (2, {})} | custom-call | bytes 8388608 | tf_op jit(solution)/shard_map/merge_sums/pallas_call | solution.py:537
  275.5 2.9 all-to-all-done.3
  278.4 4.9 %all-to-all-start.1 = ((bf16[16,768,128]{2,1,0:T(8,128)(2,1)}), bf16[16,768,128]{2,1,0:T(8,128)(2,1)}, u32[]{:S(2)}, u32[]{:S(2)}) async-start(bf16[16,768,128]{2,1,0:T(8,128)(2,1)} %merge_sums.2), calls=%async_computation.1 | async-start | bytes 6291456 | tf_op jit(solution)/shard_map/all_to_all | solution.py:258
  283.3 2.3 unpack_phase.2
  285.7 67.6 %all-to-all-done.1 = bf16[16,768,128]{2,1,0:T(8,128)(2,1)} async-done(((bf16[16,768,128]{2,1,0:T(8,128)(2,1)}), bf16[16,768,128]{2,1,0:T(8,128)(2,1)}, u32[]{:S(2)}, u32[]{:S(2)}) %all-to-all-start.1) | async-done | bytes 3145760 | tf_op jit(solution)/shard_map/all_to_all | solution.py:258
  353.3 3.2 unpack_phase.3
  (24 shorter events, 2.7 us)
Async XLA Ops:
  4.5 99.2 %all-to-all-start.2 = ((bf16[16,1024,128]{2,1,0:T(8,128)(2,1)}), bf16[16,1024,128]{2,1,0:T(8,128)(2,1)}, u32[]{:S(2)}, u32[]{:S(2)}) async-start(bf16[16,1024,128]{2,1,0:T(8,128)(2,1)} %bitcast.10), calls=%async_computation.2 | async-start | bytes 8388608 | tf_op jit(solution)/shard_map/all_to_all | solution.py:258
  11.1 3.8 %copy-start.1 = (s32[8,8]{1,0:T(8,128)S(1)}, s32[8,8]{1,0:T(8,128)}, u32[]{:S(2)}) copy-start(s32[8,8]{1,0:T(8,128)} %param.9) | copy-start | bytes 772
  15.0 1.2 collective-permute-start
  16.3 13.1 %collective-permute-start.1 = (s32[16,8]{0,1:T(8,128)S(1)}, s32[16,8]{0,1:T(8,128)S(1)}, u32[]{:S(2)}, u32[]{:S(2)}) collective-permute-start(s32[16,8]{0,1:T(8,128)S(1)} %pad_add_fusion), channel_id=1, source_target_pairs={{0,2},{1,3},{2,0},{3,1},{4,6},{5,7},{6,4},{7,5},{8,10},{9,11},{10,... | collective-permute-start | bytes 1544 | tf_op jit(solution)/shard_map/ppermute | solution.py:647
  29.6 51.5 %collective-permute-start.2 = (s32[32,8]{0,1:T(8,128)S(1)}, s32[32,8]{0,1:T(8,128)S(1)}, u32[]{:S(2)}, u32[]{:S(2)}) collective-permute-start(s32[32,8]{0,1:T(8,128)S(1)} %pad_add_fusion.1), channel_id=1, source_target_pairs={{0,4},{1,5},{2,6},{3,7},{4,0},{5,1},{6,2},{7,3},{8,12},{9,13},{10,... | collective-permute-start | bytes 3080 | tf_op jit(solution)/shard_map/ppermute | solution.py:647
  81.2 20.2 %collective-permute-start.3 = (s32[64,8]{0,1:T(8,128)S(1)}, s32[64,8]{0,1:T(8,128)S(1)}, u32[]{:S(2)}, u32[]{:S(2)}) collective-permute-start(s32[64,8]{0,1:T(8,128)S(1)} %pad_add_fusion.2), channel_id=1, source_target_pairs={{0,8},{1,9},{2,10},{3,11},{4,12},{5,13},{6,14},{7,15},{8,0},{9,1},... | collective-permute-start | bytes 6152 | tf_op jit(solution)/shard_map/ppermute | solution.py:647
  103.7 99.9 %all-to-all-start = ((bf16[16,1024,128]{2,1,0:T(8,128)(2,1)}), bf16[16,1024,128]{2,1,0:T(8,128)(2,1)}, u32[]{:S(2)}, u32[]{:S(2)}) async-start(bf16[16,1024,128]{2,1,0:T(8,128)(2,1)} %bitcast.9), calls=%async_computation | async-start | bytes 8388608 | tf_op jit(solution)/shard_map/all_to_all | solution.py:258
  112.9 4.2 %collective-permute-start.6 = (bf16[16,512,128]{2,1,0:T(8,128)(2,1)S(1)}, bf16[16,512,128]{2,1,0:T(8,128)(2,1)S(1)}, u32[]{:S(2)}, u32[]{:S(2)}) collective-permute-start(bf16[16,512,128]{2,1,0:T(8,128)(2,1)S(1)} %slice.19), channel_id=1, source_target_pairs={{0,1},{1,0},{2,3},{3,2},{4,5},{5,4},{6,7},{7,6},{8,9},{9,8},{10,11... | collective-permute-start | bytes 6291464 | tf_op jit(solution)/shard_map/ppermute | solution.py:638
  117.1 1.3 copy-start.2
  170.0 4.4 %collective-permute-start.7 = (bf16[16,512,128]{2,1,0:T(8,128)(2,1)}, bf16[16,512,128]{2,1,0:T(8,128)(2,1)S(1)}, u32[]{:S(2)}, u32[]{:S(2)}) collective-permute-start(bf16[16,512,128]{2,1,0:T(8,128)(2,1)} %get-tuple-element.24), channel_id=1, source_target_pairs={{0,1},{1,0},{2,3},{3,2},{4,5},{5,4},{6,7},{7,6},{8,9},{9,8},{10,11... | collective-permute-start | bytes 6291464 | tf_op jit(solution)/shard_map/ppermute | solution.py:638
  174.4 1.3 copy-start
  203.6 74.8 %all-to-all-start.3 = ((bf16[16,768,128]{2,1,0:T(8,128)(2,1)}), bf16[16,768,128]{2,1,0:T(8,128)(2,1)S(1)}, u32[]{:S(2)}, u32[]{:S(2)}) async-start(bf16[16,768,128]{2,1,0:T(8,128)(2,1)} %merge_sums.3), calls=%async_computation.3 | async-start | bytes 6291456 | tf_op jit(solution)/shard_map/all_to_all | solution.py:258
  210.3 4.4 %collective-permute-start.4 = (bf16[16,512,128]{2,1,0:T(8,128)(2,1)S(1)}, bf16[16,512,128]{2,1,0:T(8,128)(2,1)}, u32[]{:S(2)}, u32[]{:S(2)}) collective-permute-start(bf16[16,512,128]{2,1,0:T(8,128)(2,1)S(1)} %slice.18), channel_id=1, source_target_pairs={{0,1},{1,0},{2,3},{3,2},{4,5},{5,4},{6,7},{7,6},{8,9},{9,8},{10,11... | collective-permute-start | bytes 6291464 | tf_op jit(solution)/shard_map/ppermute | solution.py:638
  266.3 4.6 %collective-permute-start.5 = (bf16[16,512,128]{2,1,0:T(8,128)(2,1)}, bf16[16,512,128]{2,1,0:T(8,128)(2,1)}, u32[]{:S(2)}, u32[]{:S(2)}) collective-permute-start(bf16[16,512,128]{2,1,0:T(8,128)(2,1)} %get-tuple-element.21), channel_id=1, source_target_pairs={{0,1},{1,0},{2,3},{3,2},{4,5},{5,4},{6,7},{7,6},{8,9},{9,8},{10,11... | collective-permute-start | bytes 6291464 | tf_op jit(solution)/shard_map/ppermute | solution.py:638
  278.4 74.9 %all-to-all-start.1 = ((bf16[16,768,128]{2,1,0:T(8,128)(2,1)}), bf16[16,768,128]{2,1,0:T(8,128)(2,1)}, u32[]{:S(2)}, u32[]{:S(2)}) async-start(bf16[16,768,128]{2,1,0:T(8,128)(2,1)} %merge_sums.2), calls=%async_computation.1 | async-start | bytes 6291456 | tf_op jit(solution)/shard_map/all_to_all | solution.py:258

commit v10 on v8

--- a/solution.py
+++ b/solution.py
@@ -267,8 +267,9 @@
 
 def pack_kernel(tokens, lanes, k_ref, v_ref, q_ref, g_ref, *refs):
     has_table = len(refs) > 5
-    table_ref = refs[0]
-    out_ref, in_scr, out_scr, in_sems, out_sems = refs[-5:]
+    if has_table:
+        table_ref, refs, (table_scr, table_sem) = refs[0], refs[1:-2], refs[-2:]
+    out_ref, in_scr, out_scr, in_sems, out_sems = refs
     step = tokens // 2
     sources = (k_ref, v_ref, q_ref, g_ref)
     slabs = in_scr.shape[2] // PAIR
@@ -283,6 +284,9 @@
         ]
         for t in range(PARTS)
     ]
+    if has_table:
+        fetch = pltpu.make_async_copy(table_ref, table_scr, table_sem)
+        fetch.start()
     for group in loads:
         for load in group:
             load.start()
@@ -296,19 +300,6 @@
         copy.start()
         stores.append(copy)
 
-    if has_table:
-        table = table_ref[...].astype(jnp.float32)
-        table = jnp.concatenate(
-            [table, jnp.zeros((table.shape[0], PAIR - table.shape[1]), jnp.float32)], axis=1
-        )
-        table = jnp.concatenate(
-            [table, jnp.zeros((EXTRA - table.shape[0], PAIR), jnp.float32)], axis=0
-        ).astype(jnp.bfloat16)
-        for chip in range(2 * slabs):
-            for core in range(2):
-                out_scr[chip, core, 2 * tokens :, :] = table
-        for core in range(2):
-            send(core, 2 * tokens, EXTRA, 2 * PARTS + core)
     for t in range(PARTS):
         for load in loads[t]:
             load.wait()
@@ -322,7 +313,20 @@
                 out_scr[2 * j, core, place : place + step, :] = low
                 out_scr[2 * j + 1, core, place : place + step, :] = high
         send(core, start, step, 2 * t)
-        send(core, tokens + start, step, 2 * t + 1)
+        tail = EXTRA if has_table and start + step == tokens else 0
+        send(core, tokens + start, step + tail, 2 * t + 1)
+        if has_table and t == 0:
+            fetch.wait()
+            table = table_scr[...].astype(jnp.float32)
+            table = jnp.concatenate(
+                [table, jnp.zeros((table.shape[0], PAIR - table.shape[1]), jnp.float32)], axis=1
+            )
+            table = jnp.concatenate(
+                [table, jnp.zeros((EXTRA - table.shape[0], PAIR), jnp.float32)], axis=0
+            ).astype(jnp.bfloat16)
+            for chip in range(2 * slabs):
+                for core in range(2):
+                    out_scr[chip, core, 2 * tokens :, :] = table
     for copy in stores:
         copy.wait()
 
@@ -333,11 +337,12 @@
     chips = part // HD
     any_spec = pl.BlockSpec(memory_space=pl.ANY)
     in_specs, operands = [any_spec] * 4, [key_rows, value_rows, queries, grad_out]
-    length = rows
+    length, more = rows, []
     if extra is not None:
         length += EXTRA
-        in_specs.append(pl.BlockSpec(memory_space=pltpu.VMEM))
+        in_specs.append(any_spec)
         operands.append(extra)
+        more = [pltpu.VMEM(extra.shape, extra.dtype), pltpu.SemaphoreType.DMA]
     packed = pl.pallas_call(
         functools.partial(pack_kernel, rows // 2, phase * part),
         in_specs=in_specs,
@@ -347,7 +352,8 @@
             pltpu.VMEM((4, rows, part), jnp.bfloat16),
             pltpu.VMEM((chips, 2, length, PAIR), jnp.bfloat16),
             pltpu.SemaphoreType.DMA((4, PARTS)),
-            pltpu.SemaphoreType.DMA((2 * PARTS + 2,)),
+            pltpu.SemaphoreType.DMA((2 * PARTS,)),
+            *more,
         ],
         cost_estimate=pl.CostEstimate(
             flops=0, bytes_accessed=8 * rows * width, transcendentals=0
@@ -573,49 +579,38 @@
 
 def unpack_kernel(tokens, lanes, in_ref, *refs):
     gq_ref, gk_ref, gv_ref, in_scr, gq_scr, gk_scr, gv_scr, in_sems, out_sems = refs[-9:]
-    step = tokens // 2
     slabs = gq_scr.shape[1] // PAIR
-    loads = []
-    for t in range(PARTS):
-        core, side = divmod(t, 2)
-        places = (pl.ds(side * step, step), pl.ds(tokens + side * step // 2, step // 2))
-        loads.append(
-            [
-                pltpu.make_async_copy(
-                    in_ref.at[:, core, rows], in_scr.at[:, core, rows], in_sems.at[n, t]
-                )
-                for n, rows in enumerate(places)
-            ]
+    loads = [
+        pltpu.make_async_copy(
+            in_ref.at[pl.ds(2 * j, 2)], in_scr.at[pl.ds(2 * j, 2)], in_sems.at[j]
         )
-    for group in loads:
-        for load in group:
-            load.start()
+        for j in range(slabs)
+    ]
+    for load in loads:
+        load.start()
     stores = []
-    for t in range(PARTS):
-        for load in loads[t]:
-            load.wait()
-        core, side = divmod(t, 2)
-        rows = slice(t * step, (t + 1) * step)
-        for j in range(slabs):
-            cols = slice(j * PAIR, (j + 1) * PAIR)
-            place = slice(side * step, (side + 1) * step)
+    for j in range(slabs):
+        loads[j].wait()
+        cols = slice(j * PAIR, (j + 1) * PAIR)
+        for core in range(2):
+            rows = slice(core * tokens, (core + 1) * tokens)
             gk_scr[rows, cols], gv_scr[rows, cols] = merge_lanes(
-                in_scr[2 * j, core, place, :], in_scr[2 * j + 1, core, place, :]
+                in_scr[2 * j, core, :tokens, :], in_scr[2 * j + 1, core, :tokens, :]
             )
-            for m in range(step // TILE // 2):
-                base = tokens + side * step // 2 + m * TILE
+            for m in range(tokens // TILE // 2):
+                base = tokens + m * TILE
                 even, odd = merge_lanes(
                     in_scr[2 * j, core, base : base + TILE, :],
                     in_scr[2 * j + 1, core, base : base + TILE, :],
                 )
-                base = t * step + 2 * m * TILE
+                base = core * tokens + 2 * m * TILE
                 gq_scr[base : base + TILE, cols] = even
                 gq_scr[base + TILE : base + 2 * TILE, cols] = odd
         for n, (scr, ref) in enumerate(((gq_scr, gq_ref), (gk_scr, gk_ref), (gv_scr, gv_ref))):
             copy = pltpu.make_async_copy(
-                scr.at[pl.ds(t * step, step)],
-                ref.at[pl.ds(t * step, step), pl.ds(lanes, slabs * PAIR)],
-                out_sems.at[n, t],
+                scr.at[:, pl.ds(j * PAIR, PAIR)],
+                ref.at[:, pl.ds(lanes + j * PAIR, PAIR)],
+                out_sems.at[n, j],
             )
             copy.start()
             stores.append(copy)
@@ -638,7 +633,10 @@
         out_shape=[jax.ShapeDtypeStruct((rows, width), jnp.bfloat16)] * 3,
         scratch_shapes=[pltpu.VMEM(operands[0].shape, jnp.bfloat16)]
         + [pltpu.VMEM((rows, part), jnp.bfloat16)] * 3
-        + [pltpu.SemaphoreType.DMA((2, PARTS)), pltpu.SemaphoreType.DMA((3, PARTS))],
+        + [
+            pltpu.SemaphoreType.DMA((part // PAIR,)),
+            pltpu.SemaphoreType.DMA((3, part // PAIR)),
+        ],
         input_output_aliases=aliases,
         cost_estimate=pl.CostEstimate(
             flops=0, bytes_accessed=6 * rows * width, transcendentals=0

time: 357 us -> 356 us (level)
  no operation moved by 1% of the time
where the time goes in v10:
time: 356 us
  waiting for transfers between devices  199 us (56%)
  Pallas kernels  126 us (35%)
  starting transfers between devices  23 us (6%)
  local copies, waits for them, and re-layouts  5.48 us (2%)
    all_to_all x4, waiting for transfers between devices, exchange(): return lax.all_to_all(x, 'ctx', split_axis=0, concat_axis=0, tiled=True)  185 us
    pallas_call x2, Pallas kernels, attend_head(): pl.pallas_call(functools.partial(head_kernel, picks), grid_spec=pltpu.Pre...  103 us
    all_to_all x4, starting transfers between devices, exchange(): return lax.all_to_all(x, 'ctx', split_axis=0, concat_axis=0, tiled=True)  21.3 us
    ppermute x4, waiting for transfers between devices, swap(): return lax.ppermute(x, 'ctx', [(i, i ^ 1) for i in range(peers)])  14.4 us
    pallas_call x2, Pallas kernels, merge_sums(): pl.pallas_call(merge_kernel, grid=(peers // step,), in_specs=[spec, spec,...  9.28 us
    pallas_call x2, Pallas kernels, pack_phase(): pl.pallas_call(functools.partial(pack_kernel, rows // 2, phase * part), i...  7.99 us
  transfers between devices with their start and end apart: 8, of which 8 were waited for; matrix products, arithmetic and copies ran while one was open for 1% of the time, Pallas kernels for 33%

profile of v10, /device:TPU:13, one launch (start us, length us, event | category | flops | bytes accessed | tf_op | source)
XLA Modules:
  0.0 355.6 jit_solution(12229772342901471388)
XLA Ops:
  0.6 4.2 %pack_phase.2 = bf16[8,2,1040,128]{3,2,1,0:T(8,128)(2,1)} custom-call(bf16[1024,1024]{1,0:T(8,128)(2,1)} %k_ref.3, bf16[1024,1024]{1,0:T(8,128)(2,1)} %v_ref.3, bf16[1024,1024]{1,0:T(8,128)(2,1)} %q_ref.3, bf16[1024,1024]{1,0:T(8,128)(2,1)} %g_ref.3, s32[8,8]{1,0:T(8,128)} %refs_0_.1), custom_call_target="tpu_custom_call" | custom-call | bytes 8388608 | tf_op jit(solution)/shard_map/pack_phase/pallas_call | solution.py:346
  4.9 6.6 %all-to-all-start = ((bf16[16,1040,128]{2,1,0:T(8,128)(2,1)}), bf16[16,1040,128]{2,1,0:T(8,128)(2,1)}, u32[]{:S(2)}, u32[]{:S(2)}) async-start(bf16[16,1040,128]{2,1,0:T(8,128)(2,1)} %bitcast.7), calls=%async_computation | async-start | bytes 8519680 | tf_op jit(solution)/shard_map/all_to_all | solution.py:259
  11.4 3.8 %pack_phase.3 = bf16[8,2,1024,128]{3,2,1,0:T(8,128)(2,1)} custom-call(bf16[1024,1024]{1,0:T(8,128)(2,1)} %k_ref.3, bf16[1024,1024]{1,0:T(8,128)(2,1)} %v_ref.3, bf16[1024,1024]{1,0:T(8,128)(2,1)} %q_ref.3, bf16[1024,1024]{1,0:T(8,128)(2,1)} %g_ref.3), custom_call_target="tpu_custom_call" | custom-call | bytes 8388608 | tf_op jit(solution)/shard_map/pack_phase/pallas_call | solution.py:346
  15.2 90.1 %all-to-all-done.qg_ref.mine_ref = bf16[16,1040,128]{2,1,0:T(8,128)(2,1)} async-done(((bf16[16,1040,128]{2,1,0:T(8,128)(2,1)}), bf16[16,1040,128]{2,1,0:T(8,128)(2,1)}, u32[]{:S(2)}, u32[]{:S(2)}) %all-to-all-start) | async-done | bytes 4259872 | tf_op jit(solution)/shard_map/all_to_all | solution.py:259
  105.3 4.9 %all-to-all-start.1 = ((bf16[16,1024,128]{2,1,0:T(8,128)(2,1)}), bf16[16,1024,128]{2,1,0:T(8,128)(2,1)}, u32[]{:S(2)}, u32[]{:S(2)}) async-start(bf16[16,1024,128]{2,1,0:T(8,128)(2,1)} %bitcast.8), calls=%async_computation.1 | async-start | bytes 8388608 | tf_op jit(solution)/shard_map/all_to_all | solution.py:259
  110.2 1.7 slice.24
  111.9 0.4 collective-permute-start.2
  112.4 0.8 slice_convert_fusion
  113.1 0.2 fusion.4
  113.3 0.7 reshape.28.table_ref
  114.0 2.3 collective-permute-done.2.other_ref
  116.3 51.6 %attend_head.3 = (bf16[16,768,128]{2,1,0:T(8,128)(2,1)}, f32[8192,128]{1,0:T(8,128)}, bf16[16,512,128]{2,1,0:T(8,128)(2,1)}) custom-call(s32[512]{0:T(512)} %reshape.28.table_ref, bf16[16,1040,128]{2,1,0:T(8,128)(2,1)} %all-to-all-done.qg_ref.mine_ref, bf16[16,1040,128]{2,1,0:T(8,128)(2,1)} %all-to-all-done.qg_ref.mine_ref, ...), custom_call_target="tpu_custom_call" | custom-call | flops 12079595520 | bytes 25165824 | tf_op jit(solution)/shard_map/attend_head/pallas_call | solution.py:525
  167.9 0.4 collective-permute-start.3
  168.3 4.0 %collective-permute-done.3.given_ref = bf16[16,512,128]{2,1,0:T(8,128)(2,1)S(1)} collective-permute-done((bf16[16,512,128]{2,1,0:T(8,128)(2,1)}, bf16[16,512,128]{2,1,0:T(8,128)(2,1)S(1)}, u32[]{:S(2)}, u32[]{:S(2)}) %collective-permute-start.3) | collective-permute-done | bytes 2097184 | tf_op jit(solution)/shard_map/ppermute | solution.py:658
  172.3 0.0 copy-start
  172.3 1.3 copy-done
  173.7 4.6 %merge_sums.3 = bf16[16,768,128]{2,1,0:T(8,128)(2,1)} custom-call(f32[16,512,128]{2,1,0:T(8,128)} %bitcast.10, bf16[16,512,128]{2,1,0:T(8,128)(2,1)} %copy-done, bf16[16,768,128]{2,1,0:T(8,128)(2,1)} %get-tuple-element.17.before_ref), custom_call_target="tpu_custom_call", output_to_operand_aliasing={{}: (2, {})} | custom-call | bytes 8388608 | tf_op jit(solution)/shard_map/merge_sums/pallas_call | solution.py:565
  178.3 24.4 %all-to-all-done.1.qg_ref.mine_ref = bf16[16,1024,128]{2,1,0:T(8,128)(2,1)} async-done(((bf16[16,1024,128]{2,1,0:T(8,128)(2,1)}), bf16[16,1024,128]{2,1,0:T(8,128)(2,1)}, u32[]{:S(2)}, u32[]{:S(2)}) %all-to-all-start.1) | async-done | bytes 4194336 | tf_op jit(solution)/shard_map/all_to_all | solution.py:259
  202.7 4.9 %all-to-all-start.3 = ((bf16[16,768,128]{2,1,0:T(8,128)(2,1)}), bf16[16,768,128]{2,1,0:T(8,128)(2,1)S(1)}, u32[]{:S(2)}, u32[]{:S(2)}) async-start(bf16[16,768,128]{2,1,0:T(8,128)(2,1)} %merge_sums.3), calls=%async_computation.3 | async-start | bytes 6291456 | tf_op jit(solution)/shard_map/all_to_all | solution.py:259
  207.6 1.7 slice.23
  209.3 0.4 collective-permute-start
  209.8 3.9 %collective-permute-done.other_ref = bf16[16,512,128]{2,1,0:T(8,128)(2,1)} collective-permute-done((bf16[16,512,128]{2,1,0:T(8,128)(2,1)S(1)}, bf16[16,512,128]{2,1,0:T(8,128)(2,1)}, u32[]{:S(2)}, u32[]{:S(2)}) %collective-permute-start) | collective-permute-done | bytes 2097184 | tf_op jit(solution)/shard_map/ppermute | solution.py:658
  213.7 51.7 %attend_head.2 = (bf16[16,768,128]{2,1,0:T(8,128)(2,1)}, f32[8192,128]{1,0:T(8,128)}, bf16[16,512,128]{2,1,0:T(8,128)(2,1)}) custom-call(s32[512]{0:T(512)} %reshape.28.table_ref, bf16[16,1024,128]{2,1,0:T(8,128)(2,1)} %all-to-all-done.1.qg_ref.mine_ref, bf16[16,1024,128]{2,1,0:T(8,128)(2,1)} %all-to-all-done.1.qg_ref.mine_ref, ...), custom_call_target="tpu_custom_call" | custom-call | flops 12079595520 | bytes 25165824 | tf_op jit(solution)/shard_map/attend_head/pallas_call | solution.py:525
  265.4 0.4 collective-permute-start.1
  265.8 4.1 %collective-permute-done.1.given_ref = bf16[16,512,128]{2,1,0:T(8,128)(2,1)} collective-permute-done((bf16[16,512,128]{2,1,0:T(8,128)(2,1)}, bf16[16,512,128]{2,1,0:T(8,128)(2,1)}, u32[]{:S(2)}, u32[]{:S(2)}) %collective-permute-start.1) | collective-permute-done | bytes 2097184 | tf_op jit(solution)/shard_map/ppermute | solution.py:658
  269.9 4.6 %merge_sums.2 = bf16[16,768,128]{2,1,0:T(8,128)(2,1)} custom-call(f32[16,512,128]{2,1,0:T(8,128)} %bitcast.9, bf16[16,512,128]{2,1,0:T(8,128)(2,1)} %collective-permute-done.1.given_ref, bf16[16,768,128]{2,1,0:T(8,128)(2,1)} %get-tuple-element.14.before_ref), custom_call_target="tpu_custom_call", output_to_operand_aliasing={{}: (2, {})} | custom-call | bytes 8388608 | tf_op jit(solution)/shard_map/merge_sums/pallas_call | solution.py:565
  274.6 2.9 all-to-all-done.3
  277.5 4.9 %all-to-all-start.2 = ((bf16[16,768,128]{2,1,0:T(8,128)(2,1)}), bf16[16,768,128]{2,1,0:T(8,128)(2,1)}, u32[]{:S(2)}, u32[]{:S(2)}) async-start(bf16[16,768,128]{2,1,0:T(8,128)(2,1)} %merge_sums.2), calls=%async_computation.2 | async-start | bytes 6291456 | tf_op jit(solution)/shard_map/all_to_all | solution.py:259
  282.4 2.3 unpack_phase.2
  284.7 67.7 %all-to-all-done.2 = bf16[16,768,128]{2,1,0:T(8,128)(2,1)} async-done(((bf16[16,768,128]{2,1,0:T(8,128)(2,1)}), bf16[16,768,128]{2,1,0:T(8,128)(2,1)}, u32[]{:S(2)}, u32[]{:S(2)}) %all-to-all-start.2) | async-done | bytes 3145760 | tf_op jit(solution)/shard_map/all_to_all | solution.py:259
  352.4 3.2 unpack_phase.3
Async XLA Ops:
  4.9 100.4 %all-to-all-start = ((bf16[16,1040,128]{2,1,0:T(8,128)(2,1)}), bf16[16,1040,128]{2,1,0:T(8,128)(2,1)}, u32[]{:S(2)}, u32[]{:S(2)}) async-start(bf16[16,1040,128]{2,1,0:T(8,128)(2,1)} %bitcast.7), calls=%async_computation | async-start | bytes 8519680 | tf_op jit(solution)/shard_map/all_to_all | solution.py:259
  105.3 97.4 %all-to-all-start.1 = ((bf16[16,1024,128]{2,1,0:T(8,128)(2,1)}), bf16[16,1024,128]{2,1,0:T(8,128)(2,1)}, u32[]{:S(2)}, u32[]{:S(2)}) async-start(bf16[16,1024,128]{2,1,0:T(8,128)(2,1)} %bitcast.8), calls=%async_computation.1 | async-start | bytes 8388608 | tf_op jit(solution)/shard_map/all_to_all | solution.py:259
  111.9 4.4 %collective-permute-start.2 = (bf16[16,512,128]{2,1,0:T(8,128)(2,1)S(1)}, bf16[16,512,128]{2,1,0:T(8,128)(2,1)}, u32[]{:S(2)}, u32[]{:S(2)}) collective-permute-start(bf16[16,512,128]{2,1,0:T(8,128)(2,1)S(1)} %slice.24), channel_id=1, source_target_pairs={{0,1},{1,0},{2,3},{3,2},{4,5},{5,4},{6,7},{7,6},{8,9},{9,8},{10,11... | collective-permute-start | bytes 6291464 | tf_op jit(solution)/shard_map/ppermute | solution.py:658
  167.9 4.4 %collective-permute-start.3 = (bf16[16,512,128]{2,1,0:T(8,128)(2,1)}, bf16[16,512,128]{2,1,0:T(8,128)(2,1)S(1)}, u32[]{:S(2)}, u32[]{:S(2)}) collective-permute-start(bf16[16,512,128]{2,1,0:T(8,128)(2,1)} %get-tuple-element.16), channel_id=1, source_target_pairs={{0,1},{1,0},{2,3},{3,2},{4,5},{5,4},{6,7},{7,6},{8,9},{9,8},{10,11... | collective-permute-start | bytes 6291464 | tf_op jit(solution)/shard_map/ppermute | solution.py:658
  172.3 1.3 copy-start
  202.7 74.8 %all-to-all-start.3 = ((bf16[16,768,128]{2,1,0:T(8,128)(2,1)}), bf16[16,768,128]{2,1,0:T(8,128)(2,1)S(1)}, u32[]{:S(2)}, u32[]{:S(2)}) async-start(bf16[16,768,128]{2,1,0:T(8,128)(2,1)} %merge_sums.3), calls=%async_computation.3 | async-start | bytes 6291456 | tf_op jit(solution)/shard_map/all_to_all | solution.py:259
  209.3 4.4 %collective-permute-start = (bf16[16,512,128]{2,1,0:T(8,128)(2,1)S(1)}, bf16[16,512,128]{2,1,0:T(8,128)(2,1)}, u32[]{:S(2)}, u32[]{:S(2)}) collective-permute-start(bf16[16,512,128]{2,1,0:T(8,128)(2,1)S(1)} %slice.23), channel_id=1, source_target_pairs={{0,1},{1,0},{2,3},{3,2},{4,5},{5,4},{6,7},{7,6},{8,9},{9,8},{10,11... | collective-permute-start | bytes 6291464 | tf_op jit(solution)/shard_map/ppermute | solution.py:658
  265.4 4.6 %collective-permute-start.1 = (bf16[16,512,128]{2,1,0:T(8,128)(2,1)}, bf16[16,512,128]{2,1,0:T(8,128)(2,1)}, u32[]{:S(2)}, u32[]{:S(2)}) collective-permute-start(bf16[16,512,128]{2,1,0:T(8,128)(2,1)} %get-tuple-element.13), channel_id=1, source_target_pairs={{0,1},{1,0},{2,3},{3,2},{4,5},{5,4},{6,7},{7,6},{8,9},{9,8},{10,11... | collective-permute-start | bytes 6291464 | tf_op jit(solution)/shard_map/ppermute | solution.py:658
  277.5 74.9 %all-to-all-start.2 = ((bf16[16,768,128]{2,1,0:T(8,128)(2,1)}), bf16[16,768,128]{2,1,0:T(8,128)(2,1)}, u32[]{:S(2)}, u32[]{:S(2)}) async-start(bf16[16,768,128]{2,1,0:T(8,128)(2,1)} %merge_sums.2), calls=%async_computation.2 | async-start | bytes 6291456 | tf_op jit(solution)/shard_map/all_to_all | solution.py:259
